TPU v7x, 256 devices: a whole 4x4x8 slice. The times are simulated.
256 devices in a mesh: dp: 16 (over y, x), mp: 16 (over z, core).
Axes of the slice: x: 4, y: 4, z: 8, core: 2. Of those that a mesh axis runs over, the one named last changes fastest.
Arguments:
- tiles: bfloat16 [4096, 256, 256], P(('dp', 'mp')), may hold values from -0.046875 to 0.046875
- tile_rows: int32 [4096], P(('dp', 'mp')), may hold values from 0 to 3, as said below
- tile_cols: int32 [4096], P(('dp', 'mp')), may hold values from 0 to 7
- tile_count: int32 [256], P(('dp', 'mp')), may hold values from 5 to 16, as said below
- data_weight: float32 [16384], P('mp'), may hold values from 0.3 to 3
- depth_level: int32 [32768], P(('dp', 'mp')), may hold values from 0 to 31
- depth_reg: float32 [32], replicated, may hold values from 0.1 to 1
- right_side: float32 [32768, 128], P(('dp', 'mp')), may hold values from -6 to 6
Outputs:
- solution: float32 [32768, 128], P(('dp', 'mp'))
- residual: float32 [32768, 128], P(('dp', 'mp'))
Inputs may be any that keep to these rules, and one draw needn't show every extreme that they name: Within one device's 16 slots the pairs (tile_rows, tile_cols) are distinct. `tile_count`: slots of a device at or beyond its count are padding; some device has all 16 slots live.
All inputs are finite; a program needn't handle non-finite values.
Results may differ from a plain program's by a relative error of at most 0.0072.
Values may be sent and summed in bfloat16 or wider, within the bound.
No kernel may reach another device: no remote copies, remote signals or barrier semaphores. Data moves between devices by JAX's collectives and lax.ppermute only.
A program may use at most 64 MiB of HBM per device.

v0:
```python
import jax
import jax.numpy as jnp
from jax import lax
from jax.sharding import PartitionSpec as P

ITERS = 2


def slot_products(block, lookup, source, target, target_blocks, live, flipped):
    picked = source[lookup]
    if flipped:
        out = jnp.einsum("tab,tar->tbr", block, picked, preferred_element_type=jnp.float32)
    else:
        out = jnp.einsum("tab,tbr->tar", block, picked, preferred_element_type=jnp.float32)
    masked = out * live[:, None, None]
    placed = jnp.zeros((target_blocks, out.shape[1], out.shape[2]), jnp.float32)
    return placed.at[target].add(masked)


def block_product(tiles, lookup_all, target_all, count, source, target_blocks, flipped):
    slots = tiles.shape[0]
    live = (jnp.arange(slots, dtype=jnp.int32) < count).astype(jnp.float32)
    return slot_products(tiles, lookup_all, source, target_all, target_blocks, live, flipped)


def body(tiles, tile_rows, tile_cols, tile_count, data_weight, depth_level, depth_reg, right_side):
    tile = tiles.shape[1]
    cells = right_side.shape[0]
    probes = right_side.shape[1]
    group_rows = data_weight.shape[0]
    row_blocks = group_rows // tile
    col_blocks = cells * lax.axis_size("mp") // tile
    count = tile_count[0]
    levels = depth_reg.shape[0]
    level_hot = (depth_level[:, None] == jnp.arange(levels, dtype=jnp.int32)[None, :]).astype(
        jnp.float32
    )
    reg_cell = jnp.sum(level_hot * depth_reg[None, :], axis=1)
    solution = jnp.zeros_like(right_side)
    residual = right_side
    direction = right_side
    norm_now = lax.psum(jnp.sum(residual * residual, axis=0), ("dp", "mp"))
    for step_index in range(ITERS):
        gathered = lax.all_gather(direction.astype(jnp.bfloat16), "mp", axis=0, tiled=True)
        source = gathered.reshape(col_blocks, tile, probes)
        partial_value = block_product(
            tiles, tile_cols, tile_rows, count, source, row_blocks, False
        ).reshape(group_rows, probes)
        predicted = lax.psum(partial_value, "dp")
        weighted = (data_weight[:, None] * predicted).astype(jnp.bfloat16)
        back_source = weighted.reshape(row_blocks, tile, probes)
        terms = block_product(
            tiles, tile_rows, tile_cols, count, back_source, col_blocks, True
        ).reshape(col_blocks * tile, probes)
        summed = lax.psum_scatter(terms, "mp", scatter_dimension=0, tiled=True)
        image = summed + reg_cell[:, None] * direction
        curve = lax.psum(jnp.sum(direction * image, axis=0), ("dp", "mp"))
        alpha = norm_now / curve
        solution = solution + alpha[None, :] * direction
        residual = residual - alpha[None, :] * image
        if step_index + 1 < ITERS:
            norm_next = lax.psum(jnp.sum(residual * residual, axis=0), ("dp", "mp"))
            direction = residual + (norm_next / norm_now)[None, :] * direction
            norm_now = norm_next
    return (solution, residual)


def solution(mesh):
    placed = (
        P(("dp", "mp"), None, None),
        P(("dp", "mp")),
        P(("dp", "mp")),
        P(("dp", "mp")),
        P("mp"),
        P(("dp", "mp")),
        P(),
        P(("dp", "mp"), None),
    )
    return jax.shard_map(
        body,
        mesh=mesh,
        in_specs=placed,
        out_specs=(P(("dp", "mp"), None), P(("dp", "mp"), None)),
        check_vma=False,
    )
```

profile of v0, /device:TPU:1, one launch (start us, length us, event | category | flops | bytes accessed | tf_op | source)
XLA Modules:
  0.0 634.0 jit_solution(15603211454614187919)
XLA Ops:
  7.2 0.0 all-reduce.4.cloned.1.call-start
  7.2 0.8 compare_select_fusion.1
  8.0 0.8 convert_element_type.23
  8.9 22.7 %all_gather.6 = bf16[2048,128]{1,0:T(8,128)(2,1)S(1)} all-gather(bf16[128,128]{1,0:T(8,128)(2,1)S(1)} %convert_element_type.23), channel_id=1, replica_groups=mesh['dp'=16,'mp'=16] {'mp'}, dimensions={0}, use_global_device_ids=true | all-gather | bytes 557056 | tf_op jit(solution)/shard_map/all_gather | solution.py:44
  32.3 1.7 gather_fusion
  33.9 3.4 multiply_bitcast_fusion.3
  37.3 2.9 copy.23
  40.3 3.5 scatter_fusion
  43.8 0.8 copy-done.2
  44.6 0.0 reduce-scatter.3.cloned.1.call-start
  44.7 91.8 %all-reduce.4.cloned.1.call-done = f32[1024,128]{1,0:T(8,128)} async-done(((f32[1024,128]{1,0:T(8,128)}), f32[1024,128]{1,0:T(8,128)}) %all-reduce.4.cloned.1.call-update) | async-done | bytes 524304 | tf_op jit(solution)/shard_map/psum | solution.py:49
  136.4 1.2 multiply_convert_fusion.1
  137.7 0.7 gather_fusion.1
  138.4 1.9 multiply_bitcast_fusion.2
  140.3 2.9 copy.25
  143.2 0.1 broadcast.33.clone
  143.3 3.5 scatter_fusion.1
  146.9 1.0 copy-done.4
  147.8 0.0 reduce-scatter.3.cloned.1.call-update
  147.9 0.0 all-reduce.6.cloned.1.call-start
  147.9 0.1 select_reduce_fusion
  148.0 55.3 %reduce-scatter.3.cloned.1.call-done = f32[128,128]{1,0:T(8,128)} async-done(((f32[2048,128]{1,0:T(8,128)}), f32[128,128]{1,0:T(8,128)}) %reduce-scatter.3.cloned.1.call-update) | async-done | bytes 65552 | tf_op jit(solution)/shard_map/reduce_scatter | solution.py:55
  203.3 0.9 multiply_reduce_fusion.2
  204.2 79.8 %all-reduce = (f32[128]{0:T(128)S(1)}, f32[128]{0:T(128)S(1)}) all-reduce(f32[128]{0:T(128)S(1)} %get-tuple-element.3, f32[128]{0:T(128)S(1)} %get-tuple-element.2), channel_id=1, replica_groups=mesh['dp'=16,'mp'=16] {'dp','mp'}, use_global_device_ids=true, to_apply=%region_1.0 | all-reduce | flops 256 | bytes 2048 | tf_op jit(solution)/shard_map/psum | solution.py:42
  284.0 0.9 multiply_reduce_fusion.1
  285.0 72.5 %psum.45 = f32[128]{0:T(128)S(1)} all-reduce(f32[128]{0:T(128)S(1)} %multiply_reduce_fusion.1), channel_id=1, replica_groups=mesh['dp'=16,'mp'=16] {'dp','mp'}, use_global_device_ids=true, to_apply=%region_10.0 | all-reduce | flops 128 | bytes 1024 | tf_op jit(solution)/shard_map/psum | solution.py:62
  357.4 0.9 fusion
  358.4 18.1 %all_gather.7 = bf16[2048,128]{1,0:T(8,128)(2,1)S(1)} all-gather(bf16[128,128]{1,0:T(8,128)(2,1)S(1)} %fusion), channel_id=1, replica_groups=mesh['dp'=16,'mp'=16] {'mp'}, dimensions={0}, use_global_device_ids=true | all-gather | bytes 557056 | tf_op jit(solution)/shard_map/all_gather | solution.py:44
  376.5 1.7 gather_fusion.2
  378.2 3.4 multiply_bitcast_fusion.1
  381.6 2.9 copy.27
  384.5 3.5 scatter_fusion.2
  388.0 0.8 copy-done.1
  388.8 0.0 all-reduce.6.cloned.1.call-update
  388.8 0.2 reduce-scatter.5.cloned.1.call-start
  389.0 89.3 %all-reduce.6.cloned.1.call-done = f32[1024,128]{1,0:T(8,128)} async-done(((f32[1024,128]{1,0:T(8,128)}), f32[1024,128]{1,0:T(8,128)}) %all-reduce.6.cloned.1.call-update) | async-done | bytes 524304 | tf_op jit(solution)/shard_map/psum | solution.py:49
  478.3 1.2 multiply_convert_fusion
  479.6 0.7 gather_fusion.3
  480.3 1.9 multiply_bitcast_fusion
  482.2 2.9 copy.29
  485.1 0.1 broadcast.33
  485.2 3.5 scatter_fusion.3
  488.7 1.0 copy-done.3
  489.7 0.0 reduce-scatter.5.cloned.1.call-update
  489.7 55.4 %reduce-scatter.5.cloned.1.call-done = f32[128,128]{1,0:T(8,128)} async-done(((f32[2048,128]{1,0:T(8,128)}), f32[128,128]{1,0:T(8,128)}) %reduce-scatter.5.cloned.1.call-update) | async-done | bytes 65552 | tf_op jit(solution)/shard_map/reduce_scatter | solution.py:55
  545.1 0.9 multiply_reduce_fusion
  546.1 79.8 %psum.47 = f32[128]{0:T(128)S(1)} all-reduce(f32[128]{0:T(128)S(1)} %multiply_reduce_fusion), channel_id=1, replica_groups=mesh['dp'=16,'mp'=16] {'dp','mp'}, use_global_device_ids=true, to_apply=%region_16.0 | all-reduce | flops 128 | bytes 1024 | tf_op jit(solution)/shard_map/psum | solution.py:57
  625.9 1.6 multiply_subtract_fusion
  (28 shorter events, 0.2 us)
Async XLA Ops:
  7.2 26.8 %copy-start = (bf16[16,256,256]{2,1,0:T(8,128)(2,1)S(1)}, bf16[16,256,256]{2,1,0:T(8,128)(2,1)}, u32[]{:S(2)}) copy-start(bf16[16,256,256]{2,1,0:T(8,128)(2,1)} %param.8) | copy-start | bytes 6291460
  7.2 129.3 %all-reduce.4.cloned.1.call-start = ((), (), s32[]{:S(2)}) async-start(), calls=%async_computation.2 | async-start | bytes 1048576 | tf_op jit(solution)/shard_map/psum | solution.py:49
  37.3 2.9 copy-start.8
  40.3 96.2 %copy-start.7 = (f32[1024]{0:T(1024)S(1)}, f32[1024]{0:T(1024)}, u32[]{:S(2)}) copy-start(f32[1024]{0:T(1024)} %param.12) | copy-start | bytes 12292
  43.8 0.8 copy-start.2
  44.6 158.7 %reduce-scatter.3.cloned.1.call-start = ((), (), s32[]{:S(2)}) async-start(), calls=%async_computation.3 | async-start | bytes 1114112 | tf_op jit(solution)/shard_map/reduce_scatter | solution.py:55
  143.3 4.6 copy-start.9
  143.3 4.6 copy-start.10
  143.3 59.9 %copy-start.5 = (f32[128,128]{1,0:T(8,128)S(1)}, f32[128,128]{1,0:T(8,128)}, u32[]{:S(2)}) copy-start(f32[128,128]{1,0:T(8,128)} %param.15) | copy-start | bytes 196612
  146.8 1.0 copy-start.4
  147.9 330.5 %all-reduce.6.cloned.1.call-start = ((), (), s32[]{:S(2)}) async-start(), calls=%async_computation.4 | async-start | bytes 1048576 | tf_op jit(solution)/shard_map/psum | solution.py:49
  388.0 0.8 copy-start.1
  388.8 156.3 %reduce-scatter.5.cloned.1.call-start = ((), (), s32[]{:S(2)}) async-start(), calls=%async_computation.5 | async-start | bytes 1114112 | tf_op jit(solution)/shard_map/reduce_scatter | solution.py:55
  485.2 59.9 %copy-start.6 = (f32[128,128]{1,0:T(8,128)S(1)}, f32[128,128]{1,0:T(8,128)}, u32[]{:S(2)}) copy-start(f32[128,128]{1,0:T(8,128)} %reduce-scatter.3.cloned.1.call-done) | copy-start | bytes 196612
  488.7 1.0 copy-start.3
Sparse Core Ops, SparseCore 0:
  44.7 91.6 all-reduce.3
  148.0 55.2 reduce-scatter.2
  388.9 89.3 all-reduce.5
  489.8 55.2 reduce-scatter.4
where the time goes:
time: 635 us; the launch traced here: 634 us
  waiting for transfers between devices  292 us (46%)
  blocking collectives  273 us (43%)
  other arithmetic  23.6 us (4%)
  local copies, waits for them, and re-layouts  20.2 us (3%)
  between operations  14.6 us (2%)
  matrix products  10.6 us (2%)
    psum x2, waiting for transfers between devices, body(): predicted = lax.psum(partial_value, 'dp')  181 us
    reduce_scatter x2, waiting for transfers between devices, body(): summed = lax.psum_scatter(terms, 'mp', scatter_dimension=0, tiled=True)  111 us
    psum x1, blocking collectives, body(): norm_now = lax.psum(jnp.sum(residual * residual, axis=0), ('dp', 'mp'))  79.8 us
    psum x1, blocking collectives, body(): curve = lax.psum(jnp.sum(direction * image, axis=0), ('dp', 'mp'))  79.8 us
    psum x1, blocking collectives, body(): norm_next = lax.psum(jnp.sum(residual * residual, axis=0), ('dp', 'mp'))  72.5 us
    all_gather x2, blocking collectives, body(): lax.all_gather(direction.astype(jnp.bfloat16), 'mp', axis=0, tiled=True)  40.9 us
    scatter-add x4, other arithmetic, slot_products(): return placed.at[target].add(masked)  14 us
  transfers between devices with their start and end apart: 4, of which 4 were waited for; matrix products, arithmetic and copies ran while one was open for 0% of the time, Pallas kernels for 0%

commit v1 on v0

v1 whole, which is shorter than its diff:
```python
import functools

import jax
import jax.numpy as jnp
from jax import lax
from jax.experimental import pallas as pl
from jax.experimental.pallas import tpu as pltpu
from jax.sharding import PartitionSpec as P

SUMS = 8
TERMS = 3
PARTS = 16
CORES = 2
SIDE = 4
KINDS = 3
COLS = 8
PACK = 2
TOP = 10.0
VMEM_LIMIT = 16 * 1024 * 1024


def call(kernel, out_shape, operands, smem=0, scratch=()):
    spaces = [pltpu.SMEM] * smem + [pltpu.VMEM] * (len(operands) - smem)
    return pl.pallas_call(
        kernel,
        out_shape=out_shape,
        in_specs=[pl.BlockSpec(memory_space=space) for space in spaces],
        out_specs=jax.tree.map(lambda _: pl.BlockSpec(memory_space=pltpu.VMEM), out_shape),
        scratch_shapes=list(scratch),
        compiler_params=pltpu.CompilerParams(vmem_limit_bytes=VMEM_LIMIT),
    )(*operands)


def f32(*shape):
    return jax.ShapeDtypeStruct(shape, jnp.float32)


def bf16(*shape):
    return jax.ShapeDtypeStruct(shape, jnp.bfloat16)


def rows_of(*sums):
    blank = jnp.zeros((SUMS - len(sums), sums[0].shape[1]), jnp.float32)
    return jnp.concatenate(list(sums) + [blank], axis=0)


def column_sum(value):
    return jnp.sum(value, axis=0, keepdims=True)


def cell_sums(value, reg, image):
    square = value * value
    return rows_of(column_sum(reg * square), column_sum(square), column_sum(value * image))


def start_kernel(right_ref, reg_ref, sums_ref):
    right = right_ref[...]
    sums_ref[...] = cell_sums(right, reg_ref[...], jnp.zeros_like(right))


def weight_column(part, weights):
    row = weights[pl.ds(part // PACK, 1), :]
    n = row.shape[1]
    shape = (n // PACK, n)
    wanted = lax.broadcasted_iota(jnp.int32, shape, 0) + lax.rem(part, PACK) * (n // PACK)
    same = lax.broadcasted_iota(jnp.int32, shape, 1) == wanted
    return jnp.sum(jnp.where(same, row, 0.0), axis=1, keepdims=True)


def split(sums):
    left, terms = sums, []
    for _ in range(TERMS):
        high = left.astype(jnp.bfloat16).astype(jnp.float32)
        terms.append(high)
        left = left - high
    return jnp.concatenate(terms, axis=0)


def join(terms):
    return terms[:KINDS] + terms[KINDS : 2 * KINDS] + terms[2 * KINDS : TERMS * KINDS]


def padded(rows):
    blank = jnp.zeros((PARTS - rows.shape[0], rows.shape[1]), jnp.float32)
    return jnp.concatenate([rows, blank], axis=0)


def exponent(largest):
    return jnp.ceil(jnp.log2(jnp.clip(largest, 1e-30, 1e30)))


def rows_at(start, size):
    return pl.ds(pl.multiple_of(start, size), size)


def row_of(slots, slot):
    return slots[slot] // COLS


def col_of(slots, slot):
    return lax.rem(slots[slot], COLS)


def forward_kernel(dp, slots, lower, upper, tiles, sums, out, total):
    tile = tiles.shape[1]
    chunk = out.shape[1]
    total[...] = jnp.zeros_like(total)
    for slot in range(tiles.shape[0]):
        col = col_of(slots, slot)
        source = jnp.concatenate([lower[col], upper[col]], axis=0)
        total[rows_at(row_of(slots, slot) * tile, tile), :] += jnp.dot(
            tiles[slot], source, preferred_element_type=jnp.float32
        )
    for part in range(out.shape[0]):
        out[part] = total[part * chunk : (part + 1) * chunk].astype(jnp.bfloat16)


def added(got):
    total = got[0].astype(jnp.float32)
    for part in range(1, got.shape[0]):
        total = total + got[part].astype(jnp.float32)
    return total


def weight_kernel(part, got, weights, sums, out):
    chunk = got.shape[1]
    predicted = added(got)
    weighted = (weight_column(part[0], weights) * predicted).astype(jnp.bfloat16)
    curve = column_sum(predicted * weighted.astype(jnp.float32)) + sums[0:1]
    extra = padded(split(jnp.concatenate([curve, sums[1:KINDS]], axis=0))).astype(jnp.bfloat16)
    for part in range(out.shape[0]):
        out[part, :chunk] = weighted
        out[part, chunk:] = extra


def backward(half, slots, got, tiles, source, total):
    tile = tiles.shape[1]
    parts, chunk = got.shape[0], got.shape[1] - PARTS
    cells = tile // CORES
    sums = got[0, chunk:].astype(jnp.float32)
    for part in range(1, parts):
        sums = sums + got[part, chunk:].astype(jnp.float32)
    for part in range(parts):
        source[part * chunk : (part + 1) * chunk] = got[part, :chunk]
    total[...] = jnp.zeros_like(total)
    for slot in range(tiles.shape[0]):
        total[rows_at(col_of(slots, slot) * cells, cells), :] += lax.dot_general(
            tiles[slot, :, rows_at(half * cells, cells)],
            source[rows_at(row_of(slots, slot) * tile, tile), :],
            (((0,), (0,)), ((), ())),
            preferred_element_type=jnp.float32,
        )
    return join(sums)


def backward_send_kernel(core, slots, got, tiles, coded, source, total):
    sums = backward(1 - core[0], slots, got, tiles, source, total)
    cells = tiles.shape[1] // CORES
    powers = []
    for block in range(total.shape[0] // cells):
        rows = slice(block * cells, (block + 1) * cells)
        power = exponent(jnp.max(jnp.abs(total[rows]), axis=0, keepdims=True))
        coded[rows] = total[rows] * jnp.exp2(TOP - power)
        powers.append(power)
    sum_power = exponent(jnp.abs(sums))
    terms = split(sums * jnp.exp2(TOP - sum_power))
    tail = padded(jnp.concatenate([terms, sum_power], axis=0))
    coded[total.shape[0] :] = jnp.concatenate([tail] + powers, axis=0)


def backward_keep_kernel(core, slots, got, tiles, after, keep, sums_out, source):
    sums = backward(core[0], slots, got, tiles, source, keep)
    sums_out[...] = rows_of(*[sums[kind : kind + 1] for kind in range(KINDS)])


def pair_kernel(keep, kept_sums, coded, out):
    blocks = out.shape[0]
    cells = out.shape[1] - PARTS
    tail = coded[blocks * cells :]
    at = TERMS * KINDS
    sums = kept_sums[:KINDS] + join(tail[:at]) * jnp.exp2(tail[at : at + KINDS] - TOP)
    sum_power = exponent(jnp.abs(sums))
    sums = split(sums * jnp.exp2(TOP - sum_power))
    for block in range(blocks):
        rows = slice(block * cells, (block + 1) * cells)
        back = jnp.exp2(tail[PARTS + block : PARTS + block + 1] - TOP)
        total = keep[rows] + coded[rows] * back
        power = exponent(jnp.max(jnp.abs(total), axis=0, keepdims=True))
        out[block, :cells] = total * jnp.exp2(TOP - power)
        out[block, cells:] = padded(jnp.concatenate([sums, sum_power, power], axis=0))


def summed(got, cells):
    total, sums = 0.0, 0.0
    at = cells + TERMS * KINDS
    for part in range(got.shape[0]):
        total = total + got[part, :cells] * jnp.exp2(got[part, at + KINDS : at + KINDS + 1] - TOP)
        sums = sums + join(got[part, cells:at]) * jnp.exp2(got[part, at : at + KINDS] - TOP)
    return total, sums


def first_update_kernel(got, right_ref, reg_ref, residual_ref, image_ref, low_ref, sums_ref, keep_ref):
    right, reg = right_ref[...], reg_ref[...]
    terms, sums = summed(got, right.shape[0])
    curve, norm = sums[0:1], sums[1:2]
    alpha = norm / curve
    image = terms + reg * right
    residual = right - alpha * image
    residual_ref[...] = residual
    image_ref[...] = image
    low = residual.astype(jnp.bfloat16)
    for block in range(low_ref.shape[0]):
        low_ref[block] = low
    sums_ref[...] = cell_sums(residual, reg, image)
    keep_ref[...] = rows_of(norm, curve, alpha)


def last_update_kernel(got, right_ref, reg_ref, residual_ref, image_ref, keep_ref, solution_out, residual_out):
    right, residual = right_ref[...], residual_ref[...]
    terms, sums = summed(got, right.shape[0])
    norm, curve, alpha = keep_ref[0:1], keep_ref[1:2], keep_ref[2:3]
    norm_next = sums[1:2]
    ratio = norm_next / norm
    image_next = terms + reg_ref[...] * residual + ratio * image_ref[...]
    curve_next = sums[0:1] + ratio * (2.0 * sums[2:3] + ratio * curve)
    alpha_next = norm_next / curve_next
    direction = residual + ratio * right
    solution_out[...] = alpha * right + alpha_next * direction
    residual_out[...] = residual - alpha_next * image_next


def exchange(value, axis):
    return lax.all_to_all(value, axis, 0, 0)


def swap(value):
    return lax.ppermute(value, "core", [(0, 1), (1, 0)])


def body(tiles, tile_rows, tile_cols, tile_count, data_weight, depth_level, depth_reg, right_side):
    tile = tiles.shape[1]
    cells, probes = right_side.shape
    group_rows = data_weight.shape[0]
    n_dp, n_z = lax.axis_size(DP), lax.axis_size("z")
    chunk = group_rows // n_dp
    col_blocks = cells * CORES * n_z // tile
    core = lax.axis_index("core").astype(jnp.int32).reshape(1)
    dp = lax.axis_index(DP).astype(jnp.int32).reshape(1)

    low = right_side.astype(jnp.bfloat16)
    own = exchange(jnp.broadcast_to(low, (n_z, cells, probes)), "z")
    own, tiles, tile_rows, tile_cols, tile_count, depth_level, depth_reg = lax.optimization_barrier(
        (own, tiles, tile_rows, tile_cols, tile_count, depth_level, depth_reg)
    )
    live = jnp.arange(tiles.shape[0], dtype=jnp.int32) < tile_count
    tiles = jnp.where(live[:, None, None], tiles, jnp.zeros_like(tiles))
    slots = tile_rows * COLS + tile_cols
    levels = jnp.arange(depth_reg.shape[0], dtype=jnp.int32)
    level_hot = (depth_level[:, None] == levels[None, :]).astype(jnp.float32)
    reg_cell = jnp.sum(level_hot * depth_reg[None, :], axis=1)
    reg = jnp.broadcast_to(reg_cell[:, None], (cells, probes))
    sums = call(start_kernel, f32(SUMS, probes), (right_side, reg))
    weights = data_weight.reshape(-1, chunk * PACK)

    def products(own, sums):
        other = swap(own)
        first = lax.axis_index("core") == 0
        lower, upper = jnp.where(first, own, other), jnp.where(first, other, own)
        partial = call(
            forward_kernel,
            bf16(n_dp, chunk, probes),
            (dp, slots, lower, upper, tiles, sums),
            smem=2,
            scratch=[pltpu.VMEM((group_rows, probes), jnp.float32)],
        )
        weighted = call(
            weight_kernel,
            bf16(n_dp, chunk + PARTS, probes),
            (dp, exchange(partial, DP), weights, sums),
            smem=1,
        )
        operands = (core, slots, exchange(weighted, DP), tiles)
        source = pltpu.VMEM((group_rows, probes), jnp.bfloat16)
        rows = n_z * cells
        coded = call(
            backward_send_kernel,
            f32(rows + PARTS + n_z, probes),
            operands,
            smem=2,
            scratch=[source, pltpu.VMEM((rows, probes), jnp.float32)],
        )
        keep, kept_sums = call(
            backward_keep_kernel,
            [f32(rows, probes), f32(SUMS, probes)],
            (*operands, coded),
            smem=2,
            scratch=[source],
        )
        coded = swap(coded.astype(jnp.float16)).astype(jnp.float32)
        terms = call(pair_kernel, f32(n_z, cells + PARTS, probes), (keep, kept_sums, coded))
        return exchange(terms.astype(jnp.float16), "z").astype(jnp.float32)

    whole, extra = f32(cells, probes), f32(SUMS, probes)
    residual, image, low, sums, keep = call(
        first_update_kernel,
        (whole, whole, bf16(n_z, cells, probes), extra, extra),
        (products(own, sums), right_side, reg),
    )
    return call(
        last_update_kernel,
        (whole, whole),
        (products(exchange(low, "z"), sums), right_side, reg, residual, image, keep),
    )


DP = ("y", "x")


def solution(mesh):
    n_dp, n_mp = mesh.devices.shape
    split_mesh = jax.sharding.Mesh(
        mesh.devices.reshape(n_dp // SIDE, SIDE, n_mp // CORES, CORES), ("y", "x", "z", "core")
    )
    mp = ("z", "core")
    every = DP + mp
    placed = (
        P(every, None, None),
        P(every),
        P(every),
        P(every),
        P(mp),
        P(every),
        P(),
        P(every, None),
    )
    return jax.shard_map(
        body,
        mesh=split_mesh,
        in_specs=placed,
        out_specs=(P(every, None), P(every, None)),
        check_vma=False,
    )
```

time: 635 us -> 135 us (0.21)
  waiting for transfers between devices: 292 us -> 11.1 us
  blocking collectives: 273 us -> 90.2 us
  other arithmetic: 23.6 us -> 3.16 us
  local copies, waits for them, and re-layouts: 20.2 us -> 0.85 us
  starting transfers between devices: 0.34 us -> 19.1 us
  between operations: 14.6 us -> 1.53 us
  matrix products: 10.6 us -> 0 us
  Pallas kernels: 0 us -> 8.34 us
    psum x3 -> x0, blocking collectives: 232 us -> none  [the longest x1 79.8 us: body(): norm_now = lax.psum(jnp.sum(residual * residual, axis=0), ('dp', 'mp'))]
    psum x2 -> x0, waiting for transfers between devices: 181 us -> none  [body(): predicted = lax.psum(partial_value, 'dp')]
    reduce_scatter x2 -> x0, waiting for transfers between devices: 111 us -> none  [body(): summed = lax.psum_scatter(terms, 'mp', scatter_dimension=0, tiled=True)]
    all_to_all x0 -> x7, blocking collectives: none -> 90.2 us  [exchange(): return lax.all_to_all(value, axis, 0, 0)]
    all_gather x2 -> x0, blocking collectives: 40.9 us -> none  [body(): lax.all_gather(direction.astype(jnp.bfloat16), 'mp', axis=0, tiled=True)]
    scatter-add x4 -> x0, other arithmetic: 14 us -> none  [slot_products(): return placed.at[target].add(masked)]
    mul x4 -> x0, local copies, waits for them, and re-layouts: 11.5 us -> none  [slot_products(): masked = out * live[:, None, None]]
    dot_general x4 -> x0, matrix products: 10.6 us -> none  [the longest x2 6.79 us: slot_products(): jnp.einsum('tab,tbr->tar', block, picked, preferred_element_type=jnp.floa...]
  transfers between devices with their start and end apart: 4 -> 5, of which waited for: 4 -> 4; matrix products, arithmetic and copies ran while one was open for 0% -> 1% of each run, Pallas kernels for 0% -> 2%
where the time goes in v1:
time: 135 us; the launch traced here: 134 us
  blocking collectives  90.2 us (67%)
  starting transfers between devices  19.1 us (14%)
  waiting for transfers between devices  11.1 us (8%)
  Pallas kernels  8.34 us (6%)
  other arithmetic  3.16 us (2%)
  between operations  1.53 us (1%)
    all_to_all x7, blocking collectives, exchange(): return lax.all_to_all(value, axis, 0, 0)  90.2 us
    ppermute x4, starting transfers between devices, swap(): return lax.ppermute(value, 'core', [(0, 1), (1, 0)])  10.1 us
    all_to_all x1, waiting for transfers between devices, exchange(): return lax.all_to_all(value, axis, 0, 0)  9.64 us
    all_to_all x1, starting transfers between devices, exchange(): return lax.all_to_all(value, axis, 0, 0)  9.01 us
    pallas_call x13, Pallas kernels, call(): pl.pallas_call(kernel, out_shape=out_shape, in_specs=[pl.BlockSpec(memory...  8.34 us
  transfers between devices with their start and end apart: 5, of which 4 were waited for; matrix products, arithmetic and copies ran while one was open for 1% of the time, Pallas kernels for 2%

profile of v1, /device:TPU:1, one launch (start us, length us, event | category | flops | bytes accessed | tf_op | source)
XLA Modules:
  0.0 134.2 jit_solution(1268789172459391678)
XLA Ops:
  0.6 0.8 convert_element_type.28
  1.5 0.7 broadcast_in_dim.14
  2.2 9.0 %all-to-all-start = ((bf16[8,128,128]{2,1,0:T(8,128)(2,1)}), bf16[8,128,128]{2,1,0:T(8,128)(2,1)S(1)}, u32[]{:S(2)}, u32[]{:S(2)}) async-start(bf16[8,128,128]{2,1,0:T(8,128)(2,1)} %broadcast_in_dim.14), calls=%async_computation | async-start | bytes 524288 | tf_op jit(solution)/shard_map/all_to_all | solution.py:233
  11.9 0.0 copy-start.2
  11.9 0.0 copy-start.3
  11.9 0.0 copy-start
  11.9 0.0 copy-start.4
  11.9 0.0 copy-start.5
  12.0 9.6 %all-to-all-done = bf16[8,128,128]{2,1,0:T(8,128)(2,1)S(1)} async-done(((bf16[8,128,128]{2,1,0:T(8,128)(2,1)}), bf16[8,128,128]{2,1,0:T(8,128)(2,1)S(1)}, u32[]{:S(2)}, u32[]{:S(2)}) %all-to-all-start) | async-done | bytes 262176 | tf_op jit(solution)/shard_map/all_to_all | solution.py:233
  21.6 2.5 %collective-permute-start = (bf16[8,128,128]{2,1,0:T(8,128)(2,1)S(1)}, bf16[8,128,128]{2,1,0:T(8,128)(2,1)S(1)}, u32[]{:S(2)}, u32[]{:S(2)}) collective-permute-start(bf16[8,128,128]{2,1,0:T(8,128)(2,1)S(1)} %all-to-all-done), channel_id=1, source_target_pairs={{0,1},{1,0},{2,3},{3,2},{4,5},{5,4},{6,7},{7,6},{8,9},{9,8},{10,11... | collective-permute-start | bytes 786440 | tf_op jit(solution)/shard_map/ppermute | solution.py:237
  24.1 1.8 %broadcast_select_fusion.tiles = bf16[16,256,256]{2,1,0:T(8,128)(2,1)S(1)} fusion(bf16[16,256,256]{2,1,0:T(8,128)(2,1)} %param.8, pred[16]{0:T(512)(128)(4,1)S(1)} %iota_compare_fusion.1), kind=kLoop, calls=%fused_computation | loop fusion | flops 1048576 | bytes 4194320 | tf_op jit(solution)/shard_map/jit(_where)/select_n | solution.py:256
  25.9 0.0 copy-done.2
  25.9 0.0 copy-done.3
  25.9 0.1 select_reduce_fusion
  26.0 0.1 broadcast_in_dim.27.reg_ref
  26.1 0.0 copy-done
  26.1 0.0 copy-done.4
  26.1 0.0 copy-done.5
  26.1 0.0 copy-start.1
  26.1 0.0 collective-permute-done
  26.2 1.3 shard_map.96
  27.5 15.1 %all_to_all.40.got = bf16[16,64,128]{2,1,0:T(8,128)(2,1)S(1)} all-to-all(bf16[16,64,128]{2,1,0:T(8,128)(2,1)S(1)} %shard_map.96), channel_id=1, replica_groups=mesh['y'=4,'x'=4,'z'=8,'core'=2] {'y','x'}, dimensions={0} | all-to-all | bytes 524288 | tf_op jit(solution)/shard_map/all_to_all | solution.py:233
  42.6 0.0 copy-done.1
  42.6 0.1 shard_map.97
  42.7 10.7 %all_to_all.41.got = bf16[16,80,128]{2,1,0:T(8,128)(2,1)S(1)} all-to-all(bf16[16,80,128]{2,1,0:T(8,128)(2,1)S(1)} %shard_map.97), channel_id=1, replica_groups=mesh['y'=4,'x'=4,'z'=8,'core'=2] {'y','x'}, dimensions={0} | all-to-all | bytes 655360 | tf_op jit(solution)/shard_map/all_to_all | solution.py:233
  53.4 1.1 shard_map.98.after
  54.6 2.4 %collective-permute-start.1 = (f16[1048,128]{1,0:T(8,128)(2,1)S(1)}, f16[1048,128]{1,0:T(8,128)(2,1)S(1)}, u32[]{:S(2)}, u32[]{:S(2)}) collective-permute-start(f16[1048,128]{1,0:T(8,128)(2,1)S(1)} %convert_element_type.29), channel_id=1, source_target_pairs={{0,1},{1,0},{2,3},{3,2},{4,5},{5,4},{6,7},{7,6},{8,9},{9,8},{10,11... | collective-permute-start | bytes 804872 | tf_op jit(solution)/shard_map/ppermute | solution.py:237
  57.1 1.0 shard_map.99
  58.1 0.1 collective-permute-done.1
  58.3 0.1 shard_map.100
  58.5 15.0 %all_to_all.42 = f16[8,144,128]{2,1,0:T(8,128)(2,1)S(1)} all-to-all(f16[8,144,128]{2,1,0:T(8,128)(2,1)S(1)} %convert_element_type.31), channel_id=1, replica_groups=mesh['y'=4,'x'=4,'z'=8,'core'=2] {'z'}, dimensions={0} | all-to-all | bytes 589824 | tf_op jit(solution)/shard_map/all_to_all | solution.py:233
  73.5 0.1 shard_map.101
  73.6 13.0 %all_to_all.43 = bf16[8,128,128]{2,1,0:T(8,128)(2,1)S(1)} all-to-all(bf16[8,128,128]{2,1,0:T(8,128)(2,1)S(1)} %get-tuple-element.27), channel_id=1, replica_groups=mesh['y'=4,'x'=4,'z'=8,'core'=2] {'z'}, dimensions={0} | all-to-all | bytes 524288 | tf_op jit(solution)/shard_map/all_to_all | solution.py:233
  86.6 2.3 %collective-permute-start.2 = (bf16[8,128,128]{2,1,0:T(8,128)(2,1)S(1)}, bf16[8,128,128]{2,1,0:T(8,128)(2,1)S(1)}, u32[]{:S(2)}, u32[]{:S(2)}) collective-permute-start(bf16[8,128,128]{2,1,0:T(8,128)(2,1)S(1)} %all_to_all.43), channel_id=1, source_target_pairs={{0,1},{1,0},{2,3},{3,2},{4,5},{5,4},{6,7},{7,6},{8,9},{9,8},{10,11... | collective-permute-start | bytes 786440 | tf_op jit(solution)/shard_map/ppermute | solution.py:237
  88.9 1.2 collective-permute-done.2
  90.0 0.1 broadcast_select_fusion.1
  90.1 1.3 shard_map.102
  91.4 10.7 %all_to_all.44.got = bf16[16,64,128]{2,1,0:T(8,128)(2,1)S(1)} all-to-all(bf16[16,64,128]{2,1,0:T(8,128)(2,1)S(1)} %shard_map.102), channel_id=1, replica_groups=mesh['y'=4,'x'=4,'z'=8,'core'=2] {'y','x'}, dimensions={0} | all-to-all | bytes 524288 | tf_op jit(solution)/shard_map/all_to_all | solution.py:233
  102.2 0.1 shard_map.103
  102.3 10.6 %all_to_all.45.got = bf16[16,80,128]{2,1,0:T(8,128)(2,1)S(1)} all-to-all(bf16[16,80,128]{2,1,0:T(8,128)(2,1)S(1)} %shard_map.103), channel_id=1, replica_groups=mesh['y'=4,'x'=4,'z'=8,'core'=2] {'y','x'}, dimensions={0} | all-to-all | bytes 655360 | tf_op jit(solution)/shard_map/all_to_all | solution.py:233
  112.9 1.1 shard_map.104.after
  114.1 2.9 %collective-permute-start.3 = (f16[1048,128]{1,0:T(8,128)(2,1)S(1)}, f16[1048,128]{1,0:T(8,128)(2,1)S(1)}, u32[]{:S(2)}, u32[]{:S(2)}) collective-permute-start(f16[1048,128]{1,0:T(8,128)(2,1)S(1)} %convert_element_type.33), channel_id=1, source_target_pairs={{0,1},{1,0},{2,3},{3,2},{4,5},{5,4},{6,7},{7,6},{8,9},{9,8},{10,11... | collective-permute-start | bytes 804872 | tf_op jit(solution)/shard_map/ppermute | solution.py:237
  117.0 1.0 shard_map.105
  118.0 0.1 collective-permute-done.3
  118.2 0.1 shard_map.106
  118.4 15.0 %all_to_all.46 = f16[8,144,128]{2,1,0:T(8,128)(2,1)S(1)} all-to-all(f16[8,144,128]{2,1,0:T(8,128)(2,1)S(1)} %convert_element_type.35), channel_id=1, replica_groups=mesh['y'=4,'x'=4,'z'=8,'core'=2] {'z'}, dimensions={0} | all-to-all | bytes 589824 | tf_op jit(solution)/shard_map/all_to_all | solution.py:233
  133.5 0.7 shard_map.107
  (12 shorter events, 0.4 us)
Async XLA Ops:
  2.2 19.4 %all-to-all-start = ((bf16[8,128,128]{2,1,0:T(8,128)(2,1)}), bf16[8,128,128]{2,1,0:T(8,128)(2,1)S(1)}, u32[]{:S(2)}, u32[]{:S(2)}) async-start(bf16[8,128,128]{2,1,0:T(8,128)(2,1)} %broadcast_in_dim.14), calls=%async_computation | async-start | bytes 524288 | tf_op jit(solution)/shard_map/all_to_all | solution.py:233
  11.9 14.0 %copy-start.2 = (f32[32]{0:T(128)S(1)}, f32[32]{0:T(128)}, u32[]{:S(2)}) copy-start(f32[32]{0:T(128)} %param.14) | copy-start | bytes 388
  11.9 14.0 %copy-start.3 = (s32[128]{0:T(128)S(1)}, s32[128]{0:T(128)}, u32[]{:S(2)}) copy-start(s32[128]{0:T(128)} %param.13) | copy-start | bytes 1540
  11.9 14.1 %copy-start = (f32[128,128]{1,0:T(8,128)S(1)}, f32[128,128]{1,0:T(8,128)}, u32[]{:S(2)}) copy-start(f32[128,128]{1,0:T(8,128)} %right_ref.5) | copy-start | bytes 196612
  11.9 14.2 %copy-start.4 = (s32[16]{0:T(128)S(1)}, s32[16]{0:T(128)}, u32[]{:S(2)}) copy-start(s32[16]{0:T(128)} %param.10) | copy-start | bytes 196
  11.9 14.2 %copy-start.5 = (s32[16]{0:T(128)S(1)}, s32[16]{0:T(128)}, u32[]{:S(2)}) copy-start(s32[16]{0:T(128)} %param.9) | copy-start | bytes 196
  21.6 4.5 %collective-permute-start = (bf16[8,128,128]{2,1,0:T(8,128)(2,1)S(1)}, bf16[8,128,128]{2,1,0:T(8,128)(2,1)S(1)}, u32[]{:S(2)}, u32[]{:S(2)}) collective-permute-start(bf16[8,128,128]{2,1,0:T(8,128)(2,1)S(1)} %all-to-all-done), channel_id=1, source_target_pairs={{0,1},{1,0},{2,3},{3,2},{4,5},{5,4},{6,7},{7,6},{8,9},{9,8},{10,11... | collective-permute-start | bytes 786440 | tf_op jit(solution)/shard_map/ppermute | solution.py:237
  26.1 16.5 %copy-start.1 = (f32[1024]{0:T(1024)S(1)}, f32[1024]{0:T(1024)}, u32[]{:S(2)}) copy-start(f32[1024]{0:T(1024)} %param.12) | copy-start | bytes 12292
  54.6 3.6 %collective-permute-start.1 = (f16[1048,128]{1,0:T(8,128)(2,1)S(1)}, f16[1048,128]{1,0:T(8,128)(2,1)S(1)}, u32[]{:S(2)}, u32[]{:S(2)}) collective-permute-start(f16[1048,128]{1,0:T(8,128)(2,1)S(1)} %convert_element_type.29), channel_id=1, source_target_pairs={{0,1},{1,0},{2,3},{3,2},{4,5},{5,4},{6,7},{7,6},{8,9},{9,8},{10,11... | collective-permute-start | bytes 804872 | tf_op jit(solution)/shard_map/ppermute | solution.py:237
  86.6 3.4 %collective-permute-start.2 = (bf16[8,128,128]{2,1,0:T(8,128)(2,1)S(1)}, bf16[8,128,128]{2,1,0:T(8,128)(2,1)S(1)}, u32[]{:S(2)}, u32[]{:S(2)}) collective-permute-start(bf16[8,128,128]{2,1,0:T(8,128)(2,1)S(1)} %all_to_all.43), channel_id=1, source_target_pairs={{0,1},{1,0},{2,3},{3,2},{4,5},{5,4},{6,7},{7,6},{8,9},{9,8},{10,11... | collective-permute-start | bytes 786440 | tf_op jit(solution)/shard_map/ppermute | solution.py:237
  114.1 4.1 %collective-permute-start.3 = (f16[1048,128]{1,0:T(8,128)(2,1)S(1)}, f16[1048,128]{1,0:T(8,128)(2,1)S(1)}, u32[]{:S(2)}, u32[]{:S(2)}) collective-permute-start(f16[1048,128]{1,0:T(8,128)(2,1)S(1)} %convert_element_type.33), channel_id=1, source_target_pairs={{0,1},{1,0},{2,3},{3,2},{4,5},{5,4},{6,7},{7,6},{8,9},{9,8},{10,11... | collective-permute-start | bytes 804872 | tf_op jit(solution)/shard_map/ppermute | solution.py:237

commit v2 on v1

--- a/solution.py
+++ b/solution.py
@@ -16,6 +16,7 @@
 COLS = 8
 PACK = 2
 TOP = 10.0
+SUM_TOP = 14.0
 VMEM_LIMIT = 16 * 1024 * 1024
 
 
@@ -101,16 +102,26 @@
     return lax.rem(slots[slot], COLS)
 
 
-def forward_kernel(dp, slots, lower, upper, tiles, sums, out, total):
+def forward(half, slots, field, tiles, total):
     tile = tiles.shape[1]
+    cells = tile // CORES
+    for slot in range(tiles.shape[0]):
+        total[rows_at(row_of(slots, slot) * tile, tile), :] += jnp.dot(
+            tiles[slot, :, rows_at(half * cells, cells)],
+            field[col_of(slots, slot)],
+            preferred_element_type=jnp.float32,
+        )
+
+
+def forward_own_kernel(core, slots, own, tiles, total):
+    total[...] = jnp.zeros_like(total)
+    forward(core[0], slots, own, tiles, total)
+
+
+def forward_other_kernel(dp, core, slots, other, tiles, own_total, sums, out, total):
     chunk = out.shape[1]
-    total[...] = jnp.zeros_like(total)
-    for slot in range(tiles.shape[0]):
-        col = col_of(slots, slot)
-        source = jnp.concatenate([lower[col], upper[col]], axis=0)
-        total[rows_at(row_of(slots, slot) * tile, tile), :] += jnp.dot(
-            tiles[slot], source, preferred_element_type=jnp.float32
-        )
+    total[...] = own_total[...]
+    forward(1 - core[0], slots, other, tiles, total)
     for part in range(out.shape[0]):
         out[part] = total[part * chunk : (part + 1) * chunk].astype(jnp.bfloat16)
 
@@ -175,27 +186,29 @@
 
 def pair_kernel(keep, kept_sums, coded, out):
     blocks = out.shape[0]
-    cells = out.shape[1] - PARTS
+    cells = out.shape[1] - SUMS
     tail = coded[blocks * cells :]
     at = TERMS * KINDS
     sums = kept_sums[:KINDS] + join(tail[:at]) * jnp.exp2(tail[at : at + KINDS] - TOP)
-    sum_power = exponent(jnp.abs(sums))
-    sums = split(sums * jnp.exp2(TOP - sum_power))
+    sum_power = exponent(jnp.max(jnp.abs(sums), axis=0, keepdims=True))
+    sums = sums * jnp.exp2(SUM_TOP - sum_power)
+    high = sums.astype(jnp.bfloat16).astype(jnp.float32)
     for block in range(blocks):
         rows = slice(block * cells, (block + 1) * cells)
         back = jnp.exp2(tail[PARTS + block : PARTS + block + 1] - TOP)
         total = keep[rows] + coded[rows] * back
         power = exponent(jnp.max(jnp.abs(total), axis=0, keepdims=True))
         out[block, :cells] = total * jnp.exp2(TOP - power)
-        out[block, cells:] = padded(jnp.concatenate([sums, sum_power, power], axis=0))
+        out[block, cells:] = jnp.concatenate([high, sums - high, sum_power, power], axis=0)
 
 
 def summed(got, cells):
     total, sums = 0.0, 0.0
-    at = cells + TERMS * KINDS
     for part in range(got.shape[0]):
-        total = total + got[part, :cells] * jnp.exp2(got[part, at + KINDS : at + KINDS + 1] - TOP)
-        sums = sums + join(got[part, cells:at]) * jnp.exp2(got[part, at : at + KINDS] - TOP)
+        tail = got[part, cells:]
+        total = total + got[part, :cells] * jnp.exp2(tail[2 * KINDS + 1 :] - TOP)
+        high, low, power = tail[:KINDS], tail[KINDS : 2 * KINDS], tail[2 * KINDS : 2 * KINDS + 1]
+        sums = sums + (high + low) * jnp.exp2(power - SUM_TOP)
     return total, sums
 
 
@@ -247,13 +260,11 @@
     core = lax.axis_index("core").astype(jnp.int32).reshape(1)
     dp = lax.axis_index(DP).astype(jnp.int32).reshape(1)
 
-    low = right_side.astype(jnp.bfloat16)
-    own = exchange(jnp.broadcast_to(low, (n_z, cells, probes)), "z")
-    own, tiles, tile_rows, tile_cols, tile_count, depth_level, depth_reg = lax.optimization_barrier(
-        (own, tiles, tile_rows, tile_cols, tile_count, depth_level, depth_reg)
-    )
+    one = (jnp.arange(n_z, dtype=jnp.int32) + core >= 0).astype(jnp.float32)
+    own = exchange((right_side[None] * one[:, None, None]).astype(jnp.bfloat16), "z")
     live = jnp.arange(tiles.shape[0], dtype=jnp.int32) < tile_count
     tiles = jnp.where(live[:, None, None], tiles, jnp.zeros_like(tiles))
+    own = own * (tiles[0, :1, :1] == tiles[0, :1, :1]).astype(jnp.bfloat16)
     slots = tile_rows * COLS + tile_cols
     levels = jnp.arange(depth_reg.shape[0], dtype=jnp.int32)
     level_hot = (depth_level[:, None] == levels[None, :]).astype(jnp.float32)
@@ -263,14 +274,14 @@
     weights = data_weight.reshape(-1, chunk * PACK)
 
     def products(own, sums):
-        other = swap(own)
-        first = lax.axis_index("core") == 0
-        lower, upper = jnp.where(first, own, other), jnp.where(first, other, own)
+        total = call(
+            forward_own_kernel, f32(group_rows, probes), (core, slots, own, tiles), smem=2
+        )
         partial = call(
-            forward_kernel,
+            forward_other_kernel,
             bf16(n_dp, chunk, probes),
-            (dp, slots, lower, upper, tiles, sums),
-            smem=2,
+            (dp, core, slots, swap(own), tiles, total, sums),
+            smem=3,
             scratch=[pltpu.VMEM((group_rows, probes), jnp.float32)],
         )
         weighted = call(
@@ -297,7 +308,7 @@
             scratch=[source],
         )
         coded = swap(coded.astype(jnp.float16)).astype(jnp.float32)
-        terms = call(pair_kernel, f32(n_z, cells + PARTS, probes), (keep, kept_sums, coded))
+        terms = call(pair_kernel, f32(n_z, cells + SUMS, probes), (keep, kept_sums, coded))
         return exchange(terms.astype(jnp.float16), "z").astype(jnp.float32)
 
     whole, extra = f32(cells, probes), f32(SUMS, probes)

time: 135 us -> 133 us (0.985)
  waiting for transfers between devices: 11.1 us -> 6.42 us
    all_to_all x1, waiting for transfers between devices: 9.64 us -> 5.99 us  [exchange(): return lax.all_to_all(value, axis, 0, 0)]
    pallas_call x13 -> x15, Pallas kernels: 8.34 us -> 9.65 us  [call(): pl.pallas_call(kernel, out_shape=out_shape, in_specs=[pl.BlockSpec(memory...]
  transfers between devices with their start and end apart: 5 -> 5, of which waited for: 4 -> 4; matrix products, arithmetic and copies ran while one was open for 1% -> 2% of each run, Pallas kernels for 2% -> 3%
where the time goes in v2:
time: 133 us
  blocking collectives  91.2 us (69%)
  starting transfers between devices  18.2 us (14%)
  Pallas kernels  9.65 us (7%)
  waiting for transfers between devices  6.42 us (5%)
  other arithmetic  3.92 us (3%)
  between operations  2.85 us (2%)
    all_to_all x7, blocking collectives, exchange(): return lax.all_to_all(value, axis, 0, 0)  91.2 us
    pallas_call x15, Pallas kernels, call(): pl.pallas_call(kernel, out_shape=out_shape, in_specs=[pl.BlockSpec(memory...  9.65 us
    ppermute x4, starting transfers between devices, swap(): return lax.ppermute(value, 'core', [(0, 1), (1, 0)])  9.21 us
    all_to_all x1, starting transfers between devices, exchange(): return lax.all_to_all(value, axis, 0, 0)  9.01 us
    all_to_all x1, waiting for transfers between devices, exchange(): return lax.all_to_all(value, axis, 0, 0)  5.99 us
  transfers between devices with their start and end apart: 5, of which 4 were waited for; matrix products, arithmetic and copies ran while one was open for 2% of the time, Pallas kernels for 3%

profile of v2, /device:TPU:1, one launch (start us, length us, event | category | flops | bytes accessed | tf_op | source)
XLA Modules:
  0.0 132.9 jit_solution(1521046292534683486)
XLA Ops:
  0.6 1.7 %multiply_convert_fusion = bf16[8,128,128]{2,1,0:T(8,128)(2,1)} fusion(f32[8]{0:T(128)S(1)} %compare_convert_fusion, f32[128,128]{1,0:T(8,128)} %right_ref.5), kind=kLoop, calls=%fused_computation.1 | loop fusion | flops 262144 | bytes 327712 | tf_op jit(solution)/shard_map/convert_element_type | solution.py:264
  2.3 9.0 %all-to-all-start = ((bf16[8,128,128]{2,1,0:T(8,128)(2,1)}), bf16[8,128,128]{2,1,0:T(8,128)(2,1)S(1)}, u32[]{:S(2)}, u32[]{:S(2)}) async-start(bf16[8,128,128]{2,1,0:T(8,128)(2,1)} %multiply_convert_fusion), calls=%async_computation | async-start | bytes 524288 | tf_op jit(solution)/shard_map/all_to_all | solution.py:246
  12.0 0.0 copy-start.2
  12.0 0.0 copy-start.3
  12.0 0.0 copy-start
  12.0 0.0 copy-start.4
  12.0 0.0 copy-start.5
  12.0 1.8 %broadcast_select_fusion.tiles = bf16[16,256,256]{2,1,0:T(8,128)(2,1)S(1)} fusion(bf16[16,256,256]{2,1,0:T(8,128)(2,1)} %param.8, pred[16]{0:T(512)(128)(4,1)S(1)} %iota_compare_fusion.1), kind=kLoop, calls=%fused_computation | loop fusion | flops 1048576 | bytes 4194320 | tf_op jit(solution)/shard_map/jit(_where)/select_n | solution.py:266
  13.9 0.5 slice.5
  15.7 6.0 %all-to-all-done = bf16[8,128,128]{2,1,0:T(8,128)(2,1)S(1)} async-done(((bf16[8,128,128]{2,1,0:T(8,128)(2,1)}), bf16[8,128,128]{2,1,0:T(8,128)(2,1)S(1)}, u32[]{:S(2)}, u32[]{:S(2)}) %all-to-all-start) | async-done | bytes 262176 | tf_op jit(solution)/shard_map/all_to_all | solution.py:246
  21.7 2.5 %collective-permute-start = (bf16[8,128,128]{2,1,0:T(8,128)(2,1)S(1)}, bf16[8,128,128]{2,1,0:T(8,128)(2,1)S(1)}, u32[]{:S(2)}, u32[]{:S(2)}) collective-permute-start(bf16[8,128,128]{2,1,0:T(8,128)(2,1)S(1)} %broadcast_multiply_fusion.own), channel_id=1, source_target_pairs={{0,1},{1,0},{2,3},{3,2},{4,5},{5,4},{6,7},{7,6},{8,9},{9,8},{10,11... | collective-permute-start | bytes 786440 | tf_op jit(solution)/shard_map/ppermute | solution.py:250
  24.3 0.0 copy-done.2
  24.3 0.0 copy-done.3
  24.3 0.1 select_reduce_fusion
  24.4 0.1 broadcast_in_dim.14.reg_ref
  24.4 0.0 copy-done
  24.5 0.0 copy-done.4
  24.5 0.0 copy-done.5
  24.5 1.0 shard_map.95.own_total
  25.5 0.0 copy-start.1
  25.6 0.0 collective-permute-done.other
  25.6 1.0 shard_map.97
  26.6 14.8 %all_to_all.40.got = bf16[16,64,128]{2,1,0:T(8,128)(2,1)S(1)} all-to-all(bf16[16,64,128]{2,1,0:T(8,128)(2,1)S(1)} %shard_map.97), channel_id=1, replica_groups=mesh['y'=4,'x'=4,'z'=8,'core'=2] {'y','x'}, dimensions={0} | all-to-all | bytes 524288 | tf_op jit(solution)/shard_map/all_to_all | solution.py:246
  41.4 0.0 copy-done.1
  41.4 0.1 shard_map.98
  41.6 10.7 %all_to_all.41.got = bf16[16,80,128]{2,1,0:T(8,128)(2,1)S(1)} all-to-all(bf16[16,80,128]{2,1,0:T(8,128)(2,1)S(1)} %shard_map.98), channel_id=1, replica_groups=mesh['y'=4,'x'=4,'z'=8,'core'=2] {'y','x'}, dimensions={0} | all-to-all | bytes 655360 | tf_op jit(solution)/shard_map/all_to_all | solution.py:246
  52.2 1.1 shard_map.99.after
  53.4 2.7 %collective-permute-start.1 = (f16[1048,128]{1,0:T(8,128)(2,1)S(1)}, f16[1048,128]{1,0:T(8,128)(2,1)S(1)}, u32[]{:S(2)}, u32[]{:S(2)}) collective-permute-start(f16[1048,128]{1,0:T(8,128)(2,1)S(1)} %convert_element_type.39), channel_id=1, source_target_pairs={{0,1},{1,0},{2,3},{3,2},{4,5},{5,4},{6,7},{7,6},{8,9},{9,8},{10,11... | collective-permute-start | bytes 804872 | tf_op jit(solution)/shard_map/ppermute | solution.py:250
  56.1 1.0 shard_map.100
  57.1 0.1 collective-permute-done.1
  57.3 0.1 shard_map.101
  57.5 15.1 %all_to_all.42 = f16[8,136,128]{2,1,0:T(8,128)(2,1)S(1)} all-to-all(f16[8,136,128]{2,1,0:T(8,128)(2,1)S(1)} %convert_element_type.41), channel_id=1, replica_groups=mesh['y'=4,'x'=4,'z'=8,'core'=2] {'z'}, dimensions={0} | all-to-all | bytes 557056 | tf_op jit(solution)/shard_map/all_to_all | solution.py:246
  72.6 0.1 shard_map.102
  72.7 14.2 %all_to_all.43.own = bf16[8,128,128]{2,1,0:T(8,128)(2,1)S(1)} all-to-all(bf16[8,128,128]{2,1,0:T(8,128)(2,1)S(1)} %get-tuple-element.13), channel_id=1, replica_groups=mesh['y'=4,'x'=4,'z'=8,'core'=2] {'z'}, dimensions={0} | all-to-all | bytes 524288 | tf_op jit(solution)/shard_map/all_to_all | solution.py:246
  86.9 1.0 collective-permute-start.2
  87.9 1.0 shard_map.103.own_total
  88.9 0.2 collective-permute-done.2.other
  89.1 1.0 shard_map.104
  90.1 10.7 %all_to_all.44.got = bf16[16,64,128]{2,1,0:T(8,128)(2,1)S(1)} all-to-all(bf16[16,64,128]{2,1,0:T(8,128)(2,1)S(1)} %shard_map.104), channel_id=1, replica_groups=mesh['y'=4,'x'=4,'z'=8,'core'=2] {'y','x'}, dimensions={0} | all-to-all | bytes 524288 | tf_op jit(solution)/shard_map/all_to_all | solution.py:246
  100.8 0.1 shard_map.105
  100.9 10.6 %all_to_all.45.got = bf16[16,80,128]{2,1,0:T(8,128)(2,1)S(1)} all-to-all(bf16[16,80,128]{2,1,0:T(8,128)(2,1)S(1)} %shard_map.105), channel_id=1, replica_groups=mesh['y'=4,'x'=4,'z'=8,'core'=2] {'y','x'}, dimensions={0} | all-to-all | bytes 655360 | tf_op jit(solution)/shard_map/all_to_all | solution.py:246
  111.6 1.1 shard_map.106.after
  112.7 2.9 %collective-permute-start.3 = (f16[1048,128]{1,0:T(8,128)(2,1)S(1)}, f16[1048,128]{1,0:T(8,128)(2,1)S(1)}, u32[]{:S(2)}, u32[]{:S(2)}) collective-permute-start(f16[1048,128]{1,0:T(8,128)(2,1)S(1)} %convert_element_type.43), channel_id=1, source_target_pairs={{0,1},{1,0},{2,3},{3,2},{4,5},{5,4},{6,7},{7,6},{8,9},{9,8},{10,11... | collective-permute-start | bytes 804872 | tf_op jit(solution)/shard_map/ppermute | solution.py:250
  115.6 1.0 shard_map.107
  116.7 0.1 collective-permute-done.3
  116.9 0.1 shard_map.108
  117.1 15.1 %all_to_all.46 = f16[8,136,128]{2,1,0:T(8,128)(2,1)S(1)} all-to-all(f16[8,136,128]{2,1,0:T(8,128)(2,1)S(1)} %convert_element_type.45), channel_id=1, replica_groups=mesh['y'=4,'x'=4,'z'=8,'core'=2] {'z'}, dimensions={0} | all-to-all | bytes 557056 | tf_op jit(solution)/shard_map/all_to_all | solution.py:246
  132.1 0.7 shard_map.109
  (13 shorter events, 0.4 us)
Async XLA Ops:
  2.3 19.4 %all-to-all-start = ((bf16[8,128,128]{2,1,0:T(8,128)(2,1)}), bf16[8,128,128]{2,1,0:T(8,128)(2,1)S(1)}, u32[]{:S(2)}, u32[]{:S(2)}) async-start(bf16[8,128,128]{2,1,0:T(8,128)(2,1)} %multiply_convert_fusion), calls=%async_computation | async-start | bytes 524288 | tf_op jit(solution)/shard_map/all_to_all | solution.py:246
  12.0 12.3 %copy-start.2 = (f32[32]{0:T(128)S(1)}, f32[32]{0:T(128)}, u32[]{:S(2)}) copy-start(f32[32]{0:T(128)} %param.14) | copy-start | bytes 388
  12.0 12.3 %copy-start.3 = (s32[128]{0:T(128)S(1)}, s32[128]{0:T(128)}, u32[]{:S(2)}) copy-start(s32[128]{0:T(128)} %param.13) | copy-start | bytes 1540
  12.0 12.4 %copy-start = (f32[128,128]{1,0:T(8,128)S(1)}, f32[128,128]{1,0:T(8,128)}, u32[]{:S(2)}) copy-start(f32[128,128]{1,0:T(8,128)} %right_ref.5) | copy-start | bytes 196612
  12.0 12.5 %copy-start.4 = (s32[16]{0:T(128)S(1)}, s32[16]{0:T(128)}, u32[]{:S(2)}) copy-start(s32[16]{0:T(128)} %param.10) | copy-start | bytes 196
  12.0 12.5 %copy-start.5 = (s32[16]{0:T(128)S(1)}, s32[16]{0:T(128)}, u32[]{:S(2)}) copy-start(s32[16]{0:T(128)} %param.9) | copy-start | bytes 196
  21.7 3.8 %collective-permute-start = (bf16[8,128,128]{2,1,0:T(8,128)(2,1)S(1)}, bf16[8,128,128]{2,1,0:T(8,128)(2,1)S(1)}, u32[]{:S(2)}, u32[]{:S(2)}) collective-permute-start(bf16[8,128,128]{2,1,0:T(8,128)(2,1)S(1)} %broadcast_multiply_fusion.own), channel_id=1, source_target_pairs={{0,1},{1,0},{2,3},{3,2},{4,5},{5,4},{6,7},{7,6},{8,9},{9,8},{10,11... | collective-permute-start | bytes 786440 | tf_op jit(solution)/shard_map/ppermute | solution.py:250
  25.5 15.9 %copy-start.1 = (f32[1024]{0:T(1024)S(1)}, f32[1024]{0:T(1024)}, u32[]{:S(2)}) copy-start(f32[1024]{0:T(1024)} %param.12) | copy-start | bytes 12292
  53.4 3.9 %collective-permute-start.1 = (f16[1048,128]{1,0:T(8,128)(2,1)S(1)}, f16[1048,128]{1,0:T(8,128)(2,1)S(1)}, u32[]{:S(2)}, u32[]{:S(2)}) collective-permute-start(f16[1048,128]{1,0:T(8,128)(2,1)S(1)} %convert_element_type.39), channel_id=1, source_target_pairs={{0,1},{1,0},{2,3},{3,2},{4,5},{5,4},{6,7},{7,6},{8,9},{9,8},{10,11... | collective-permute-start | bytes 804872 | tf_op jit(solution)/shard_map/ppermute | solution.py:250
  86.9 2.2 %collective-permute-start.2 = (bf16[8,128,128]{2,1,0:T(8,128)(2,1)S(1)}, bf16[8,128,128]{2,1,0:T(8,128)(2,1)S(1)}, u32[]{:S(2)}, u32[]{:S(2)}) collective-permute-start(bf16[8,128,128]{2,1,0:T(8,128)(2,1)S(1)} %all_to_all.43.own), channel_id=1, source_target_pairs={{0,1},{1,0},{2,3},{3,2},{4,5},{5,4},{6,7},{7,6},{8,9},{9,8},{10,11... | collective-permute-start | bytes 786440 | tf_op jit(solution)/shard_map/ppermute | solution.py:250
  112.7 4.1 %collective-permute-start.3 = (f16[1048,128]{1,0:T(8,128)(2,1)S(1)}, f16[1048,128]{1,0:T(8,128)(2,1)S(1)}, u32[]{:S(2)}, u32[]{:S(2)}) collective-permute-start(f16[1048,128]{1,0:T(8,128)(2,1)S(1)} %convert_element_type.43), channel_id=1, source_target_pairs={{0,1},{1,0},{2,3},{3,2},{4,5},{5,4},{6,7},{7,6},{8,9},{9,8},{10,11... | collective-permute-start | bytes 804872 | tf_op jit(solution)/shard_map/ppermute | solution.py:250

commit v3 on v2

--- a/solution.py
+++ b/solution.py
@@ -18,6 +18,7 @@
 TOP = 10.0
 SUM_TOP = 14.0
 VMEM_LIMIT = 16 * 1024 * 1024
+VMEM_WHOLE = 60 * 1024 * 1024
 
 
 def call(kernel, out_shape, operands, smem=0, scratch=()):
@@ -52,6 +53,21 @@
 def cell_sums(value, reg, image):
     square = value * value
     return rows_of(column_sum(reg * square), column_sum(square), column_sum(value * image))
+
+
+def copies_kernel(right_in, low_out, right, low, sems):
+    load = pltpu.make_async_copy(right_in, right, sems.at[0])
+    load.start()
+    load.wait()
+    low[...] = right[...].astype(jnp.bfloat16)
+    stores = [
+        pltpu.make_async_copy(low, low_out.at[block], sems.at[block + 1])
+        for block in range(low_out.shape[0])
+    ]
+    for store in stores:
+        store.start()
+    for store in stores:
+        store.wait()
 
 
 def start_kernel(right_ref, reg_ref, sums_ref):
@@ -260,8 +276,20 @@
     core = lax.axis_index("core").astype(jnp.int32).reshape(1)
     dp = lax.axis_index(DP).astype(jnp.int32).reshape(1)
 
-    one = (jnp.arange(n_z, dtype=jnp.int32) + core >= 0).astype(jnp.float32)
-    own = exchange((right_side[None] * one[:, None, None]).astype(jnp.bfloat16), "z")
+    anywhere = pl.BlockSpec(memory_space=pl.ANY)
+    copies = pl.pallas_call(
+        copies_kernel,
+        out_shape=bf16(n_z, cells, probes),
+        in_specs=[anywhere],
+        out_specs=anywhere,
+        scratch_shapes=[
+            pltpu.VMEM((cells, probes), jnp.float32),
+            pltpu.VMEM((cells, probes), jnp.bfloat16),
+            pltpu.SemaphoreType.DMA((n_z + 1,)),
+        ],
+        compiler_params=pltpu.CompilerParams(vmem_limit_bytes=VMEM_WHOLE),
+    )
+    own = exchange(copies(right_side), "z")
     live = jnp.arange(tiles.shape[0], dtype=jnp.int32) < tile_count
     tiles = jnp.where(live[:, None, None], tiles, jnp.zeros_like(tiles))
     own = own * (tiles[0, :1, :1] == tiles[0, :1, :1]).astype(jnp.bfloat16)

time: 133 us -> 133 us (level)
  other arithmetic: 3.92 us -> 2.26 us
  Pallas kernels: 9.65 us -> 11.3 us
    convert_element_type x2 -> x0, other arithmetic: 1.66 us -> none  [the longest x1 1.66 us: body(): (right_side[None] * one[:, None, None]).astype(jnp.bfloat16)]
    pallas_call x0 -> x1, Pallas kernels: none -> 1.63 us  [body(): own = exchange(copies(right_side), 'z')]
where the time goes in v3:
time: 133 us
  blocking collectives  91.1 us (68%)
  starting transfers between devices  18.3 us (14%)
  Pallas kernels  11.3 us (8%)
  waiting for transfers between devices  6.42 us (5%)
  between operations  2.85 us (2%)
  other arithmetic  2.26 us (2%)
    all_to_all x7, blocking collectives, exchange(): return lax.all_to_all(value, axis, 0, 0)  91.1 us
    pallas_call x15, Pallas kernels, call(): pl.pallas_call(kernel, out_shape=out_shape, in_specs=[pl.BlockSpec(memory...  9.65 us
    ppermute x4, starting transfers between devices, swap(): return lax.ppermute(value, 'core', [(0, 1), (1, 0)])  9.23 us
    all_to_all x1, starting transfers between devices, exchange(): return lax.all_to_all(value, axis, 0, 0)  9.03 us
    all_to_all x1, waiting for transfers between devices, exchange(): return lax.all_to_all(value, axis, 0, 0)  5.99 us
  transfers between devices with their start and end apart: 5, of which 4 were waited for; matrix products, arithmetic and copies ran while one was open for 2% of the time, Pallas kernels for 3%

profile of v3, /device:TPU:1, one launch (start us, length us, event | category | flops | bytes accessed | tf_op | source)
XLA Modules:
  0.0 132.8 jit_solution(15813583732315465217)
XLA Ops:
  0.6 1.6 %shard_map.95 = bf16[8,128,128]{2,1,0:T(8,128)(2,1)} custom-call(f32[128,128]{1,0:T(8,128)} %right_ref.5), custom_call_target="tpu_custom_call" | custom-call | tf_op jit(solution)/shard_map/pallas_call | solution.py:292
  2.3 9.0 %all-to-all-start = ((bf16[8,128,128]{2,1,0:T(8,128)(2,1)}), bf16[8,128,128]{2,1,0:T(8,128)(2,1)S(1)}, u32[]{:S(2)}, u32[]{:S(2)}) async-start(bf16[8,128,128]{2,1,0:T(8,128)(2,1)} %shard_map.95), calls=%async_computation | async-start | bytes 524288 | tf_op jit(solution)/shard_map/all_to_all | solution.py:262
  12.0 0.0 copy-start.2
  12.0 0.0 copy-start.3
  12.0 0.0 copy-start
  12.0 0.0 copy-start.4
  12.0 0.0 copy-start.5
  12.0 1.8 %broadcast_select_fusion.tiles = bf16[16,256,256]{2,1,0:T(8,128)(2,1)S(1)} fusion(bf16[16,256,256]{2,1,0:T(8,128)(2,1)} %param.8, pred[16]{0:T(512)(128)(4,1)S(1)} %iota_compare_fusion.1), kind=kLoop, calls=%fused_computation | loop fusion | flops 1048576 | bytes 4194320 | tf_op jit(solution)/shard_map/jit(_where)/select_n | solution.py:294
  13.9 0.5 slice.5
  15.7 6.0 %all-to-all-done = bf16[8,128,128]{2,1,0:T(8,128)(2,1)S(1)} async-done(((bf16[8,128,128]{2,1,0:T(8,128)(2,1)}), bf16[8,128,128]{2,1,0:T(8,128)(2,1)S(1)}, u32[]{:S(2)}, u32[]{:S(2)}) %all-to-all-start) | async-done | bytes 262176 | tf_op jit(solution)/shard_map/all_to_all | solution.py:262
  21.7 2.5 %collective-permute-start = (bf16[8,128,128]{2,1,0:T(8,128)(2,1)S(1)}, bf16[8,128,128]{2,1,0:T(8,128)(2,1)S(1)}, u32[]{:S(2)}, u32[]{:S(2)}) collective-permute-start(bf16[8,128,128]{2,1,0:T(8,128)(2,1)S(1)} %broadcast_multiply_fusion.own), channel_id=1, source_target_pairs={{0,1},{1,0},{2,3},{3,2},{4,5},{5,4},{6,7},{7,6},{8,9},{9,8},{10,11... | collective-permute-start | bytes 786440 | tf_op jit(solution)/shard_map/ppermute | solution.py:266
  24.2 0.0 copy-done.2
  24.2 0.0 copy-done.3
  24.2 0.1 select_reduce_fusion
  24.3 0.1 broadcast_in_dim.14.reg_ref
  24.4 0.0 copy-done
  24.5 0.0 copy-done.4
  24.5 0.0 copy-done.5
  24.5 1.0 shard_map.96.own_total
  25.5 0.0 copy-start.1
  25.5 0.0 collective-permute-done.other
  25.5 1.0 shard_map.98
  26.6 14.8 %all_to_all.40.got = bf16[16,64,128]{2,1,0:T(8,128)(2,1)S(1)} all-to-all(bf16[16,64,128]{2,1,0:T(8,128)(2,1)S(1)} %shard_map.98), channel_id=1, replica_groups=mesh['y'=4,'x'=4,'z'=8,'core'=2] {'y','x'}, dimensions={0} | all-to-all | bytes 524288 | tf_op jit(solution)/shard_map/all_to_all | solution.py:262
  41.4 0.0 copy-done.1
  41.4 0.1 shard_map.99
  41.5 10.7 %all_to_all.41.got = bf16[16,80,128]{2,1,0:T(8,128)(2,1)S(1)} all-to-all(bf16[16,80,128]{2,1,0:T(8,128)(2,1)S(1)} %shard_map.99), channel_id=1, replica_groups=mesh['y'=4,'x'=4,'z'=8,'core'=2] {'y','x'}, dimensions={0} | all-to-all | bytes 655360 | tf_op jit(solution)/shard_map/all_to_all | solution.py:262
  52.2 1.1 shard_map.100.after
  53.3 2.7 %collective-permute-start.1 = (f16[1048,128]{1,0:T(8,128)(2,1)S(1)}, f16[1048,128]{1,0:T(8,128)(2,1)S(1)}, u32[]{:S(2)}, u32[]{:S(2)}) collective-permute-start(f16[1048,128]{1,0:T(8,128)(2,1)S(1)} %convert_element_type.27), channel_id=1, source_target_pairs={{0,1},{1,0},{2,3},{3,2},{4,5},{5,4},{6,7},{7,6},{8,9},{9,8},{10,11... | collective-permute-start | bytes 804872 | tf_op jit(solution)/shard_map/ppermute | solution.py:266
  56.1 1.0 shard_map.101
  57.1 0.1 collective-permute-done.1
  57.3 0.1 shard_map.102
  57.5 15.1 %all_to_all.42 = f16[8,136,128]{2,1,0:T(8,128)(2,1)S(1)} all-to-all(f16[8,136,128]{2,1,0:T(8,128)(2,1)S(1)} %convert_element_type.29), channel_id=1, replica_groups=mesh['y'=4,'x'=4,'z'=8,'core'=2] {'z'}, dimensions={0} | all-to-all | bytes 557056 | tf_op jit(solution)/shard_map/all_to_all | solution.py:262
  72.6 0.1 shard_map.103
  72.7 14.2 %all_to_all.43.own = bf16[8,128,128]{2,1,0:T(8,128)(2,1)S(1)} all-to-all(bf16[8,128,128]{2,1,0:T(8,128)(2,1)S(1)} %get-tuple-element.13), channel_id=1, replica_groups=mesh['y'=4,'x'=4,'z'=8,'core'=2] {'z'}, dimensions={0} | all-to-all | bytes 524288 | tf_op jit(solution)/shard_map/all_to_all | solution.py:262
  86.9 1.0 collective-permute-start.2
  87.9 1.0 shard_map.104.own_total
  88.9 0.2 collective-permute-done.2.other
  89.1 1.0 shard_map.105
  90.1 10.7 %all_to_all.44.got = bf16[16,64,128]{2,1,0:T(8,128)(2,1)S(1)} all-to-all(bf16[16,64,128]{2,1,0:T(8,128)(2,1)S(1)} %shard_map.105), channel_id=1, replica_groups=mesh['y'=4,'x'=4,'z'=8,'core'=2] {'y','x'}, dimensions={0} | all-to-all | bytes 524288 | tf_op jit(solution)/shard_map/all_to_all | solution.py:262
  100.8 0.1 shard_map.106
  100.9 10.6 %all_to_all.45.got = bf16[16,80,128]{2,1,0:T(8,128)(2,1)S(1)} all-to-all(bf16[16,80,128]{2,1,0:T(8,128)(2,1)S(1)} %shard_map.106), channel_id=1, replica_groups=mesh['y'=4,'x'=4,'z'=8,'core'=2] {'y','x'}, dimensions={0} | all-to-all | bytes 655360 | tf_op jit(solution)/shard_map/all_to_all | solution.py:262
  111.5 1.1 shard_map.107.after
  112.7 2.9 %collective-permute-start.3 = (f16[1048,128]{1,0:T(8,128)(2,1)S(1)}, f16[1048,128]{1,0:T(8,128)(2,1)S(1)}, u32[]{:S(2)}, u32[]{:S(2)}) collective-permute-start(f16[1048,128]{1,0:T(8,128)(2,1)S(1)} %convert_element_type.31), channel_id=1, source_target_pairs={{0,1},{1,0},{2,3},{3,2},{4,5},{5,4},{6,7},{7,6},{8,9},{9,8},{10,11... | collective-permute-start | bytes 804872 | tf_op jit(solution)/shard_map/ppermute | solution.py:266
  115.6 1.0 shard_map.108
  116.7 0.1 collective-permute-done.3
  116.8 0.1 shard_map.109
  117.0 15.1 %all_to_all.46 = f16[8,136,128]{2,1,0:T(8,128)(2,1)S(1)} all-to-all(f16[8,136,128]{2,1,0:T(8,128)(2,1)S(1)} %convert_element_type.33), channel_id=1, replica_groups=mesh['y'=4,'x'=4,'z'=8,'core'=2] {'z'}, dimensions={0} | all-to-all | bytes 557056 | tf_op jit(solution)/shard_map/all_to_all | solution.py:262
  132.1 0.7 shard_map.110
  (12 shorter events, 0.4 us)
Async XLA Ops:
  2.3 19.4 %all-to-all-start = ((bf16[8,128,128]{2,1,0:T(8,128)(2,1)}), bf16[8,128,128]{2,1,0:T(8,128)(2,1)S(1)}, u32[]{:S(2)}, u32[]{:S(2)}) async-start(bf16[8,128,128]{2,1,0:T(8,128)(2,1)} %shard_map.95), calls=%async_computation | async-start | bytes 524288 | tf_op jit(solution)/shard_map/all_to_all | solution.py:262
  12.0 12.3 %copy-start.2 = (f32[32]{0:T(128)S(1)}, f32[32]{0:T(128)}, u32[]{:S(2)}) copy-start(f32[32]{0:T(128)} %param.14) | copy-start | bytes 388
  12.0 12.3 %copy-start.3 = (s32[128]{0:T(128)S(1)}, s32[128]{0:T(128)}, u32[]{:S(2)}) copy-start(s32[128]{0:T(128)} %param.13) | copy-start | bytes 1540
  12.0 12.4 %copy-start = (f32[128,128]{1,0:T(8,128)S(1)}, f32[128,128]{1,0:T(8,128)}, u32[]{:S(2)}) copy-start(f32[128,128]{1,0:T(8,128)} %right_ref.5) | copy-start | bytes 196612
  12.0 12.5 %copy-start.4 = (s32[16]{0:T(128)S(1)}, s32[16]{0:T(128)}, u32[]{:S(2)}) copy-start(s32[16]{0:T(128)} %param.10) | copy-start | bytes 196
  12.0 12.5 %copy-start.5 = (s32[16]{0:T(128)S(1)}, s32[16]{0:T(128)}, u32[]{:S(2)}) copy-start(s32[16]{0:T(128)} %param.9) | copy-start | bytes 196
  21.7 3.8 %collective-permute-start = (bf16[8,128,128]{2,1,0:T(8,128)(2,1)S(1)}, bf16[8,128,128]{2,1,0:T(8,128)(2,1)S(1)}, u32[]{:S(2)}, u32[]{:S(2)}) collective-permute-start(bf16[8,128,128]{2,1,0:T(8,128)(2,1)S(1)} %broadcast_multiply_fusion.own), channel_id=1, source_target_pairs={{0,1},{1,0},{2,3},{3,2},{4,5},{5,4},{6,7},{7,6},{8,9},{9,8},{10,11... | collective-permute-start | bytes 786440 | tf_op jit(solution)/shard_map/ppermute | solution.py:266
  25.5 15.9 %copy-start.1 = (f32[1024]{0:T(1024)S(1)}, f32[1024]{0:T(1024)}, u32[]{:S(2)}) copy-start(f32[1024]{0:T(1024)} %param.12) | copy-start | bytes 12292
  53.3 3.9 %collective-permute-start.1 = (f16[1048,128]{1,0:T(8,128)(2,1)S(1)}, f16[1048,128]{1,0:T(8,128)(2,1)S(1)}, u32[]{:S(2)}, u32[]{:S(2)}) collective-permute-start(f16[1048,128]{1,0:T(8,128)(2,1)S(1)} %convert_element_type.27), channel_id=1, source_target_pairs={{0,1},{1,0},{2,3},{3,2},{4,5},{5,4},{6,7},{7,6},{8,9},{9,8},{10,11... | collective-permute-start | bytes 804872 | tf_op jit(solution)/shard_map/ppermute | solution.py:266
  86.9 2.2 %collective-permute-start.2 = (bf16[8,128,128]{2,1,0:T(8,128)(2,1)S(1)}, bf16[8,128,128]{2,1,0:T(8,128)(2,1)S(1)}, u32[]{:S(2)}, u32[]{:S(2)}) collective-permute-start(bf16[8,128,128]{2,1,0:T(8,128)(2,1)S(1)} %all_to_all.43.own), channel_id=1, source_target_pairs={{0,1},{1,0},{2,3},{3,2},{4,5},{5,4},{6,7},{7,6},{8,9},{9,8},{10,11... | collective-permute-start | bytes 786440 | tf_op jit(solution)/shard_map/ppermute | solution.py:266
  112.7 4.1 %collective-permute-start.3 = (f16[1048,128]{1,0:T(8,128)(2,1)S(1)}, f16[1048,128]{1,0:T(8,128)(2,1)S(1)}, u32[]{:S(2)}, u32[]{:S(2)}) collective-permute-start(f16[1048,128]{1,0:T(8,128)(2,1)S(1)} %convert_element_type.31), channel_id=1, source_target_pairs={{0,1},{1,0},{2,3},{3,2},{4,5},{5,4},{6,7},{7,6},{8,9},{9,8},{10,11... | collective-permute-start | bytes 804872 | tf_op jit(solution)/shard_map/ppermute | solution.py:266

commit v4 on v3

--- a/solution.py
+++ b/solution.py
@@ -13,6 +13,8 @@
 CORES = 2
 SIDE = 4
 KINDS = 3
+CELLS = 128
+FOUR = 4
 COLS = 8
 PACK = 2
 TOP = 10.0
@@ -98,6 +100,8 @@
 
 
 def padded(rows):
+    if rows.shape[0] == PARTS:
+        return rows
     blank = jnp.zeros((PARTS - rows.shape[0], rows.shape[1]), jnp.float32)
     return jnp.concatenate([rows, blank], axis=0)
 
@@ -218,6 +222,75 @@
         out[block, cells:] = jnp.concatenate([high, sums - high, sum_power, power], axis=0)
 
 
+def pair_sum(keep, kept_sums, coded, block):
+    cells = CELLS
+    blocks = keep.shape[0] // cells
+    tail = coded[blocks * cells :]
+    at = TERMS * KINDS
+    sums = kept_sums[:KINDS] + join(tail[:at]) * jnp.exp2(tail[at : at + KINDS] - TOP)
+    rows = slice(block * cells, (block + 1) * cells)
+    back = jnp.exp2(tail[PARTS + block : PARTS + block + 1] - TOP)
+    return keep[rows] + coded[rows] * back, sums
+
+
+def emit(kept_blocks, sent_blocks, sums, kept, coded, kept_sums):
+    cells = CELLS
+    powers = []
+    for at, block in enumerate(kept_blocks):
+        kept[at * cells : (at + 1) * cells] = block
+    for at, block in enumerate(sent_blocks):
+        power = exponent(jnp.max(jnp.abs(block), axis=0, keepdims=True))
+        coded[at * cells : (at + 1) * cells] = block * jnp.exp2(TOP - power)
+        powers.append(power)
+    power = exponent(jnp.abs(sums))
+    terms = split(sums * jnp.exp2(TOP - power))
+    coded[len(sent_blocks) * cells :] = padded(jnp.concatenate([terms, power] + powers, axis=0))
+    kept_sums[...] = rows_of(*[sums[kind : kind + 1] for kind in range(KINDS)])
+
+
+def absorb(kept, coded, kept_sums, order):
+    cells = CELLS
+    tail = coded[kept.shape[0] :]
+    at = TERMS * KINDS
+    blocks = []
+    for block, place in enumerate(order):
+        arrived = coded[place * cells : (place + 1) * cells]
+        power = tail[at + KINDS + place : at + KINDS + place + 1]
+        blocks.append(kept[block * cells : (block + 1) * cells] + arrived * jnp.exp2(power - TOP))
+    return blocks, kept_sums[:KINDS] + join(tail[:at]) * jnp.exp2(tail[at : at + KINDS] - TOP)
+
+
+def spread_kernel(height, keep, keep_sums, swapped, kept, coded, kept_sums, total):
+    cells = CELLS
+    for block in range(COLS):
+        part, sums = pair_sum(keep, keep_sums, swapped, block)
+        total[block * cells : (block + 1) * cells] = part
+    half, own = height[0] // FOUR, lax.rem(height[0], FOUR)
+
+    def blocks(chips):
+        at = [z for chip in chips for z in (half * FOUR + chip, (2 - half) * FOUR - 1 - chip)]
+        return [total[rows_at(z * cells, cells), :] for z in at]
+
+    emit(
+        blocks([own, jnp.bitwise_xor(own, 2)]),
+        blocks([jnp.bitwise_xor(own, 1), jnp.bitwise_xor(own, 3)]),
+        sums,
+        kept,
+        coded,
+        kept_sums,
+    )
+
+
+def halve_kernel(kept_in, coded_in, sums_in, kept, coded, kept_sums):
+    blocks, sums = absorb(kept_in, coded_in, sums_in, range(4))
+    emit(blocks[:2], blocks[2:], sums, kept, coded, kept_sums)
+
+
+def cross_kernel(kept_in, coded_in, sums_in, right_ref, reg_ref, kept, coded, kept_sums):
+    (own, other), sums = absorb(kept_in, coded_in, sums_in, range(2))
+    emit([own, other], [own + reg_ref[...] * right_ref[...], other], sums, kept, coded, kept_sums)
+
+
 def summed(got, cells):
     total, sums = 0.0, 0.0
     for part in range(got.shape[0]):
@@ -228,18 +301,20 @@
     return total, sums
 
 
-def first_update_kernel(got, right_ref, reg_ref, residual_ref, image_ref, low_ref, sums_ref, keep_ref):
+def first_update_kernel(
+    height, kept, coded, kept_sums, gathered, right_ref, reg_ref, residual_ref, image_ref, low_ref, sums_ref, keep_ref
+):
+    (terms, other), sums = absorb(kept, coded, kept_sums, (1, 0))
     right, reg = right_ref[...], reg_ref[...]
-    terms, sums = summed(got, right.shape[0])
     curve, norm = sums[0:1], sums[1:2]
     alpha = norm / curve
     image = terms + reg * right
     residual = right - alpha * image
     residual_ref[...] = residual
     image_ref[...] = image
-    low = residual.astype(jnp.bfloat16)
-    for block in range(low_ref.shape[0]):
-        low_ref[block] = low
+    low_ref[0] = residual.astype(jnp.bfloat16)
+    other_right = gathered[COLS - 1 - height[0]].astype(jnp.float32)
+    low_ref[1] = (other_right - alpha * other).astype(jnp.bfloat16)
     sums_ref[...] = cell_sums(residual, reg, image)
     keep_ref[...] = rows_of(norm, curve, alpha)
 
@@ -262,6 +337,27 @@
     return lax.all_to_all(value, axis, 0, 0)
 
 
+def along_z(value, to):
+    pairs = [
+        (z * CORES + core, to(z) * CORES + core)
+        for z in range(lax.axis_size("z"))
+        for core in range(CORES)
+    ]
+    return lax.ppermute(value, ("z", "core"), pairs)
+
+
+def near(z):
+    return z ^ 1
+
+
+def far(z):
+    return z ^ 2
+
+
+def mirror(z):
+    return COLS - 1 - z
+
+
 def swap(value):
     return lax.ppermute(value, "core", [(0, 1), (1, 0)])
 
@@ -274,6 +370,7 @@
     chunk = group_rows // n_dp
     col_blocks = cells * CORES * n_z // tile
     core = lax.axis_index("core").astype(jnp.int32).reshape(1)
+    height = lax.axis_index("z").astype(jnp.int32).reshape(1)
     dp = lax.axis_index(DP).astype(jnp.int32).reshape(1)
 
     anywhere = pl.BlockSpec(memory_space=pl.ANY)
@@ -294,6 +391,11 @@
     tiles = jnp.where(live[:, None, None], tiles, jnp.zeros_like(tiles))
     own = own * (tiles[0, :1, :1] == tiles[0, :1, :1]).astype(jnp.bfloat16)
     slots = tile_rows * COLS + tile_cols
+    half, chip = height >> 2, height & 3
+    same = (tile_cols >> 2) == half
+    apart = jnp.where(same, tile_cols & 3, 3 - (tile_cols & 3)) ^ chip
+    place = ((apart & 1) * 2 + (apart >> 1)) * 2 + jnp.where(same, 0, 1)
+    last_slots = tile_rows * COLS + place
     levels = jnp.arange(depth_reg.shape[0], dtype=jnp.int32)
     level_hot = (depth_level[:, None] == levels[None, :]).astype(jnp.float32)
     reg_cell = jnp.sum(level_hot * depth_reg[None, :], axis=1)
@@ -301,14 +403,14 @@
     sums = call(start_kernel, f32(SUMS, probes), (right_side, reg))
     weights = data_weight.reshape(-1, chunk * PACK)
 
-    def products(own, sums):
+    def products(own, sums, places):
         total = call(
-            forward_own_kernel, f32(group_rows, probes), (core, slots, own, tiles), smem=2
+            forward_own_kernel, f32(group_rows, probes), (core, places, own, tiles), smem=2
         )
         partial = call(
             forward_other_kernel,
             bf16(n_dp, chunk, probes),
-            (dp, core, slots, swap(own), tiles, total, sums),
+            (dp, core, places, swap(own), tiles, total, sums),
             smem=3,
             scratch=[pltpu.VMEM((group_rows, probes), jnp.float32)],
         )
@@ -335,20 +437,44 @@
             smem=2,
             scratch=[source],
         )
-        coded = swap(coded.astype(jnp.float16)).astype(jnp.float32)
-        terms = call(pair_kernel, f32(n_z, cells + SUMS, probes), (keep, kept_sums, coded))
-        return exchange(terms.astype(jnp.float16), "z").astype(jnp.float32)
+        return keep, kept_sums, swap(coded.astype(jnp.float16)).astype(jnp.float32)
+
+    def halved(kernel, blocks, operands, to, smem=0, scratch=()):
+        kept, coded, sums = call(
+            kernel,
+            (f32(blocks * cells, probes), f32(blocks * cells + PARTS, probes), f32(SUMS, probes)),
+            operands,
+            smem=smem,
+            scratch=scratch,
+        )
+        return kept, along_z(coded.astype(jnp.float16), to).astype(jnp.float32), sums
 
     whole, extra = f32(cells, probes), f32(SUMS, probes)
+    terms = products(own, sums, slots)
+    terms = halved(
+        spread_kernel,
+        4,
+        (height, *terms),
+        near,
+        smem=1,
+        scratch=[pltpu.VMEM((n_z * cells, probes), jnp.float32)],
+    )
+    terms = halved(halve_kernel, 2, terms, far)
+    terms = halved(cross_kernel, 2, (*terms, right_side, reg), mirror)
     residual, image, low, sums, keep = call(
         first_update_kernel,
-        (whole, whole, bf16(n_z, cells, probes), extra, extra),
-        (products(own, sums), right_side, reg),
-    )
+        (whole, whole, bf16(2, cells, probes), extra, extra),
+        (height, *terms, own, right_side, reg),
+        smem=1,
+    )
+    low = jnp.concatenate([low, along_z(low, far)], axis=0)
+    low = jnp.concatenate([low, along_z(low, near)], axis=0)
+    terms = call(pair_kernel, f32(n_z, cells + SUMS, probes), products(low, sums, last_slots))
+    got = exchange(terms.astype(jnp.float16), "z").astype(jnp.float32)
     return call(
         last_update_kernel,
         (whole, whole),
-        (products(exchange(low, "z"), sums), right_side, reg, residual, image, keep),
+        (got, right_side, reg, residual, image, keep),
     )
 
 

time: 133 us -> 132 us (level)
  blocking collectives: 91.1 us -> 61.3 us
  waiting for transfers between devices: 6.42 us -> 29.2 us
  starting transfers between devices: 18.3 us -> 23.5 us
    all_to_all x7 -> x5, blocking collectives: 91.1 us -> 61.3 us  [exchange(): return lax.all_to_all(value, axis, 0, 0)]
    ppermute x0 -> x5, waiting for transfers between devices: none -> 22.8 us  [along_z(): return lax.ppermute(value, ('z', 'core'), pairs)]
    ppermute x4, starting transfers between devices: 9.23 us -> 12.9 us  [swap(): return lax.ppermute(value, 'core', [(0, 1), (1, 0)])]
    ppermute x0 -> x5, starting transfers between devices: none -> 1.54 us  [along_z(): return lax.ppermute(value, ('z', 'core'), pairs)]
    pallas_call x15 -> x17, Pallas kernels: 9.65 us -> 9.76 us  [call(): pl.pallas_call(kernel, out_shape=out_shape, in_specs=[pl.BlockSpec(memory...]
  transfers between devices with their start and end apart: 5 -> 10, of which waited for: 4 -> 9; matrix products, arithmetic and copies ran while one was open for 2% -> 2% of each run, Pallas kernels for 3% -> 3%
where the time goes in v4:
time: 132 us; the launch traced here: 131 us
  blocking collectives  61.3 us (46%)
  waiting for transfers between devices  29.2 us (22%)
  starting transfers between devices  23.5 us (18%)
  Pallas kernels  11.4 us (9%)
  between operations  2.91 us (2%)
  other arithmetic  2.3 us (2%)
    all_to_all x5, blocking collectives, exchange(): return lax.all_to_all(value, axis, 0, 0)  61.3 us
    ppermute x5, waiting for transfers between devices, along_z(): return lax.ppermute(value, ('z', 'core'), pairs)  22.8 us
    ppermute x4, starting transfers between devices, swap(): return lax.ppermute(value, 'core', [(0, 1), (1, 0)])  12.9 us
    pallas_call x17, Pallas kernels, call(): pl.pallas_call(kernel, out_shape=out_shape, in_specs=[pl.BlockSpec(memory...  9.76 us
    all_to_all x1, starting transfers between devices, exchange(): return lax.all_to_all(value, axis, 0, 0)  9.03 us
    all_to_all x1, waiting for transfers between devices, exchange(): return lax.all_to_all(value, axis, 0, 0)  5.99 us
  transfers between devices with their start and end apart: 10, of which 9 were waited for; matrix products, arithmetic and copies ran while one was open for 2% of the time, Pallas kernels for 3%

profile of v4, /device:TPU:1, one launch (start us, length us, event | category | flops | bytes accessed | tf_op | source)
XLA Modules:
  0.0 131.3 jit_solution(14011396732022150032)
XLA Ops:
  0.6 1.6 %shard_map.95 = bf16[8,128,128]{2,1,0:T(8,128)(2,1)} custom-call(f32[128,128]{1,0:T(8,128)} %right_ref.7), custom_call_target="tpu_custom_call" | custom-call | tf_op jit(solution)/shard_map/pallas_call | solution.py:389
  2.3 9.0 %all-to-all-start = ((bf16[8,128,128]{2,1,0:T(8,128)(2,1)}), bf16[8,128,128]{2,1,0:T(8,128)(2,1)S(1)}, u32[]{:S(2)}, u32[]{:S(2)}) async-start(bf16[8,128,128]{2,1,0:T(8,128)(2,1)} %shard_map.95), calls=%async_computation | async-start | bytes 524288 | tf_op jit(solution)/shard_map/all_to_all | solution.py:337
  12.0 0.0 copy-start
  12.0 0.0 copy-start.2
  12.0 1.8 %broadcast_select_fusion.tiles = bf16[16,256,256]{2,1,0:T(8,128)(2,1)S(1)} fusion(bf16[16,256,256]{2,1,0:T(8,128)(2,1)} %param.8, pred[16]{0:T(512)(128)(4,1)S(1)} %iota_compare_fusion.1), kind=kLoop, calls=%fused_computation | loop fusion | flops 1048576 | bytes 4194320 | tf_op jit(solution)/shard_map/jit(_where)/select_n | solution.py:391
  13.8 0.5 slice.5
  15.7 6.0 %all-to-all-done = bf16[8,128,128]{2,1,0:T(8,128)(2,1)S(1)} async-done(((bf16[8,128,128]{2,1,0:T(8,128)(2,1)}), bf16[8,128,128]{2,1,0:T(8,128)(2,1)S(1)}, u32[]{:S(2)}, u32[]{:S(2)}) %all-to-all-start) | async-done | bytes 262176 | tf_op jit(solution)/shard_map/all_to_all | solution.py:337
  21.7 2.5 %collective-permute-start = (bf16[8,128,128]{2,1,0:T(8,128)(2,1)S(1)}, bf16[8,128,128]{2,1,0:T(8,128)(2,1)S(1)}, u32[]{:S(2)}, u32[]{:S(2)}) collective-permute-start(bf16[8,128,128]{2,1,0:T(8,128)(2,1)S(1)} %broadcast_multiply_fusion.own.gathered), channel_id=1, source_target_pairs={{0,1},{1,0},{2,3},{3,2},{4,5},{5,4},{6,7},{7,6},{8,9},{9,8},{10,11... | collective-permute-start | bytes 786440 | tf_op jit(solution)/shard_map/ppermute | solution.py:362
  24.2 0.1 select_reduce_fusion
  24.3 0.1 broadcast_in_dim.31.reg_ref
  24.5 1.0 shard_map.96.own_total
  25.5 0.0 copy-start.1
  25.5 1.0 shard_map.98
  26.6 14.8 %all_to_all.30.got = bf16[16,64,128]{2,1,0:T(8,128)(2,1)S(1)} all-to-all(bf16[16,64,128]{2,1,0:T(8,128)(2,1)S(1)} %shard_map.98), channel_id=1, replica_groups=mesh['y'=4,'x'=4,'z'=8,'core'=2] {'y','x'}, dimensions={0} | all-to-all | bytes 524288 | tf_op jit(solution)/shard_map/all_to_all | solution.py:337
  41.4 0.1 shard_map.99
  41.5 10.7 %all_to_all.31.got = bf16[16,80,128]{2,1,0:T(8,128)(2,1)S(1)} all-to-all(bf16[16,80,128]{2,1,0:T(8,128)(2,1)S(1)} %shard_map.99), channel_id=1, replica_groups=mesh['y'=4,'x'=4,'z'=8,'core'=2] {'y','x'}, dimensions={0} | all-to-all | bytes 655360 | tf_op jit(solution)/shard_map/all_to_all | solution.py:337
  52.2 1.1 shard_map.100.after
  53.3 2.7 %collective-permute-start.1 = (f16[1048,128]{1,0:T(8,128)(2,1)S(1)}, f16[1048,128]{1,0:T(8,128)(2,1)S(1)}, u32[]{:S(2)}, u32[]{:S(2)}) collective-permute-start(f16[1048,128]{1,0:T(8,128)(2,1)S(1)} %convert_element_type.39), channel_id=1, source_target_pairs={{0,1},{1,0},{2,3},{3,2},{4,5},{5,4},{6,7},{7,6},{8,9},{9,8},{10,11... | collective-permute-start | bytes 804872 | tf_op jit(solution)/shard_map/ppermute | solution.py:362
  56.1 1.0 shard_map.101
  57.1 0.1 collective-permute-done.1
  57.3 0.1 shard_map.102
  57.4 0.4 collective-permute-start.2
  57.8 4.5 %collective-permute-done.2 = f16[528,128]{1,0:T(8,128)(2,1)S(1)} collective-permute-done((f16[528,128]{1,0:T(8,128)(2,1)S(1)}, f16[528,128]{1,0:T(8,128)(2,1)S(1)}, u32[]{:S(2)}, u32[]{:S(2)}) %collective-permute-start.2) | collective-permute-done | bytes 135200 | tf_op jit(solution)/shard_map/ppermute | solution.py:346
  62.4 0.1 shard_map.103
  62.5 0.1 collective-permute-start.3
  62.6 4.8 %collective-permute-done.3 = f16[272,128]{1,0:T(8,128)(2,1)S(1)} collective-permute-done((f16[272,128]{1,0:T(8,128)(2,1)S(1)}, f16[272,128]{1,0:T(8,128)(2,1)S(1)}, u32[]{:S(2)}, u32[]{:S(2)}) %collective-permute-start.3) | collective-permute-done | bytes 69664 | tf_op jit(solution)/shard_map/ppermute | solution.py:346
  67.4 0.1 shard_map.104
  67.5 0.1 collective-permute-start.4
  67.6 5.1 %collective-permute-done.4 = f16[272,128]{1,0:T(8,128)(2,1)S(1)} collective-permute-done((f16[272,128]{1,0:T(8,128)(2,1)S(1)}, f16[272,128]{1,0:T(8,128)(2,1)S(1)}, u32[]{:S(2)}, u32[]{:S(2)}) %collective-permute-start.4) | collective-permute-done | bytes 69664 | tf_op jit(solution)/shard_map/ppermute | solution.py:346
  72.7 0.1 shard_map.105
  72.7 0.7 collective-permute-start.5
  73.4 4.1 %collective-permute-done.5 = bf16[2,128,128]{2,1,0:T(8,128)(2,1)S(1)} collective-permute-done((bf16[2,128,128]{2,1,0:T(8,128)(2,1)S(1)}, bf16[2,128,128]{2,1,0:T(8,128)(2,1)S(1)}, u32[]{:S(2)}, u32[]{:S(2)}) %collective-permute-start.5) | collective-permute-done | bytes 65568 | tf_op jit(solution)/shard_map/ppermute | solution.py:346
  77.6 0.3 collective-permute-start.6
  77.9 4.3 %collective-permute-done.6 = bf16[4,128,128]{2,1,0:T(8,128)(2,1)S(1)} collective-permute-done((bf16[4,128,128]{2,1,0:T(8,128)(2,1)S(1)}, bf16[4,128,128]{2,1,0:T(8,128)(2,1)S(1)}, u32[]{:S(2)}, u32[]{:S(2)}) %collective-permute-start.6) | collective-permute-done | bytes 131104 | tf_op jit(solution)/shard_map/ppermute | solution.py:346
  82.2 4.7 %collective-permute-start.7 = (bf16[8,128,128]{2,1,0:T(8,128)(2,1)S(1)}, bf16[8,128,128]{2,1,0:T(8,128)(2,1)S(1)}, u32[]{:S(2)}, u32[]{:S(2)}) collective-permute-start(bf16[8,128,128]{2,1,0:T(8,128)(2,1)S(1)} %constant_dynamic-update-slice_fusion.own), channel_id=1, source_target_pairs={{0,1},{1,0},{2,3},{3,2},{4,5},{5,4},{6,7},{7,6},{8,9},{9,8},{10,11... | collective-permute-start | bytes 786440 | tf_op jit(solution)/shard_map/ppermute | solution.py:362
  86.9 1.0 shard_map.106.own_total
  87.9 0.2 collective-permute-done.7.other
  88.1 1.0 shard_map.107
  89.1 10.7 %all_to_all.32.got = bf16[16,64,128]{2,1,0:T(8,128)(2,1)S(1)} all-to-all(bf16[16,64,128]{2,1,0:T(8,128)(2,1)S(1)} %shard_map.107), channel_id=1, replica_groups=mesh['y'=4,'x'=4,'z'=8,'core'=2] {'y','x'}, dimensions={0} | all-to-all | bytes 524288 | tf_op jit(solution)/shard_map/all_to_all | solution.py:337
  99.8 0.1 shard_map.108
  99.9 10.6 %all_to_all.33.got = bf16[16,80,128]{2,1,0:T(8,128)(2,1)S(1)} all-to-all(bf16[16,80,128]{2,1,0:T(8,128)(2,1)S(1)} %shard_map.108), channel_id=1, replica_groups=mesh['y'=4,'x'=4,'z'=8,'core'=2] {'y','x'}, dimensions={0} | all-to-all | bytes 655360 | tf_op jit(solution)/shard_map/all_to_all | solution.py:337
  110.5 1.1 shard_map.109.after
  111.7 2.9 %collective-permute-start.8 = (f16[1048,128]{1,0:T(8,128)(2,1)S(1)}, f16[1048,128]{1,0:T(8,128)(2,1)S(1)}, u32[]{:S(2)}, u32[]{:S(2)}) collective-permute-start(f16[1048,128]{1,0:T(8,128)(2,1)S(1)} %convert_element_type.47), channel_id=1, source_target_pairs={{0,1},{1,0},{2,3},{3,2},{4,5},{5,4},{6,7},{7,6},{8,9},{9,8},{10,11... | collective-permute-start | bytes 804872 | tf_op jit(solution)/shard_map/ppermute | solution.py:362
  114.6 1.0 shard_map.110
  115.7 0.1 collective-permute-done.8
  115.8 0.1 shard_map.111
  116.0 14.5 %all_to_all.34 = f16[8,136,128]{2,1,0:T(8,128)(2,1)S(1)} all-to-all(f16[8,136,128]{2,1,0:T(8,128)(2,1)S(1)} %convert_element_type.49), channel_id=1, replica_groups=mesh['y'=4,'x'=4,'z'=8,'core'=2] {'z'}, dimensions={0} | all-to-all | bytes 557056 | tf_op jit(solution)/shard_map/all_to_all | solution.py:337
  130.6 0.7 shard_map.112
  (30 shorter events, 0.5 us)
Async XLA Ops:
  2.3 19.4 %all-to-all-start = ((bf16[8,128,128]{2,1,0:T(8,128)(2,1)}), bf16[8,128,128]{2,1,0:T(8,128)(2,1)S(1)}, u32[]{:S(2)}, u32[]{:S(2)}) async-start(bf16[8,128,128]{2,1,0:T(8,128)(2,1)} %shard_map.95), calls=%async_computation | async-start | bytes 524288 | tf_op jit(solution)/shard_map/all_to_all | solution.py:337
  11.9 12.3 %copy-start.4 = (f32[32]{0:T(128)S(1)}, f32[32]{0:T(128)}, u32[]{:S(2)}) copy-start(f32[32]{0:T(128)} %param.14) | copy-start | bytes 388
  12.0 12.3 %copy-start.5 = (s32[128]{0:T(128)S(1)}, s32[128]{0:T(128)}, u32[]{:S(2)}) copy-start(s32[128]{0:T(128)} %param.13) | copy-start | bytes 1540
  12.0 12.4 %copy-start = (f32[128,128]{1,0:T(8,128)S(1)}, f32[128,128]{1,0:T(8,128)}, u32[]{:S(2)}) copy-start(f32[128,128]{1,0:T(8,128)} %right_ref.7) | copy-start | bytes 196612
  12.0 12.5 %copy-start.2 = (s32[16]{0:T(128)S(1)}, s32[16]{0:T(128)}, u32[]{:S(2)}) copy-start(s32[16]{0:T(128)} %param.10) | copy-start | bytes 196
  12.0 12.5 %copy-start.3 = (s32[16]{0:T(128)S(1)}, s32[16]{0:T(128)}, u32[]{:S(2)}) copy-start(s32[16]{0:T(128)} %param.9) | copy-start | bytes 196
  21.7 3.8 %collective-permute-start = (bf16[8,128,128]{2,1,0:T(8,128)(2,1)S(1)}, bf16[8,128,128]{2,1,0:T(8,128)(2,1)S(1)}, u32[]{:S(2)}, u32[]{:S(2)}) collective-permute-start(bf16[8,128,128]{2,1,0:T(8,128)(2,1)S(1)} %broadcast_multiply_fusion.own.gathered), channel_id=1, source_target_pairs={{0,1},{1,0},{2,3},{3,2},{4,5},{5,4},{6,7},{7,6},{8,9},{9,8},{10,11... | collective-permute-start | bytes 786440 | tf_op jit(solution)/shard_map/ppermute | solution.py:362
  25.5 15.9 %copy-start.1 = (f32[1024]{0:T(1024)S(1)}, f32[1024]{0:T(1024)}, u32[]{:S(2)}) copy-start(f32[1024]{0:T(1024)} %param.12) | copy-start | bytes 12292
  53.3 3.9 %collective-permute-start.1 = (f16[1048,128]{1,0:T(8,128)(2,1)S(1)}, f16[1048,128]{1,0:T(8,128)(2,1)S(1)}, u32[]{:S(2)}, u32[]{:S(2)}) collective-permute-start(f16[1048,128]{1,0:T(8,128)(2,1)S(1)} %convert_element_type.39), channel_id=1, source_target_pairs={{0,1},{1,0},{2,3},{3,2},{4,5},{5,4},{6,7},{7,6},{8,9},{9,8},{10,11... | collective-permute-start | bytes 804872 | tf_op jit(solution)/shard_map/ppermute | solution.py:362
  57.4 4.9 %collective-permute-start.2 = (f16[528,128]{1,0:T(8,128)(2,1)S(1)}, f16[528,128]{1,0:T(8,128)(2,1)S(1)}, u32[]{:S(2)}, u32[]{:S(2)}) collective-permute-start(f16[528,128]{1,0:T(8,128)(2,1)S(1)} %convert_element_type.41), channel_id=1, source_target_pairs={{0,2},{1,3},{2,0},{3,1},{4,6},{5,7},{6,4},{7,5},{8,10},{9,11},{10,... | collective-permute-start | bytes 405512 | tf_op jit(solution)/shard_map/ppermute | solution.py:346
  62.5 4.9 %collective-permute-start.3 = (f16[272,128]{1,0:T(8,128)(2,1)S(1)}, f16[272,128]{1,0:T(8,128)(2,1)S(1)}, u32[]{:S(2)}, u32[]{:S(2)}) collective-permute-start(f16[272,128]{1,0:T(8,128)(2,1)S(1)} %convert_element_type.43), channel_id=1, source_target_pairs={{0,4},{1,5},{2,6},{3,7},{4,0},{5,1},{6,2},{7,3},{8,12},{9,13},{10,... | collective-permute-start | bytes 208904 | tf_op jit(solution)/shard_map/ppermute | solution.py:346
  67.5 5.2 %collective-permute-start.4 = (f16[272,128]{1,0:T(8,128)(2,1)S(1)}, f16[272,128]{1,0:T(8,128)(2,1)S(1)}, u32[]{:S(2)}, u32[]{:S(2)}) collective-permute-start(f16[272,128]{1,0:T(8,128)(2,1)S(1)} %convert_element_type.45), channel_id=1, source_target_pairs={{0,14},{1,15},{2,12},{3,13},{4,10},{5,11},{6,8},{7,9},{8,6},{9,7},... | collective-permute-start | bytes 208904 | tf_op jit(solution)/shard_map/ppermute | solution.py:346
  72.7 4.8 %collective-permute-start.5 = (bf16[2,128,128]{2,1,0:T(8,128)(2,1)S(1)}, bf16[2,128,128]{2,1,0:T(8,128)(2,1)S(1)}, u32[]{:S(2)}, u32[]{:S(2)}) collective-permute-start(bf16[2,128,128]{2,1,0:T(8,128)(2,1)S(1)} %get-tuple-element.31), channel_id=1, source_target_pairs={{0,4},{1,5},{2,6},{3,7},{4,0},{5,1},{6,2},{7,3},{8,12},{9,13},{10,... | collective-permute-start | bytes 196616 | tf_op jit(solution)/shard_map/ppermute | solution.py:346
  77.6 4.6 %collective-permute-start.6 = (bf16[4,128,128]{2,1,0:T(8,128)(2,1)S(1)}, bf16[4,128,128]{2,1,0:T(8,128)(2,1)S(1)}, u32[]{:S(2)}, u32[]{:S(2)}) collective-permute-start(bf16[4,128,128]{2,1,0:T(8,128)(2,1)S(1)} %pad_maximum_fusion), channel_id=1, source_target_pairs={{0,2},{1,3},{2,0},{3,1},{4,6},{5,7},{6,4},{7,5},{8,10},{9,11},{10,... | collective-permute-start | bytes 393224 | tf_op jit(solution)/shard_map/ppermute | solution.py:346
  82.2 5.9 %collective-permute-start.7 = (bf16[8,128,128]{2,1,0:T(8,128)(2,1)S(1)}, bf16[8,128,128]{2,1,0:T(8,128)(2,1)S(1)}, u32[]{:S(2)}, u32[]{:S(2)}) collective-permute-start(bf16[8,128,128]{2,1,0:T(8,128)(2,1)S(1)} %constant_dynamic-update-slice_fusion.own), channel_id=1, source_target_pairs={{0,1},{1,0},{2,3},{3,2},{4,5},{5,4},{6,7},{7,6},{8,9},{9,8},{10,11... | collective-permute-start | bytes 786440 | tf_op jit(solution)/shard_map/ppermute | solution.py:362
  111.7 4.1 %collective-permute-start.8 = (f16[1048,128]{1,0:T(8,128)(2,1)S(1)}, f16[1048,128]{1,0:T(8,128)(2,1)S(1)}, u32[]{:S(2)}, u32[]{:S(2)}) collective-permute-start(f16[1048,128]{1,0:T(8,128)(2,1)S(1)} %convert_element_type.47), channel_id=1, source_target_pairs={{0,1},{1,0},{2,3},{3,2},{4,5},{5,4},{6,7},{7,6},{8,9},{9,8},{10,11... | collective-permute-start | bytes 804872 | tf_op jit(solution)/shard_map/ppermute | solution.py:362

commit v5 on v4

--- a/solution.py
+++ b/solution.py
@@ -23,7 +23,7 @@
 VMEM_WHOLE = 60 * 1024 * 1024
 
 
-def call(kernel, out_shape, operands, smem=0, scratch=()):
+def call(kernel, out_shape, operands, smem=0, scratch=(), flops=None):
     spaces = [pltpu.SMEM] * smem + [pltpu.VMEM] * (len(operands) - smem)
     return pl.pallas_call(
         kernel,
@@ -31,6 +31,7 @@
         in_specs=[pl.BlockSpec(memory_space=space) for space in spaces],
         out_specs=jax.tree.map(lambda _: pl.BlockSpec(memory_space=pltpu.VMEM), out_shape),
         scratch_shapes=list(scratch),
+        cost_estimate=flops and pl.CostEstimate(flops=flops, bytes_accessed=0, transcendentals=0),
         compiler_params=pltpu.CompilerParams(vmem_limit_bytes=VMEM_LIMIT),
     )(*operands)
 
@@ -164,18 +165,22 @@
         out[part, chunk:] = extra
 
 
-def backward(half, slots, got, tiles, source, total):
+def backward(half, slots, got, tiles, source, total, part):
     tile = tiles.shape[1]
     parts, chunk = got.shape[0], got.shape[1] - PARTS
     cells = tile // CORES
     sums = got[0, chunk:].astype(jnp.float32)
-    for part in range(1, parts):
-        sums = sums + got[part, chunk:].astype(jnp.float32)
-    for part in range(parts):
-        source[part * chunk : (part + 1) * chunk] = got[part, :chunk]
+    for piece in range(1, parts):
+        sums = sums + got[piece, chunk:].astype(jnp.float32)
+    for piece in range(parts):
+        source[piece * chunk : (piece + 1) * chunk] = got[piece, :chunk]
     total[...] = jnp.zeros_like(total)
+
     for slot in range(tiles.shape[0]):
-        total[rows_at(col_of(slots, slot) * cells, cells), :] += lax.dot_general(
+        block = col_of(slots, slot)
+        if part is not None:
+            block = jnp.where(block // FOUR == part, lax.rem(block, FOUR), FOUR)
+        total[rows_at(block * cells, cells), :] += lax.dot_general(
             tiles[slot, :, rows_at(half * cells, cells)],
             source[rows_at(row_of(slots, slot) * tile, tile), :],
             (((0,), (0,)), ((), ())),
@@ -184,11 +189,13 @@
     return join(sums)
 
 
-def backward_send_kernel(core, slots, got, tiles, coded, source, total):
-    sums = backward(1 - core[0], slots, got, tiles, source, total)
+def backward_send_kernel(part, core, slots, got, tiles, *refs):
+    coded, source, total = refs[-3:]
+    sums = backward(1 - core[0], slots, got, tiles, source, total, part)
     cells = tiles.shape[1] // CORES
     powers = []
-    for block in range(total.shape[0] // cells):
+    blocks = COLS if part is None else FOUR
+    for block in range(blocks):
         rows = slice(block * cells, (block + 1) * cells)
         power = exponent(jnp.max(jnp.abs(total[rows]), axis=0, keepdims=True))
         coded[rows] = total[rows] * jnp.exp2(TOP - power)
@@ -196,11 +203,14 @@
     sum_power = exponent(jnp.abs(sums))
     terms = split(sums * jnp.exp2(TOP - sum_power))
     tail = padded(jnp.concatenate([terms, sum_power], axis=0))
-    coded[total.shape[0] :] = jnp.concatenate([tail] + powers, axis=0)
-
-
-def backward_keep_kernel(core, slots, got, tiles, after, keep, sums_out, source):
-    sums = backward(core[0], slots, got, tiles, source, keep)
+    powers += [jnp.zeros_like(powers[0])] * (COLS - len(powers))
+    if part != 0:
+        powers = [tail] + powers
+    coded[blocks * cells :] = jnp.concatenate(powers, axis=0)
+
+
+def backward_keep_kernel(part, core, slots, got, tiles, after, keep, sums_out, source):
+    sums = backward(core[0], slots, got, tiles, source, keep, part)
     sums_out[...] = rows_of(*[sums[kind : kind + 1] for kind in range(KINDS)])
 
 
@@ -222,9 +232,8 @@
         out[block, cells:] = jnp.concatenate([high, sums - high, sum_power, power], axis=0)
 
 
-def pair_sum(keep, kept_sums, coded, block):
+def pair_sum(keep, kept_sums, coded, block, blocks):
     cells = CELLS
-    blocks = keep.shape[0] // cells
     tail = coded[blocks * cells :]
     at = TERMS * KINDS
     sums = kept_sums[:KINDS] + join(tail[:at]) * jnp.exp2(tail[at : at + KINDS] - TOP)
@@ -260,29 +269,18 @@
     return blocks, kept_sums[:KINDS] + join(tail[:at]) * jnp.exp2(tail[at : at + KINDS] - TOP)
 
 
-def spread_kernel(height, keep, keep_sums, swapped, kept, coded, kept_sums, total):
+def spread_kernel(keep, keep_sums, swapped, coded, kept_sums):
+    blocks = [pair_sum(keep, keep_sums, swapped, block, FOUR) for block in range(FOUR)]
+    emit([], [total for total, _ in blocks], blocks[0][1], None, coded, kept_sums)
+
+
+def halve_kernel(keep, keep_sums, swapped, coded_in, sums_in, kept, coded, kept_sums, total):
     cells = CELLS
-    for block in range(COLS):
-        part, sums = pair_sum(keep, keep_sums, swapped, block)
-        total[block * cells : (block + 1) * cells] = part
-    half, own = height[0] // FOUR, lax.rem(height[0], FOUR)
-
-    def blocks(chips):
-        at = [z for chip in chips for z in (half * FOUR + chip, (2 - half) * FOUR - 1 - chip)]
-        return [total[rows_at(z * cells, cells), :] for z in at]
-
-    emit(
-        blocks([own, jnp.bitwise_xor(own, 2)]),
-        blocks([jnp.bitwise_xor(own, 1), jnp.bitwise_xor(own, 3)]),
-        sums,
-        kept,
-        coded,
-        kept_sums,
-    )
-
-
-def halve_kernel(kept_in, coded_in, sums_in, kept, coded, kept_sums):
-    blocks, sums = absorb(kept_in, coded_in, sums_in, range(4))
+    for block in range(FOUR):
+        rows = slice(block * cells, (block + 1) * cells)
+        power = swapped[FOUR * cells + block : FOUR * cells + block + 1]
+        total[rows] = keep[rows] + swapped[rows] * jnp.exp2(power - TOP)
+    blocks, sums = absorb(total, coded_in, sums_in, range(FOUR))
     emit(blocks[:2], blocks[2:], sums, kept, coded, kept_sums)
 
 
@@ -403,7 +401,7 @@
     sums = call(start_kernel, f32(SUMS, probes), (right_side, reg))
     weights = data_weight.reshape(-1, chunk * PACK)
 
-    def products(own, sums, places):
+    def weighted_data(own, sums, places):
         total = call(
             forward_own_kernel, f32(group_rows, probes), (core, places, own, tiles), smem=2
         )
@@ -420,56 +418,61 @@
             (dp, exchange(partial, DP), weights, sums),
             smem=1,
         )
-        operands = (core, slots, exchange(weighted, DP), tiles)
+        return exchange(weighted, DP)
+
+    def transposed(gathered, places, part=None, after=()):
+        operands = (core, places, gathered, tiles)
         source = pltpu.VMEM((group_rows, probes), jnp.bfloat16)
-        rows = n_z * cells
+        blocks = n_z if part is None else FOUR
+        rows = blocks * cells
+        room = rows if part is None else rows + cells
+        flops = 2 * tiles.shape[0] * tile * cells * probes
         coded = call(
-            backward_send_kernel,
-            f32(rows + PARTS + n_z, probes),
-            operands,
+            functools.partial(backward_send_kernel, part),
+            f32(rows + (COLS if part == 0 else PARTS + COLS), probes),
+            (*operands, *after),
             smem=2,
-            scratch=[source, pltpu.VMEM((rows, probes), jnp.float32)],
+            flops=flops,
+            scratch=[source, pltpu.VMEM((room, probes), jnp.float32)],
         )
         keep, kept_sums = call(
-            backward_keep_kernel,
-            [f32(rows, probes), f32(SUMS, probes)],
+            functools.partial(backward_keep_kernel, part),
+            [f32(room, probes), f32(SUMS, probes)],
             (*operands, coded),
             smem=2,
+            flops=flops,
             scratch=[source],
         )
         return keep, kept_sums, swap(coded.astype(jnp.float16)).astype(jnp.float32)
 
-    def halved(kernel, blocks, operands, to, smem=0, scratch=()):
-        kept, coded, sums = call(
-            kernel,
-            (f32(blocks * cells, probes), f32(blocks * cells + PARTS, probes), f32(SUMS, probes)),
-            operands,
-            smem=smem,
-            scratch=scratch,
-        )
-        return kept, along_z(coded.astype(jnp.float16), to).astype(jnp.float32), sums
+    def sent(coded, to):
+        return along_z(coded.astype(jnp.float16), to).astype(jnp.float32)
 
     whole, extra = f32(cells, probes), f32(SUMS, probes)
-    terms = products(own, sums, slots)
-    terms = halved(
-        spread_kernel,
-        4,
-        (height, *terms),
-        near,
-        smem=1,
-        scratch=[pltpu.VMEM((n_z * cells, probes), jnp.float32)],
-    )
-    terms = halved(halve_kernel, 2, terms, far)
-    terms = halved(cross_kernel, 2, (*terms, right_side, reg), mirror)
+    pair, pair_coded = f32(2 * cells, probes), f32(2 * cells + PARTS, probes)
+    four_coded = f32(FOUR * cells + PARTS, probes)
+    gathered = weighted_data(own, sums, slots)
+    coded, sums = call(spread_kernel, (four_coded, extra), transposed(gathered, last_slots, 1))
+    stays = transposed(gathered, last_slots, 0, after=(coded,))
+    kept, coded, sums = call(
+        halve_kernel,
+        (pair, pair_coded, extra),
+        (*stays, sent(coded, near), sums),
+        scratch=[pltpu.VMEM((FOUR * cells, probes), jnp.float32)],
+    )
+    kept, coded, sums = call(
+        cross_kernel, (pair, pair_coded, extra), (kept, sent(coded, far), sums, right_side, reg)
+    )
     residual, image, low, sums, keep = call(
         first_update_kernel,
         (whole, whole, bf16(2, cells, probes), extra, extra),
-        (height, *terms, own, right_side, reg),
+        (height, kept, sent(coded, mirror), sums, own, right_side, reg),
         smem=1,
     )
     low = jnp.concatenate([low, along_z(low, far)], axis=0)
     low = jnp.concatenate([low, along_z(low, near)], axis=0)
-    terms = call(pair_kernel, f32(n_z, cells + SUMS, probes), products(low, sums, last_slots))
+    terms = transposed(weighted_data(low, sums, last_slots), slots)
+    terms = call(pair_kernel, f32(n_z, cells + SUMS, probes), terms)
     got = exchange(terms.astype(jnp.float16), "z").astype(jnp.float32)
     return call(
         last_update_kernel,

time: 132 us -> 133 us (level)
  waiting for transfers between devices: 29.2 us -> 26.2 us
  Pallas kernels: 11.4 us -> 14.1 us
    ppermute x5, waiting for transfers between devices: 22.8 us -> 19.9 us  [along_z(): return lax.ppermute(value, ('z', 'core'), pairs)]
    pallas_call x17 -> x19, Pallas kernels: 9.76 us -> 12.4 us  [call(): pl.pallas_call(kernel, out_shape=out_shape, in_specs=[pl.BlockSpec(memory...]
    ppermute x4 -> x5, starting transfers between devices: 12.9 us -> 13.5 us  [swap(): return lax.ppermute(value, 'core', [(0, 1), (1, 0)])]
  transfers between devices with their start and end apart: 10 -> 11, of which waited for: 9 -> 8; matrix products, arithmetic and copies ran while one was open for 2% -> 2% of each run, Pallas kernels for 3% -> 5%
where the time goes in v5:
time: 133 us; the launch traced here: 132 us
  blocking collectives  61.9 us (47%)
  waiting for transfers between devices  26.2 us (20%)
  starting transfers between devices  24 us (18%)
  Pallas kernels  14.1 us (11%)
  between operations  2.95 us (2%)
  other arithmetic  2.3 us (2%)
    all_to_all x5, blocking collectives, exchange(): return lax.all_to_all(value, axis, 0, 0)  61.9 us
    ppermute x5, waiting for transfers between devices, along_z(): return lax.ppermute(value, ('z', 'core'), pairs)  19.9 us
    ppermute x5, starting transfers between devices, swap(): return lax.ppermute(value, 'core', [(0, 1), (1, 0)])  13.5 us
    pallas_call x19, Pallas kernels, call(): pl.pallas_call(kernel, out_shape=out_shape, in_specs=[pl.BlockSpec(memory...  12.4 us
    all_to_all x1, starting transfers between devices, exchange(): return lax.all_to_all(value, axis, 0, 0)  9.03 us
    all_to_all x1, waiting for transfers between devices, exchange(): return lax.all_to_all(value, axis, 0, 0)  5.99 us
  transfers between devices with their start and end apart: 11, of which 8 were waited for; matrix products, arithmetic and copies ran while one was open for 2% of the time, Pallas kernels for 5%

profile of v5, /device:TPU:1, one launch (start us, length us, event | category | flops | bytes accessed | tf_op | source)
XLA Modules:
  0.0 132.1 jit_solution(13999478660599372116)
XLA Ops:
  0.6 1.6 %shard_map.95 = bf16[8,128,128]{2,1,0:T(8,128)(2,1)} custom-call(f32[128,128]{1,0:T(8,128)} %right_ref.7), custom_call_target="tpu_custom_call" | custom-call | tf_op jit(solution)/shard_map/pallas_call | solution.py:387
  2.3 9.0 %all-to-all-start = ((bf16[8,128,128]{2,1,0:T(8,128)(2,1)}), bf16[8,128,128]{2,1,0:T(8,128)(2,1)S(1)}, u32[]{:S(2)}, u32[]{:S(2)}) async-start(bf16[8,128,128]{2,1,0:T(8,128)(2,1)} %shard_map.95), calls=%async_computation | async-start | bytes 524288 | tf_op jit(solution)/shard_map/all_to_all | solution.py:335
  12.0 0.0 copy-start.5
  12.0 1.8 %broadcast_select_fusion.tiles = bf16[16,256,256]{2,1,0:T(8,128)(2,1)S(1)} fusion(bf16[16,256,256]{2,1,0:T(8,128)(2,1)} %param.8, pred[16]{0:T(512)(128)(4,1)S(1)} %iota_compare_fusion.1), kind=kLoop, calls=%fused_computation | loop fusion | flops 1048576 | bytes 4194320 | tf_op jit(solution)/shard_map/jit(_where)/select_n | solution.py:389
  13.8 0.5 slice.5
  15.7 6.0 %all-to-all-done = bf16[8,128,128]{2,1,0:T(8,128)(2,1)S(1)} async-done(((bf16[8,128,128]{2,1,0:T(8,128)(2,1)}), bf16[8,128,128]{2,1,0:T(8,128)(2,1)S(1)}, u32[]{:S(2)}, u32[]{:S(2)}) %all-to-all-start) | async-done | bytes 262176 | tf_op jit(solution)/shard_map/all_to_all | solution.py:335
  21.7 2.5 %collective-permute-start = (bf16[8,128,128]{2,1,0:T(8,128)(2,1)S(1)}, bf16[8,128,128]{2,1,0:T(8,128)(2,1)S(1)}, u32[]{:S(2)}, u32[]{:S(2)}) collective-permute-start(bf16[8,128,128]{2,1,0:T(8,128)(2,1)S(1)} %broadcast_multiply_fusion.own.gathered), channel_id=1, source_target_pairs={{0,1},{1,0},{2,3},{3,2},{4,5},{5,4},{6,7},{7,6},{8,9},{9,8},{10,11... | collective-permute-start | bytes 786440 | tf_op jit(solution)/shard_map/ppermute | solution.py:360
  24.2 0.1 select_reduce_fusion
  24.3 0.1 broadcast_in_dim.31.reg_ref
  24.5 1.0 shard_map.96.own_total
  25.5 1.0 shard_map.98
  26.6 14.8 %all_to_all.30.got = bf16[16,64,128]{2,1,0:T(8,128)(2,1)S(1)} all-to-all(bf16[16,64,128]{2,1,0:T(8,128)(2,1)S(1)} %shard_map.98), channel_id=1, replica_groups=mesh['y'=4,'x'=4,'z'=8,'core'=2] {'y','x'}, dimensions={0} | all-to-all | bytes 524288 | tf_op jit(solution)/shard_map/all_to_all | solution.py:335
  41.4 0.1 shard_map.99
  41.5 10.7 %all_to_all.31.got = bf16[16,80,128]{2,1,0:T(8,128)(2,1)S(1)} all-to-all(bf16[16,80,128]{2,1,0:T(8,128)(2,1)S(1)} %shard_map.99), channel_id=1, replica_groups=mesh['y'=4,'x'=4,'z'=8,'core'=2] {'y','x'}, dimensions={0} | all-to-all | bytes 655360 | tf_op jit(solution)/shard_map/all_to_all | solution.py:335
  52.2 1.3 shard_map.100.after
  53.5 2.7 %collective-permute-start.1 = (f16[536,128]{1,0:T(8,128)(2,1)S(1)}, f16[536,128]{1,0:T(8,128)(2,1)S(1)}, u32[]{:S(2)}, u32[]{:S(2)}) collective-permute-start(f16[536,128]{1,0:T(8,128)(2,1)S(1)} %convert_element_type.45), channel_id=1, source_target_pairs={{0,1},{1,0},{2,3},{3,2},{4,5},{5,4},{6,7},{7,6},{8,9},{9,8},{10,11... | collective-permute-start | bytes 411656 | tf_op jit(solution)/shard_map/ppermute | solution.py:360
  56.2 1.2 shard_map.101
  57.4 0.1 shard_map.102
  57.5 0.4 collective-permute-start.3
  57.9 1.2 shard_map.103.after
  59.2 0.5 collective-permute-start.2
  59.7 1.2 shard_map.104
  60.9 1.7 %collective-permute-done.3 = f16[528,128]{1,0:T(8,128)(2,1)S(1)} collective-permute-done((f16[528,128]{1,0:T(8,128)(2,1)S(1)}, f16[528,128]{1,0:T(8,128)(2,1)S(1)}, u32[]{:S(2)}, u32[]{:S(2)}) %collective-permute-start.3) | collective-permute-done | bytes 135200 | tf_op jit(solution)/shard_map/ppermute | solution.py:344
  62.7 0.1 shard_map.105
  62.8 0.1 collective-permute-start.4
  62.9 4.8 %collective-permute-done.4 = f16[272,128]{1,0:T(8,128)(2,1)S(1)} collective-permute-done((f16[272,128]{1,0:T(8,128)(2,1)S(1)}, f16[272,128]{1,0:T(8,128)(2,1)S(1)}, u32[]{:S(2)}, u32[]{:S(2)}) %collective-permute-start.4) | collective-permute-done | bytes 69664 | tf_op jit(solution)/shard_map/ppermute | solution.py:344
  67.7 0.1 shard_map.106
  67.8 0.1 collective-permute-start.5
  67.9 5.1 %collective-permute-done.5 = f16[272,128]{1,0:T(8,128)(2,1)S(1)} collective-permute-done((f16[272,128]{1,0:T(8,128)(2,1)S(1)}, f16[272,128]{1,0:T(8,128)(2,1)S(1)}, u32[]{:S(2)}, u32[]{:S(2)}) %collective-permute-start.5) | collective-permute-done | bytes 69664 | tf_op jit(solution)/shard_map/ppermute | solution.py:344
  73.0 0.1 shard_map.107
  73.1 0.7 collective-permute-start.6
  73.8 4.1 %collective-permute-done.6 = bf16[2,128,128]{2,1,0:T(8,128)(2,1)S(1)} collective-permute-done((bf16[2,128,128]{2,1,0:T(8,128)(2,1)S(1)}, bf16[2,128,128]{2,1,0:T(8,128)(2,1)S(1)}, u32[]{:S(2)}, u32[]{:S(2)}) %collective-permute-start.6) | collective-permute-done | bytes 65568 | tf_op jit(solution)/shard_map/ppermute | solution.py:344
  77.9 0.3 collective-permute-start.7
  78.2 4.2 %collective-permute-done.7 = bf16[4,128,128]{2,1,0:T(8,128)(2,1)S(1)} collective-permute-done((bf16[4,128,128]{2,1,0:T(8,128)(2,1)S(1)}, bf16[4,128,128]{2,1,0:T(8,128)(2,1)S(1)}, u32[]{:S(2)}, u32[]{:S(2)}) %collective-permute-start.7) | collective-permute-done | bytes 131104 | tf_op jit(solution)/shard_map/ppermute | solution.py:344
  82.4 4.7 %collective-permute-start.8 = (bf16[8,128,128]{2,1,0:T(8,128)(2,1)S(1)}, bf16[8,128,128]{2,1,0:T(8,128)(2,1)S(1)}, u32[]{:S(2)}, u32[]{:S(2)}) collective-permute-start(bf16[8,128,128]{2,1,0:T(8,128)(2,1)S(1)} %constant_dynamic-update-slice_fusion.own), channel_id=1, source_target_pairs={{0,1},{1,0},{2,3},{3,2},{4,5},{5,4},{6,7},{7,6},{8,9},{9,8},{10,11... | collective-permute-start | bytes 786440 | tf_op jit(solution)/shard_map/ppermute | solution.py:360
  87.1 1.0 shard_map.108.own_total
  88.1 0.2 collective-permute-done.8.other
  88.3 1.0 shard_map.109
  89.3 10.7 %all_to_all.32.got = bf16[16,64,128]{2,1,0:T(8,128)(2,1)S(1)} all-to-all(bf16[16,64,128]{2,1,0:T(8,128)(2,1)S(1)} %shard_map.109), channel_id=1, replica_groups=mesh['y'=4,'x'=4,'z'=8,'core'=2] {'y','x'}, dimensions={0} | all-to-all | bytes 524288 | tf_op jit(solution)/shard_map/all_to_all | solution.py:335
  100.1 0.1 shard_map.110
  100.2 10.6 %all_to_all.33.got = bf16[16,80,128]{2,1,0:T(8,128)(2,1)S(1)} all-to-all(bf16[16,80,128]{2,1,0:T(8,128)(2,1)S(1)} %shard_map.110), channel_id=1, replica_groups=mesh['y'=4,'x'=4,'z'=8,'core'=2] {'y','x'}, dimensions={0} | all-to-all | bytes 655360 | tf_op jit(solution)/shard_map/all_to_all | solution.py:335
  110.8 1.1 shard_map.111.after
  112.0 2.9 %collective-permute-start.9 = (f16[1048,128]{1,0:T(8,128)(2,1)S(1)}, f16[1048,128]{1,0:T(8,128)(2,1)S(1)}, u32[]{:S(2)}, u32[]{:S(2)}) collective-permute-start(f16[1048,128]{1,0:T(8,128)(2,1)S(1)} %convert_element_type.55), channel_id=1, source_target_pairs={{0,1},{1,0},{2,3},{3,2},{4,5},{5,4},{6,7},{7,6},{8,9},{9,8},{10,11... | collective-permute-start | bytes 804872 | tf_op jit(solution)/shard_map/ppermute | solution.py:360
  114.9 1.0 shard_map.112
  115.9 0.1 collective-permute-done.9
  116.1 0.1 shard_map.113
  116.3 15.0 %all_to_all.34 = f16[8,136,128]{2,1,0:T(8,128)(2,1)S(1)} all-to-all(f16[8,136,128]{2,1,0:T(8,128)(2,1)S(1)} %convert_element_type.57), channel_id=1, replica_groups=mesh['y'=4,'x'=4,'z'=8,'core'=2] {'z'}, dimensions={0} | all-to-all | bytes 557056 | tf_op jit(solution)/shard_map/all_to_all | solution.py:335
  131.4 0.7 shard_map.114
  (36 shorter events, 0.5 us)
Async XLA Ops:
  2.3 19.4 %all-to-all-start = ((bf16[8,128,128]{2,1,0:T(8,128)(2,1)}), bf16[8,128,128]{2,1,0:T(8,128)(2,1)S(1)}, u32[]{:S(2)}, u32[]{:S(2)}) async-start(bf16[8,128,128]{2,1,0:T(8,128)(2,1)} %shard_map.95), calls=%async_computation | async-start | bytes 524288 | tf_op jit(solution)/shard_map/all_to_all | solution.py:335
  11.9 12.3 %copy-start.4 = (f32[32]{0:T(128)S(1)}, f32[32]{0:T(128)}, u32[]{:S(2)}) copy-start(f32[32]{0:T(128)} %param.14) | copy-start | bytes 388
  12.0 12.3 %copy-start.5 = (s32[128]{0:T(128)S(1)}, s32[128]{0:T(128)}, u32[]{:S(2)}) copy-start(s32[128]{0:T(128)} %param.13) | copy-start | bytes 1540
  12.0 12.4 %copy-start = (f32[128,128]{1,0:T(8,128)S(1)}, f32[128,128]{1,0:T(8,128)}, u32[]{:S(2)}) copy-start(f32[128,128]{1,0:T(8,128)} %right_ref.7) | copy-start | bytes 196612
  12.0 12.5 %copy-start.2 = (s32[16]{0:T(128)S(1)}, s32[16]{0:T(128)}, u32[]{:S(2)}) copy-start(s32[16]{0:T(128)} %param.10) | copy-start | bytes 196
  12.0 12.5 %copy-start.3 = (s32[16]{0:T(128)S(1)}, s32[16]{0:T(128)}, u32[]{:S(2)}) copy-start(s32[16]{0:T(128)} %param.9) | copy-start | bytes 196
  21.7 3.8 %collective-permute-start = (bf16[8,128,128]{2,1,0:T(8,128)(2,1)S(1)}, bf16[8,128,128]{2,1,0:T(8,128)(2,1)S(1)}, u32[]{:S(2)}, u32[]{:S(2)}) collective-permute-start(bf16[8,128,128]{2,1,0:T(8,128)(2,1)S(1)} %broadcast_multiply_fusion.own.gathered), channel_id=1, source_target_pairs={{0,1},{1,0},{2,3},{3,2},{4,5},{5,4},{6,7},{7,6},{8,9},{9,8},{10,11... | collective-permute-start | bytes 786440 | tf_op jit(solution)/shard_map/ppermute | solution.py:360
  25.5 15.9 %copy-start.1 = (f32[1024]{0:T(1024)S(1)}, f32[1024]{0:T(1024)}, u32[]{:S(2)}) copy-start(f32[1024]{0:T(1024)} %param.12) | copy-start | bytes 12292
  53.5 3.9 %collective-permute-start.1 = (f16[536,128]{1,0:T(8,128)(2,1)S(1)}, f16[536,128]{1,0:T(8,128)(2,1)S(1)}, u32[]{:S(2)}, u32[]{:S(2)}) collective-permute-start(f16[536,128]{1,0:T(8,128)(2,1)S(1)} %convert_element_type.45), channel_id=1, source_target_pairs={{0,1},{1,0},{2,3},{3,2},{4,5},{5,4},{6,7},{7,6},{8,9},{9,8},{10,11... | collective-permute-start | bytes 411656 | tf_op jit(solution)/shard_map/ppermute | solution.py:360
  57.5 5.1 %collective-permute-start.3 = (f16[528,128]{1,0:T(8,128)(2,1)S(1)}, f16[528,128]{1,0:T(8,128)(2,1)S(1)}, u32[]{:S(2)}, u32[]{:S(2)}) collective-permute-start(f16[528,128]{1,0:T(8,128)(2,1)S(1)} %convert_element_type.49), channel_id=1, source_target_pairs={{0,2},{1,3},{2,0},{3,1},{4,6},{5,7},{6,4},{7,5},{8,10},{9,11},{10,... | collective-permute-start | bytes 405512 | tf_op jit(solution)/shard_map/ppermute | solution.py:344
  59.2 1.7 %collective-permute-start.2 = (f16[520,128]{1,0:T(8,128)(2,1)S(1)}, f16[520,128]{1,0:T(8,128)(2,1)S(1)}, u32[]{:S(2)}, u32[]{:S(2)}) collective-permute-start(f16[520,128]{1,0:T(8,128)(2,1)S(1)} %convert_element_type.47), channel_id=1, source_target_pairs={{0,1},{1,0},{2,3},{3,2},{4,5},{5,4},{6,7},{7,6},{8,9},{9,8},{10,11... | collective-permute-start | bytes 399368 | tf_op jit(solution)/shard_map/ppermute | solution.py:360
  62.8 4.9 %collective-permute-start.4 = (f16[272,128]{1,0:T(8,128)(2,1)S(1)}, f16[272,128]{1,0:T(8,128)(2,1)S(1)}, u32[]{:S(2)}, u32[]{:S(2)}) collective-permute-start(f16[272,128]{1,0:T(8,128)(2,1)S(1)} %convert_element_type.51), channel_id=1, source_target_pairs={{0,4},{1,5},{2,6},{3,7},{4,0},{5,1},{6,2},{7,3},{8,12},{9,13},{10,... | collective-permute-start | bytes 208904 | tf_op jit(solution)/shard_map/ppermute | solution.py:344
  67.8 5.2 %collective-permute-start.5 = (f16[272,128]{1,0:T(8,128)(2,1)S(1)}, f16[272,128]{1,0:T(8,128)(2,1)S(1)}, u32[]{:S(2)}, u32[]{:S(2)}) collective-permute-start(f16[272,128]{1,0:T(8,128)(2,1)S(1)} %convert_element_type.53), channel_id=1, source_target_pairs={{0,14},{1,15},{2,12},{3,13},{4,10},{5,11},{6,8},{7,9},{8,6},{9,7},... | collective-permute-start | bytes 208904 | tf_op jit(solution)/shard_map/ppermute | solution.py:344
  73.1 4.8 %collective-permute-start.6 = (bf16[2,128,128]{2,1,0:T(8,128)(2,1)S(1)}, bf16[2,128,128]{2,1,0:T(8,128)(2,1)S(1)}, u32[]{:S(2)}, u32[]{:S(2)}) collective-permute-start(bf16[2,128,128]{2,1,0:T(8,128)(2,1)S(1)} %get-tuple-element.33), channel_id=1, source_target_pairs={{0,4},{1,5},{2,6},{3,7},{4,0},{5,1},{6,2},{7,3},{8,12},{9,13},{10,... | collective-permute-start | bytes 196616 | tf_op jit(solution)/shard_map/ppermute | solution.py:344
  77.9 4.5 %collective-permute-start.7 = (bf16[4,128,128]{2,1,0:T(8,128)(2,1)S(1)}, bf16[4,128,128]{2,1,0:T(8,128)(2,1)S(1)}, u32[]{:S(2)}, u32[]{:S(2)}) collective-permute-start(bf16[4,128,128]{2,1,0:T(8,128)(2,1)S(1)} %pad_maximum_fusion), channel_id=1, source_target_pairs={{0,2},{1,3},{2,0},{3,1},{4,6},{5,7},{6,4},{7,5},{8,10},{9,11},{10,... | collective-permute-start | bytes 393224 | tf_op jit(solution)/shard_map/ppermute | solution.py:344
  82.4 5.9 %collective-permute-start.8 = (bf16[8,128,128]{2,1,0:T(8,128)(2,1)S(1)}, bf16[8,128,128]{2,1,0:T(8,128)(2,1)S(1)}, u32[]{:S(2)}, u32[]{:S(2)}) collective-permute-start(bf16[8,128,128]{2,1,0:T(8,128)(2,1)S(1)} %constant_dynamic-update-slice_fusion.own), channel_id=1, source_target_pairs={{0,1},{1,0},{2,3},{3,2},{4,5},{5,4},{6,7},{7,6},{8,9},{9,8},{10,11... | collective-permute-start | bytes 786440 | tf_op jit(solution)/shard_map/ppermute | solution.py:360
  112.0 4.1 %collective-permute-start.9 = (f16[1048,128]{1,0:T(8,128)(2,1)S(1)}, f16[1048,128]{1,0:T(8,128)(2,1)S(1)}, u32[]{:S(2)}, u32[]{:S(2)}) collective-permute-start(f16[1048,128]{1,0:T(8,128)(2,1)S(1)} %convert_element_type.55), channel_id=1, source_target_pairs={{0,1},{1,0},{2,3},{3,2},{4,5},{5,4},{6,7},{7,6},{8,9},{9,8},{10,11... | collective-permute-start | bytes 804872 | tf_op jit(solution)/shard_map/ppermute | solution.py:360

commit v6 on v4

--- a/solution.py
+++ b/solution.py
@@ -403,14 +403,14 @@
     sums = call(start_kernel, f32(SUMS, probes), (right_side, reg))
     weights = data_weight.reshape(-1, chunk * PACK)
 
-    def products(own, sums, places):
+    def products(own, other, sums, places):
         total = call(
             forward_own_kernel, f32(group_rows, probes), (core, places, own, tiles), smem=2
         )
         partial = call(
             forward_other_kernel,
             bf16(n_dp, chunk, probes),
-            (dp, core, places, swap(own), tiles, total, sums),
+            (dp, core, places, other, tiles, total, sums),
             smem=3,
             scratch=[pltpu.VMEM((group_rows, probes), jnp.float32)],
         )
@@ -450,7 +450,7 @@
         return kept, along_z(coded.astype(jnp.float16), to).astype(jnp.float32), sums
 
     whole, extra = f32(cells, probes), f32(SUMS, probes)
-    terms = products(own, sums, slots)
+    terms = products(own, swap(own), sums, slots)
     terms = halved(
         spread_kernel,
         4,
@@ -468,8 +468,10 @@
         smem=1,
     )
     low = jnp.concatenate([low, along_z(low, far)], axis=0)
-    low = jnp.concatenate([low, along_z(low, near)], axis=0)
-    terms = call(pair_kernel, f32(n_z, cells + SUMS, probes), products(low, sums, last_slots))
+    later = along_z(low, near)
+    other = jnp.concatenate([swap(low), swap(later)], axis=0)
+    low = jnp.concatenate([low, later], axis=0)
+    terms = call(pair_kernel, f32(n_z, cells + SUMS, probes), products(low, other, sums, last_slots))
     got = exchange(terms.astype(jnp.float16), "z").astype(jnp.float32)
     return call(
         last_update_kernel,

time: 132 us -> 132 us (level)
  waiting for transfers between devices: 29.2 us -> 24.8 us
  starting transfers between devices: 23.5 us -> 27.6 us
    ppermute x5, waiting for transfers between devices: 22.8 us -> 18.5 us  [along_z(): return lax.ppermute(value, ('z', 'core'), pairs)]
    ppermute x4 -> x5, starting transfers between devices: 12.9 us -> 17.1 us  [swap(): return lax.ppermute(value, 'core', [(0, 1), (1, 0)])]
  transfers between devices with their start and end apart: 10 -> 11, of which waited for: 9 -> 7; matrix products, arithmetic and copies ran while one was open for 2% -> 2% of each run, Pallas kernels for 3% -> 3%
where the time goes in v6:
time: 132 us; the launch traced here: 131 us
  blocking collectives  61.4 us (47%)
  starting transfers between devices  27.6 us (21%)
  waiting for transfers between devices  24.8 us (19%)
  Pallas kernels  11.4 us (9%)
  between operations  2.93 us (2%)
  other arithmetic  2.34 us (2%)
    all_to_all x5, blocking collectives, exchange(): return lax.all_to_all(value, axis, 0, 0)  61.4 us
    ppermute x5, waiting for transfers between devices, along_z(): return lax.ppermute(value, ('z', 'core'), pairs)  18.5 us
    ppermute x5, starting transfers between devices, swap(): return lax.ppermute(value, 'core', [(0, 1), (1, 0)])  17.1 us
    pallas_call x17, Pallas kernels, call(): pl.pallas_call(kernel, out_shape=out_shape, in_specs=[pl.BlockSpec(memory...  9.82 us
    all_to_all x1, starting transfers between devices, exchange(): return lax.all_to_all(value, axis, 0, 0)  9.03 us
    all_to_all x1, waiting for transfers between devices, exchange(): return lax.all_to_all(value, axis, 0, 0)  5.99 us
  transfers between devices with their start and end apart: 11, of which 7 were waited for; matrix products, arithmetic and copies ran while one was open for 2% of the time, Pallas kernels for 3%

profile of v6, /device:TPU:1, one launch (start us, length us, event | category | flops | bytes accessed | tf_op | source)
XLA Modules:
  0.0 131.2 jit_solution(17097391358560787634)
XLA Ops:
  0.6 1.6 %shard_map.95 = bf16[8,128,128]{2,1,0:T(8,128)(2,1)} custom-call(f32[128,128]{1,0:T(8,128)} %right_ref.7), custom_call_target="tpu_custom_call" | custom-call | tf_op jit(solution)/shard_map/pallas_call | solution.py:389
  2.3 9.0 %all-to-all-start = ((bf16[8,128,128]{2,1,0:T(8,128)(2,1)}), bf16[8,128,128]{2,1,0:T(8,128)(2,1)S(1)}, u32[]{:S(2)}, u32[]{:S(2)}) async-start(bf16[8,128,128]{2,1,0:T(8,128)(2,1)} %shard_map.95), calls=%async_computation | async-start | bytes 524288 | tf_op jit(solution)/shard_map/all_to_all | solution.py:337
  11.9 0.0 copy-start.4
  12.0 0.0 copy-start.5
  12.0 0.0 copy-start
  12.0 0.0 copy-start.3
  12.0 1.8 %broadcast_select_fusion.tiles = bf16[16,256,256]{2,1,0:T(8,128)(2,1)S(1)} fusion(bf16[16,256,256]{2,1,0:T(8,128)(2,1)} %param.8, pred[16]{0:T(512)(128)(4,1)S(1)} %iota_compare_fusion.1), kind=kLoop, calls=%fused_computation | loop fusion | flops 1048576 | bytes 4194320 | tf_op jit(solution)/shard_map/jit(_where)/select_n | solution.py:391
  13.8 0.5 slice.5
  15.7 6.0 %all-to-all-done = bf16[8,128,128]{2,1,0:T(8,128)(2,1)S(1)} async-done(((bf16[8,128,128]{2,1,0:T(8,128)(2,1)}), bf16[8,128,128]{2,1,0:T(8,128)(2,1)S(1)}, u32[]{:S(2)}, u32[]{:S(2)}) %all-to-all-start) | async-done | bytes 262176 | tf_op jit(solution)/shard_map/all_to_all | solution.py:337
  21.7 2.5 %collective-permute-start = (bf16[8,128,128]{2,1,0:T(8,128)(2,1)S(1)}, bf16[8,128,128]{2,1,0:T(8,128)(2,1)S(1)}, u32[]{:S(2)}, u32[]{:S(2)}) collective-permute-start(bf16[8,128,128]{2,1,0:T(8,128)(2,1)S(1)} %broadcast_multiply_fusion.own.gathered), channel_id=1, source_target_pairs={{0,1},{1,0},{2,3},{3,2},{4,5},{5,4},{6,7},{7,6},{8,9},{9,8},{10,11... | collective-permute-start | bytes 786440 | tf_op jit(solution)/shard_map/ppermute | solution.py:362
  24.2 0.1 select_reduce_fusion
  24.3 0.1 broadcast_in_dim.31.reg_ref
  24.5 1.0 shard_map.96.own_total
  25.5 1.0 shard_map.98
  26.6 14.8 %all_to_all.30.got = bf16[16,64,128]{2,1,0:T(8,128)(2,1)S(1)} all-to-all(bf16[16,64,128]{2,1,0:T(8,128)(2,1)S(1)} %shard_map.98), channel_id=1, replica_groups=mesh['y'=4,'x'=4,'z'=8,'core'=2] {'y','x'}, dimensions={0} | all-to-all | bytes 524288 | tf_op jit(solution)/shard_map/all_to_all | solution.py:337
  41.4 0.1 shard_map.99
  41.5 10.7 %all_to_all.31.got = bf16[16,80,128]{2,1,0:T(8,128)(2,1)S(1)} all-to-all(bf16[16,80,128]{2,1,0:T(8,128)(2,1)S(1)} %shard_map.99), channel_id=1, replica_groups=mesh['y'=4,'x'=4,'z'=8,'core'=2] {'y','x'}, dimensions={0} | all-to-all | bytes 655360 | tf_op jit(solution)/shard_map/all_to_all | solution.py:337
  52.2 1.1 shard_map.100.after
  53.4 2.7 %collective-permute-start.1 = (f16[1048,128]{1,0:T(8,128)(2,1)S(1)}, f16[1048,128]{1,0:T(8,128)(2,1)S(1)}, u32[]{:S(2)}, u32[]{:S(2)}) collective-permute-start(f16[1048,128]{1,0:T(8,128)(2,1)S(1)} %convert_element_type.39), channel_id=1, source_target_pairs={{0,1},{1,0},{2,3},{3,2},{4,5},{5,4},{6,7},{7,6},{8,9},{9,8},{10,11... | collective-permute-start | bytes 804872 | tf_op jit(solution)/shard_map/ppermute | solution.py:362
  56.1 1.0 shard_map.101
  57.1 0.1 collective-permute-done.1
  57.3 0.1 shard_map.102
  57.5 0.4 collective-permute-start.2
  57.8 4.5 %collective-permute-done.2 = f16[528,128]{1,0:T(8,128)(2,1)S(1)} collective-permute-done((f16[528,128]{1,0:T(8,128)(2,1)S(1)}, f16[528,128]{1,0:T(8,128)(2,1)S(1)}, u32[]{:S(2)}, u32[]{:S(2)}) %collective-permute-start.2) | collective-permute-done | bytes 135200 | tf_op jit(solution)/shard_map/ppermute | solution.py:346
  62.4 0.1 shard_map.103
  62.5 0.1 collective-permute-start.3
  62.6 4.8 %collective-permute-done.3 = f16[272,128]{1,0:T(8,128)(2,1)S(1)} collective-permute-done((f16[272,128]{1,0:T(8,128)(2,1)S(1)}, f16[272,128]{1,0:T(8,128)(2,1)S(1)}, u32[]{:S(2)}, u32[]{:S(2)}) %collective-permute-start.3) | collective-permute-done | bytes 69664 | tf_op jit(solution)/shard_map/ppermute | solution.py:346
  67.4 0.1 shard_map.104
  67.5 0.1 collective-permute-start.4
  67.6 5.1 %collective-permute-done.4 = f16[272,128]{1,0:T(8,128)(2,1)S(1)} collective-permute-done((f16[272,128]{1,0:T(8,128)(2,1)S(1)}, f16[272,128]{1,0:T(8,128)(2,1)S(1)}, u32[]{:S(2)}, u32[]{:S(2)}) %collective-permute-start.4) | collective-permute-done | bytes 69664 | tf_op jit(solution)/shard_map/ppermute | solution.py:346
  72.7 0.1 shard_map.105
  72.8 0.7 collective-permute-start.5
  73.5 4.1 %collective-permute-done.5 = bf16[2,128,128]{2,1,0:T(8,128)(2,1)S(1)} collective-permute-done((bf16[2,128,128]{2,1,0:T(8,128)(2,1)S(1)}, bf16[2,128,128]{2,1,0:T(8,128)(2,1)S(1)}, u32[]{:S(2)}, u32[]{:S(2)}) %collective-permute-start.5) | collective-permute-done | bytes 65568 | tf_op jit(solution)/shard_map/ppermute | solution.py:346
  77.6 0.3 collective-permute-start.7
  77.9 5.5 %collective-permute-start.6 = (bf16[4,128,128]{2,1,0:T(8,128)(2,1)S(1)}, bf16[4,128,128]{2,1,0:T(8,128)(2,1)S(1)}, u32[]{:S(2)}, u32[]{:S(2)}) collective-permute-start(bf16[4,128,128]{2,1,0:T(8,128)(2,1)S(1)} %constant_dynamic-update-slice_fusion), channel_id=1, source_target_pairs={{0,1},{1,0},{2,3},{3,2},{4,5},{5,4},{6,7},{7,6},{8,9},{9,8},{10,11... | collective-permute-start | bytes 393224 | tf_op jit(solution)/shard_map/ppermute | solution.py:362
  83.4 3.4 %collective-permute-start.8 = (bf16[4,128,128]{2,1,0:T(8,128)(2,1)S(1)}, bf16[4,128,128]{2,1,0:T(8,128)(2,1)S(1)}, u32[]{:S(2)}, u32[]{:S(2)}) collective-permute-start(bf16[4,128,128]{2,1,0:T(8,128)(2,1)S(1)} %collective-permute-done.7), channel_id=1, source_target_pairs={{0,1},{1,0},{2,3},{3,2},{4,5},{5,4},{6,7},{7,6},{8,9},{9,8},{10,11... | collective-permute-start | bytes 393224 | tf_op jit(solution)/shard_map/ppermute | solution.py:362
  86.9 1.0 shard_map.106.own_total
  87.9 1.0 shard_map.107
  89.0 10.8 %all_to_all.32.got = bf16[16,64,128]{2,1,0:T(8,128)(2,1)S(1)} all-to-all(bf16[16,64,128]{2,1,0:T(8,128)(2,1)S(1)} %shard_map.107), channel_id=1, replica_groups=mesh['y'=4,'x'=4,'z'=8,'core'=2] {'y','x'}, dimensions={0} | all-to-all | bytes 524288 | tf_op jit(solution)/shard_map/all_to_all | solution.py:337
  99.8 0.1 shard_map.108
  99.9 10.6 %all_to_all.33.got = bf16[16,80,128]{2,1,0:T(8,128)(2,1)S(1)} all-to-all(bf16[16,80,128]{2,1,0:T(8,128)(2,1)S(1)} %shard_map.108), channel_id=1, replica_groups=mesh['y'=4,'x'=4,'z'=8,'core'=2] {'y','x'}, dimensions={0} | all-to-all | bytes 655360 | tf_op jit(solution)/shard_map/all_to_all | solution.py:337
  110.5 1.1 shard_map.109.after
  111.7 2.9 %collective-permute-start.9 = (f16[1048,128]{1,0:T(8,128)(2,1)S(1)}, f16[1048,128]{1,0:T(8,128)(2,1)S(1)}, u32[]{:S(2)}, u32[]{:S(2)}) collective-permute-start(f16[1048,128]{1,0:T(8,128)(2,1)S(1)} %convert_element_type.47), channel_id=1, source_target_pairs={{0,1},{1,0},{2,3},{3,2},{4,5},{5,4},{6,7},{7,6},{8,9},{9,8},{10,11... | collective-permute-start | bytes 804872 | tf_op jit(solution)/shard_map/ppermute | solution.py:362
  114.5 1.0 shard_map.110
  115.6 0.1 collective-permute-done.9
  115.7 0.1 shard_map.111
  115.9 14.5 %all_to_all.34 = f16[8,136,128]{2,1,0:T(8,128)(2,1)S(1)} all-to-all(f16[8,136,128]{2,1,0:T(8,128)(2,1)S(1)} %convert_element_type.49), channel_id=1, replica_groups=mesh['y'=4,'x'=4,'z'=8,'core'=2] {'z'}, dimensions={0} | all-to-all | bytes 557056 | tf_op jit(solution)/shard_map/all_to_all | solution.py:337
  130.5 0.7 shard_map.112
  (32 shorter events, 0.5 us)
Async XLA Ops:
  2.3 19.4 %all-to-all-start = ((bf16[8,128,128]{2,1,0:T(8,128)(2,1)}), bf16[8,128,128]{2,1,0:T(8,128)(2,1)S(1)}, u32[]{:S(2)}, u32[]{:S(2)}) async-start(bf16[8,128,128]{2,1,0:T(8,128)(2,1)} %shard_map.95), calls=%async_computation | async-start | bytes 524288 | tf_op jit(solution)/shard_map/all_to_all | solution.py:337
  11.9 12.3 %copy-start.4 = (f32[32]{0:T(128)S(1)}, f32[32]{0:T(128)}, u32[]{:S(2)}) copy-start(f32[32]{0:T(128)} %param.14) | copy-start | bytes 388
  12.0 12.3 %copy-start.5 = (s32[128]{0:T(128)S(1)}, s32[128]{0:T(128)}, u32[]{:S(2)}) copy-start(s32[128]{0:T(128)} %param.13) | copy-start | bytes 1540
  12.0 12.4 %copy-start = (f32[128,128]{1,0:T(8,128)S(1)}, f32[128,128]{1,0:T(8,128)}, u32[]{:S(2)}) copy-start(f32[128,128]{1,0:T(8,128)} %right_ref.7) | copy-start | bytes 196612
  12.0 12.5 %copy-start.2 = (s32[16]{0:T(128)S(1)}, s32[16]{0:T(128)}, u32[]{:S(2)}) copy-start(s32[16]{0:T(128)} %param.10) | copy-start | bytes 196
  12.0 12.5 %copy-start.3 = (s32[16]{0:T(128)S(1)}, s32[16]{0:T(128)}, u32[]{:S(2)}) copy-start(s32[16]{0:T(128)} %param.9) | copy-start | bytes 196
  21.7 3.8 %collective-permute-start = (bf16[8,128,128]{2,1,0:T(8,128)(2,1)S(1)}, bf16[8,128,128]{2,1,0:T(8,128)(2,1)S(1)}, u32[]{:S(2)}, u32[]{:S(2)}) collective-permute-start(bf16[8,128,128]{2,1,0:T(8,128)(2,1)S(1)} %broadcast_multiply_fusion.own.gathered), channel_id=1, source_target_pairs={{0,1},{1,0},{2,3},{3,2},{4,5},{5,4},{6,7},{7,6},{8,9},{9,8},{10,11... | collective-permute-start | bytes 786440 | tf_op jit(solution)/shard_map/ppermute | solution.py:362
  25.5 15.9 %copy-start.1 = (f32[1024]{0:T(1024)S(1)}, f32[1024]{0:T(1024)}, u32[]{:S(2)}) copy-start(f32[1024]{0:T(1024)} %param.12) | copy-start | bytes 12292
  53.4 3.9 %collective-permute-start.1 = (f16[1048,128]{1,0:T(8,128)(2,1)S(1)}, f16[1048,128]{1,0:T(8,128)(2,1)S(1)}, u32[]{:S(2)}, u32[]{:S(2)}) collective-permute-start(f16[1048,128]{1,0:T(8,128)(2,1)S(1)} %convert_element_type.39), channel_id=1, source_target_pairs={{0,1},{1,0},{2,3},{3,2},{4,5},{5,4},{6,7},{7,6},{8,9},{9,8},{10,11... | collective-permute-start | bytes 804872 | tf_op jit(solution)/shard_map/ppermute | solution.py:362
  57.5 4.9 %collective-permute-start.2 = (f16[528,128]{1,0:T(8,128)(2,1)S(1)}, f16[528,128]{1,0:T(8,128)(2,1)S(1)}, u32[]{:S(2)}, u32[]{:S(2)}) collective-permute-start(f16[528,128]{1,0:T(8,128)(2,1)S(1)} %convert_element_type.41), channel_id=1, source_target_pairs={{0,2},{1,3},{2,0},{3,1},{4,6},{5,7},{6,4},{7,5},{8,10},{9,11},{10,... | collective-permute-start | bytes 405512 | tf_op jit(solution)/shard_map/ppermute | solution.py:346
  62.5 4.9 %collective-permute-start.3 = (f16[272,128]{1,0:T(8,128)(2,1)S(1)}, f16[272,128]{1,0:T(8,128)(2,1)S(1)}, u32[]{:S(2)}, u32[]{:S(2)}) collective-permute-start(f16[272,128]{1,0:T(8,128)(2,1)S(1)} %convert_element_type.43), channel_id=1, source_target_pairs={{0,4},{1,5},{2,6},{3,7},{4,0},{5,1},{6,2},{7,3},{8,12},{9,13},{10,... | collective-permute-start | bytes 208904 | tf_op jit(solution)/shard_map/ppermute | solution.py:346
  67.5 5.2 %collective-permute-start.4 = (f16[272,128]{1,0:T(8,128)(2,1)S(1)}, f16[272,128]{1,0:T(8,128)(2,1)S(1)}, u32[]{:S(2)}, u32[]{:S(2)}) collective-permute-start(f16[272,128]{1,0:T(8,128)(2,1)S(1)} %convert_element_type.45), channel_id=1, source_target_pairs={{0,14},{1,15},{2,12},{3,13},{4,10},{5,11},{6,8},{7,9},{8,6},{9,7},... | collective-permute-start | bytes 208904 | tf_op jit(solution)/shard_map/ppermute | solution.py:346
  72.8 4.8 %collective-permute-start.5 = (bf16[2,128,128]{2,1,0:T(8,128)(2,1)S(1)}, bf16[2,128,128]{2,1,0:T(8,128)(2,1)S(1)}, u32[]{:S(2)}, u32[]{:S(2)}) collective-permute-start(bf16[2,128,128]{2,1,0:T(8,128)(2,1)S(1)} %get-tuple-element.31), channel_id=1, source_target_pairs={{0,4},{1,5},{2,6},{3,7},{4,0},{5,1},{6,2},{7,3},{8,12},{9,13},{10,... | collective-permute-start | bytes 196616 | tf_op jit(solution)/shard_map/ppermute | solution.py:346
  77.6 5.8 %collective-permute-start.7 = (bf16[4,128,128]{2,1,0:T(8,128)(2,1)S(1)}, bf16[4,128,128]{2,1,0:T(8,128)(2,1)S(1)}, u32[]{:S(2)}, u32[]{:S(2)}) collective-permute-start(bf16[4,128,128]{2,1,0:T(8,128)(2,1)S(1)} %constant_dynamic-update-slice_fusion), channel_id=1, source_target_pairs={{0,2},{1,3},{2,0},{3,1},{4,6},{5,7},{6,4},{7,5},{8,10},{9,11},{10,... | collective-permute-start | bytes 393224 | tf_op jit(solution)/shard_map/ppermute | solution.py:346
  77.9 10.0 %collective-permute-start.6 = (bf16[4,128,128]{2,1,0:T(8,128)(2,1)S(1)}, bf16[4,128,128]{2,1,0:T(8,128)(2,1)S(1)}, u32[]{:S(2)}, u32[]{:S(2)}) collective-permute-start(bf16[4,128,128]{2,1,0:T(8,128)(2,1)S(1)} %constant_dynamic-update-slice_fusion), channel_id=1, source_target_pairs={{0,1},{1,0},{2,3},{3,2},{4,5},{5,4},{6,7},{7,6},{8,9},{9,8},{10,11... | collective-permute-start | bytes 393224 | tf_op jit(solution)/shard_map/ppermute | solution.py:362
  83.4 4.5 %collective-permute-start.8 = (bf16[4,128,128]{2,1,0:T(8,128)(2,1)S(1)}, bf16[4,128,128]{2,1,0:T(8,128)(2,1)S(1)}, u32[]{:S(2)}, u32[]{:S(2)}) collective-permute-start(bf16[4,128,128]{2,1,0:T(8,128)(2,1)S(1)} %collective-permute-done.7), channel_id=1, source_target_pairs={{0,1},{1,0},{2,3},{3,2},{4,5},{5,4},{6,7},{7,6},{8,9},{9,8},{10,11... | collective-permute-start | bytes 393224 | tf_op jit(solution)/shard_map/ppermute | solution.py:362
  111.7 4.0 %collective-permute-start.9 = (f16[1048,128]{1,0:T(8,128)(2,1)S(1)}, f16[1048,128]{1,0:T(8,128)(2,1)S(1)}, u32[]{:S(2)}, u32[]{:S(2)}) collective-permute-start(f16[1048,128]{1,0:T(8,128)(2,1)S(1)} %convert_element_type.47), channel_id=1, source_target_pairs={{0,1},{1,0},{2,3},{3,2},{4,5},{5,4},{6,7},{7,6},{8,9},{9,8},{10,11... | collective-permute-start | bytes 804872 | tf_op jit(solution)/shard_map/ppermute | solution.py:362

commit v7 on v6

--- a/solution.py
+++ b/solution.py
@@ -20,7 +20,6 @@
 TOP = 10.0
 SUM_TOP = 14.0
 VMEM_LIMIT = 16 * 1024 * 1024
-VMEM_WHOLE = 60 * 1024 * 1024
 
 
 def call(kernel, out_shape, operands, smem=0, scratch=()):
@@ -57,19 +56,10 @@
     return rows_of(column_sum(reg * square), column_sum(square), column_sum(value * image))
 
 
-def copies_kernel(right_in, low_out, right, low, sems):
-    load = pltpu.make_async_copy(right_in, right, sems.at[0])
-    load.start()
-    load.wait()
-    low[...] = right[...].astype(jnp.bfloat16)
-    stores = [
-        pltpu.make_async_copy(low, low_out.at[block], sems.at[block + 1])
-        for block in range(low_out.shape[0])
-    ]
-    for store in stores:
-        store.start()
-    for store in stores:
-        store.wait()
+def copies_kernel(right_ref, low_ref):
+    low = right_ref[...].astype(jnp.bfloat16)
+    for block in range(low_ref.shape[0]):
+        low_ref[block] = low
 
 
 def start_kernel(right_ref, reg_ref, sums_ref):
@@ -260,7 +250,7 @@
     return blocks, kept_sums[:KINDS] + join(tail[:at]) * jnp.exp2(tail[at : at + KINDS] - TOP)
 
 
-def spread_kernel(height, keep, keep_sums, swapped, kept, coded, kept_sums, total):
+def spread_kernel(core, height, keep, keep_sums, swapped, kept, coded, kept_sums, total):
     cells = CELLS
     for block in range(COLS):
         part, sums = pair_sum(keep, keep_sums, swapped, block)
@@ -272,8 +262,8 @@
         return [total[rows_at(z * cells, cells), :] for z in at]
 
     emit(
-        blocks([own, jnp.bitwise_xor(own, 2)]),
-        blocks([jnp.bitwise_xor(own, 1), jnp.bitwise_xor(own, 3)]),
+        blocks([own, jnp.bitwise_xor(own, 2 - core[0])]),
+        blocks([jnp.bitwise_xor(own, 1 + core[0]), jnp.bitwise_xor(own, 3)]),
         sums,
         kept,
         coded,
@@ -339,22 +329,30 @@
 
 def along_z(value, to):
     pairs = [
-        (z * CORES + core, to(z) * CORES + core)
+        (z * CORES + core, to(z, core) * CORES + core)
         for z in range(lax.axis_size("z"))
         for core in range(CORES)
     ]
     return lax.ppermute(value, ("z", "core"), pairs)
 
 
-def near(z):
+def near(z, core):
     return z ^ 1
 
 
-def far(z):
+def far(z, core):
     return z ^ 2
 
 
-def mirror(z):
+def first(z, core):
+    return z ^ (1 + core)
+
+
+def second(z, core):
+    return z ^ (2 - core)
+
+
+def mirror(z, core):
     return COLS - 1 - z
 
 
@@ -373,20 +371,8 @@
     height = lax.axis_index("z").astype(jnp.int32).reshape(1)
     dp = lax.axis_index(DP).astype(jnp.int32).reshape(1)
 
-    anywhere = pl.BlockSpec(memory_space=pl.ANY)
-    copies = pl.pallas_call(
-        copies_kernel,
-        out_shape=bf16(n_z, cells, probes),
-        in_specs=[anywhere],
-        out_specs=anywhere,
-        scratch_shapes=[
-            pltpu.VMEM((cells, probes), jnp.float32),
-            pltpu.VMEM((cells, probes), jnp.bfloat16),
-            pltpu.SemaphoreType.DMA((n_z + 1,)),
-        ],
-        compiler_params=pltpu.CompilerParams(vmem_limit_bytes=VMEM_WHOLE),
-    )
-    own = exchange(copies(right_side), "z")
+    copies = call(copies_kernel, bf16(n_z, cells, probes), (right_side,))
+    own = exchange(copies, "z")
     live = jnp.arange(tiles.shape[0], dtype=jnp.int32) < tile_count
     tiles = jnp.where(live[:, None, None], tiles, jnp.zeros_like(tiles))
     own = own * (tiles[0, :1, :1] == tiles[0, :1, :1]).astype(jnp.bfloat16)
@@ -454,12 +440,12 @@
     terms = halved(
         spread_kernel,
         4,
-        (height, *terms),
-        near,
-        smem=1,
+        (core, height, *terms),
+        first,
+        smem=2,
         scratch=[pltpu.VMEM((n_z * cells, probes), jnp.float32)],
     )
-    terms = halved(halve_kernel, 2, terms, far)
+    terms = halved(halve_kernel, 2, terms, second)
     terms = halved(cross_kernel, 2, (*terms, right_side, reg), mirror)
     residual, image, low, sums, keep = call(
         first_update_kernel,

time: 132 us -> 132 us (level)
  waiting for transfers between devices: 24.8 us -> 22.6 us
  starting transfers between devices: 27.6 us -> 29.6 us
    ppermute x5, starting transfers between devices: 1.54 us -> 4.36 us  [along_z(): return lax.ppermute(value, ('z', 'core'), pairs)]
    ppermute x5, waiting for transfers between devices: 18.5 us -> 16.4 us  [along_z(): return lax.ppermute(value, ('z', 'core'), pairs)]
    pallas_call x1 -> x0, Pallas kernels: 1.62 us -> none  [body(): own = exchange(copies(right_side), 'z')]
    pallas_call x17 -> x18, Pallas kernels: 9.82 us -> 10.5 us  [call(): pl.pallas_call(kernel, out_shape=out_shape, in_specs=[pl.BlockSpec(memory...]
where the time goes in v7:
time: 132 us; the launch traced here: 131 us
  blocking collectives  61.6 us (47%)
  starting transfers between devices  29.6 us (22%)
  waiting for transfers between devices  22.6 us (17%)
  Pallas kernels  10.5 us (8%)
  between operations  2.94 us (2%)
  other arithmetic  2.34 us (2%)
  local copies, waits for them, and re-layouts  1.48 us (1%)
    all_to_all x5, blocking collectives, exchange(): return lax.all_to_all(value, axis, 0, 0)  61.6 us
    ppermute x5, waiting for transfers between devices, along_z(): return lax.ppermute(value, ('z', 'core'), pairs)  16.4 us
    ppermute x5, starting transfers between devices, swap(): return lax.ppermute(value, 'core', [(0, 1), (1, 0)])  16.2 us
    pallas_call x18, Pallas kernels, call(): pl.pallas_call(kernel, out_shape=out_shape, in_specs=[pl.BlockSpec(memory...  10.5 us
    all_to_all x1, starting transfers between devices, exchange(): return lax.all_to_all(value, axis, 0, 0)  9.01 us
    all_to_all x1, waiting for transfers between devices, exchange(): return lax.all_to_all(value, axis, 0, 0)  5.99 us
    ppermute x5, starting transfers between devices, along_z(): return lax.ppermute(value, ('z', 'core'), pairs)  4.36 us
  transfers between devices with their start and end apart: 11, of which 7 were waited for; matrix products, arithmetic and copies ran while one was open for 2% of the time, Pallas kernels for 3%

profile of v7, /device:TPU:1, one launch (start us, length us, event | category | flops | bytes accessed | tf_op | source)
XLA Modules:
  0.0 131.1 jit_solution(17403863889132302747)
XLA Ops:
  0.6 0.0 copy-start
  0.6 0.8 copy-done
  1.5 0.7 shard_map.95
  2.2 9.0 %all-to-all-start = ((bf16[8,128,128]{2,1,0:T(8,128)(2,1)}), bf16[8,128,128]{2,1,0:T(8,128)(2,1)S(1)}, u32[]{:S(2)}, u32[]{:S(2)}) async-start(bf16[8,128,128]{2,1,0:T(8,128)(2,1)} %shard_map.95), calls=%async_computation | async-start | bytes 524288 | tf_op jit(solution)/shard_map/all_to_all | solution.py:327
  11.9 0.0 copy-start.5
  11.9 0.0 copy-start.1
  11.9 1.8 %broadcast_select_fusion.tiles = bf16[16,256,256]{2,1,0:T(8,128)(2,1)S(1)} fusion(bf16[16,256,256]{2,1,0:T(8,128)(2,1)} %param.8, pred[16]{0:T(512)(128)(4,1)S(1)} %iota_compare_fusion.1), kind=kLoop, calls=%fused_computation | loop fusion | flops 1048576 | bytes 4194320 | tf_op jit(solution)/shard_map/jit(_where)/select_n | solution.py:377
  13.8 0.5 slice.5
  15.6 6.0 %all-to-all-done = bf16[8,128,128]{2,1,0:T(8,128)(2,1)S(1)} async-done(((bf16[8,128,128]{2,1,0:T(8,128)(2,1)}), bf16[8,128,128]{2,1,0:T(8,128)(2,1)S(1)}, u32[]{:S(2)}, u32[]{:S(2)}) %all-to-all-start) | async-done | bytes 262176 | tf_op jit(solution)/shard_map/all_to_all | solution.py:327
  21.6 2.5 %collective-permute-start = (bf16[8,128,128]{2,1,0:T(8,128)(2,1)S(1)}, bf16[8,128,128]{2,1,0:T(8,128)(2,1)S(1)}, u32[]{:S(2)}, u32[]{:S(2)}) collective-permute-start(bf16[8,128,128]{2,1,0:T(8,128)(2,1)S(1)} %broadcast_multiply_fusion.own.gathered), channel_id=1, source_target_pairs={{0,1},{1,0},{2,3},{3,2},{4,5},{5,4},{6,7},{7,6},{8,9},{9,8},{10,11... | collective-permute-start | bytes 786440 | tf_op jit(solution)/shard_map/ppermute | solution.py:360
  24.2 0.1 select_reduce_fusion
  24.2 0.1 broadcast_in_dim.31.reg_ref
  24.4 1.0 shard_map.96.own_total
  25.5 1.0 shard_map.98
  26.5 14.8 %all_to_all.30.got = bf16[16,64,128]{2,1,0:T(8,128)(2,1)S(1)} all-to-all(bf16[16,64,128]{2,1,0:T(8,128)(2,1)S(1)} %shard_map.98), channel_id=1, replica_groups=mesh['y'=4,'x'=4,'z'=8,'core'=2] {'y','x'}, dimensions={0} | all-to-all | bytes 524288 | tf_op jit(solution)/shard_map/all_to_all | solution.py:327
  41.3 0.1 shard_map.99
  41.5 10.7 %all_to_all.31.got = bf16[16,80,128]{2,1,0:T(8,128)(2,1)S(1)} all-to-all(bf16[16,80,128]{2,1,0:T(8,128)(2,1)S(1)} %shard_map.99), channel_id=1, replica_groups=mesh['y'=4,'x'=4,'z'=8,'core'=2] {'y','x'}, dimensions={0} | all-to-all | bytes 655360 | tf_op jit(solution)/shard_map/all_to_all | solution.py:327
  52.1 1.1 shard_map.100.after
  53.3 2.7 %collective-permute-start.1 = (f16[1048,128]{1,0:T(8,128)(2,1)S(1)}, f16[1048,128]{1,0:T(8,128)(2,1)S(1)}, u32[]{:S(2)}, u32[]{:S(2)}) collective-permute-start(f16[1048,128]{1,0:T(8,128)(2,1)S(1)} %convert_element_type.39), channel_id=1, source_target_pairs={{0,1},{1,0},{2,3},{3,2},{4,5},{5,4},{6,7},{7,6},{8,9},{9,8},{10,11... | collective-permute-start | bytes 804872 | tf_op jit(solution)/shard_map/ppermute | solution.py:360
  56.0 1.0 shard_map.101
  57.0 0.1 collective-permute-done.1
  57.2 0.1 shard_map.102
  57.4 0.1 collective-permute-start.2
  57.5 6.2 %collective-permute-done.2 = f16[528,128]{1,0:T(8,128)(2,1)S(1)} collective-permute-done((f16[528,128]{1,0:T(8,128)(2,1)S(1)}, f16[528,128]{1,0:T(8,128)(2,1)S(1)}, u32[]{:S(2)}, u32[]{:S(2)}) %collective-permute-start.2) | collective-permute-done | bytes 135200 | tf_op jit(solution)/shard_map/ppermute | solution.py:336
  63.7 0.1 shard_map.103
  63.8 0.1 collective-permute-start.3
  63.9 3.1 %collective-permute-done.3 = f16[272,128]{1,0:T(8,128)(2,1)S(1)} collective-permute-done((f16[272,128]{1,0:T(8,128)(2,1)S(1)}, f16[272,128]{1,0:T(8,128)(2,1)S(1)}, u32[]{:S(2)}, u32[]{:S(2)}) %collective-permute-start.3) | collective-permute-done | bytes 69664 | tf_op jit(solution)/shard_map/ppermute | solution.py:336
  67.1 0.1 shard_map.104
  67.2 0.1 collective-permute-start.4
  67.3 4.4 %collective-permute-done.4 = f16[272,128]{1,0:T(8,128)(2,1)S(1)} collective-permute-done((f16[272,128]{1,0:T(8,128)(2,1)S(1)}, f16[272,128]{1,0:T(8,128)(2,1)S(1)}, u32[]{:S(2)}, u32[]{:S(2)}) %collective-permute-start.4) | collective-permute-done | bytes 69664 | tf_op jit(solution)/shard_map/ppermute | solution.py:336
  71.6 0.1 shard_map.105
  71.7 1.4 %collective-permute-start.5 = (bf16[2,128,128]{2,1,0:T(8,128)(2,1)S(1)}, bf16[2,128,128]{2,1,0:T(8,128)(2,1)S(1)}, u32[]{:S(2)}, u32[]{:S(2)}) collective-permute-start(bf16[2,128,128]{2,1,0:T(8,128)(2,1)S(1)} %get-tuple-element.31), channel_id=1, source_target_pairs={{0,4},{1,5},{2,6},{3,7},{4,0},{5,1},{6,2},{7,3},{8,12},{9,13},{10,... | collective-permute-start | bytes 196616 | tf_op jit(solution)/shard_map/ppermute | solution.py:336
  73.2 2.7 %collective-permute-done.5 = bf16[2,128,128]{2,1,0:T(8,128)(2,1)S(1)} collective-permute-done((bf16[2,128,128]{2,1,0:T(8,128)(2,1)S(1)}, bf16[2,128,128]{2,1,0:T(8,128)(2,1)S(1)}, u32[]{:S(2)}, u32[]{:S(2)}) %collective-permute-start.5) | collective-permute-done | bytes 65568 | tf_op jit(solution)/shard_map/ppermute | solution.py:336
  75.8 2.6 %collective-permute-start.7 = (bf16[4,128,128]{2,1,0:T(8,128)(2,1)S(1)}, bf16[4,128,128]{2,1,0:T(8,128)(2,1)S(1)}, u32[]{:S(2)}, u32[]{:S(2)}) collective-permute-start(bf16[4,128,128]{2,1,0:T(8,128)(2,1)S(1)} %constant_dynamic-update-slice_fusion), channel_id=1, source_target_pairs={{0,2},{1,3},{2,0},{3,1},{4,6},{5,7},{6,4},{7,5},{8,10},{9,11},{10,... | collective-permute-start | bytes 393224 | tf_op jit(solution)/shard_map/ppermute | solution.py:336
  78.5 4.5 %collective-permute-start.6 = (bf16[4,128,128]{2,1,0:T(8,128)(2,1)S(1)}, bf16[4,128,128]{2,1,0:T(8,128)(2,1)S(1)}, u32[]{:S(2)}, u32[]{:S(2)}) collective-permute-start(bf16[4,128,128]{2,1,0:T(8,128)(2,1)S(1)} %constant_dynamic-update-slice_fusion), channel_id=1, source_target_pairs={{0,1},{1,0},{2,3},{3,2},{4,5},{5,4},{6,7},{7,6},{8,9},{9,8},{10,11... | collective-permute-start | bytes 393224 | tf_op jit(solution)/shard_map/ppermute | solution.py:360
  83.0 3.6 %collective-permute-start.8 = (bf16[4,128,128]{2,1,0:T(8,128)(2,1)S(1)}, bf16[4,128,128]{2,1,0:T(8,128)(2,1)S(1)}, u32[]{:S(2)}, u32[]{:S(2)}) collective-permute-start(bf16[4,128,128]{2,1,0:T(8,128)(2,1)S(1)} %collective-permute-done.7), channel_id=1, source_target_pairs={{0,1},{1,0},{2,3},{3,2},{4,5},{5,4},{6,7},{7,6},{8,9},{9,8},{10,11... | collective-permute-start | bytes 393224 | tf_op jit(solution)/shard_map/ppermute | solution.py:360
  86.6 1.0 shard_map.106.own_total
  87.7 1.0 shard_map.107
  88.7 10.8 %all_to_all.32.got = bf16[16,64,128]{2,1,0:T(8,128)(2,1)S(1)} all-to-all(bf16[16,64,128]{2,1,0:T(8,128)(2,1)S(1)} %shard_map.107), channel_id=1, replica_groups=mesh['y'=4,'x'=4,'z'=8,'core'=2] {'y','x'}, dimensions={0} | all-to-all | bytes 524288 | tf_op jit(solution)/shard_map/all_to_all | solution.py:327
  99.6 0.1 shard_map.108
  99.7 10.6 %all_to_all.33.got = bf16[16,80,128]{2,1,0:T(8,128)(2,1)S(1)} all-to-all(bf16[16,80,128]{2,1,0:T(8,128)(2,1)S(1)} %shard_map.108), channel_id=1, replica_groups=mesh['y'=4,'x'=4,'z'=8,'core'=2] {'y','x'}, dimensions={0} | all-to-all | bytes 655360 | tf_op jit(solution)/shard_map/all_to_all | solution.py:327
  110.3 1.1 shard_map.109.after
  111.5 2.8 %collective-permute-start.9 = (f16[1048,128]{1,0:T(8,128)(2,1)S(1)}, f16[1048,128]{1,0:T(8,128)(2,1)S(1)}, u32[]{:S(2)}, u32[]{:S(2)}) collective-permute-start(f16[1048,128]{1,0:T(8,128)(2,1)S(1)} %convert_element_type.47), channel_id=1, source_target_pairs={{0,1},{1,0},{2,3},{3,2},{4,5},{5,4},{6,7},{7,6},{8,9},{9,8},{10,11... | collective-permute-start | bytes 804872 | tf_op jit(solution)/shard_map/ppermute | solution.py:360
  114.3 1.0 shard_map.110
  115.3 0.1 collective-permute-done.9
  115.5 0.1 shard_map.111
  115.7 14.7 %all_to_all.34 = f16[8,136,128]{2,1,0:T(8,128)(2,1)S(1)} all-to-all(f16[8,136,128]{2,1,0:T(8,128)(2,1)S(1)} %convert_element_type.49), channel_id=1, replica_groups=mesh['y'=4,'x'=4,'z'=8,'core'=2] {'z'}, dimensions={0} | all-to-all | bytes 557056 | tf_op jit(solution)/shard_map/all_to_all | solution.py:327
  130.4 0.7 shard_map.112
  (34 shorter events, 0.5 us)
Async XLA Ops:
  0.6 0.8 copy-start
  2.2 19.4 %all-to-all-start = ((bf16[8,128,128]{2,1,0:T(8,128)(2,1)}), bf16[8,128,128]{2,1,0:T(8,128)(2,1)S(1)}, u32[]{:S(2)}, u32[]{:S(2)}) async-start(bf16[8,128,128]{2,1,0:T(8,128)(2,1)} %shard_map.95), calls=%async_computation | async-start | bytes 524288 | tf_op jit(solution)/shard_map/all_to_all | solution.py:327
  11.9 12.3 %copy-start.5 = (f32[32]{0:T(128)S(1)}, f32[32]{0:T(128)}, u32[]{:S(2)}) copy-start(f32[32]{0:T(128)} %param.14) | copy-start | bytes 388
  11.9 12.3 %copy-start.6 = (s32[128]{0:T(128)S(1)}, s32[128]{0:T(128)}, u32[]{:S(2)}) copy-start(s32[128]{0:T(128)} %param.13) | copy-start | bytes 1540
  11.9 12.4 %copy-start.1 = (f32[128,128]{1,0:T(8,128)S(1)}, f32[128,128]{1,0:T(8,128)}, u32[]{:S(2)}) copy-start(f32[128,128]{1,0:T(8,128)} %right_ref.9) | copy-start | bytes 196612
  11.9 12.5 %copy-start.3 = (s32[16]{0:T(128)S(1)}, s32[16]{0:T(128)}, u32[]{:S(2)}) copy-start(s32[16]{0:T(128)} %param.10) | copy-start | bytes 196
  11.9 12.5 %copy-start.4 = (s32[16]{0:T(128)S(1)}, s32[16]{0:T(128)}, u32[]{:S(2)}) copy-start(s32[16]{0:T(128)} %param.9) | copy-start | bytes 196
  21.6 3.8 %collective-permute-start = (bf16[8,128,128]{2,1,0:T(8,128)(2,1)S(1)}, bf16[8,128,128]{2,1,0:T(8,128)(2,1)S(1)}, u32[]{:S(2)}, u32[]{:S(2)}) collective-permute-start(bf16[8,128,128]{2,1,0:T(8,128)(2,1)S(1)} %broadcast_multiply_fusion.own.gathered), channel_id=1, source_target_pairs={{0,1},{1,0},{2,3},{3,2},{4,5},{5,4},{6,7},{7,6},{8,9},{9,8},{10,11... | collective-permute-start | bytes 786440 | tf_op jit(solution)/shard_map/ppermute | solution.py:360
  25.4 15.9 %copy-start.2 = (f32[1024]{0:T(1024)S(1)}, f32[1024]{0:T(1024)}, u32[]{:S(2)}) copy-start(f32[1024]{0:T(1024)} %param.12) | copy-start | bytes 12292
  53.3 3.9 %collective-permute-start.1 = (f16[1048,128]{1,0:T(8,128)(2,1)S(1)}, f16[1048,128]{1,0:T(8,128)(2,1)S(1)}, u32[]{:S(2)}, u32[]{:S(2)}) collective-permute-start(f16[1048,128]{1,0:T(8,128)(2,1)S(1)} %convert_element_type.39), channel_id=1, source_target_pairs={{0,1},{1,0},{2,3},{3,2},{4,5},{5,4},{6,7},{7,6},{8,9},{9,8},{10,11... | collective-permute-start | bytes 804872 | tf_op jit(solution)/shard_map/ppermute | solution.py:360
  57.4 6.3 %collective-permute-start.2 = (f16[528,128]{1,0:T(8,128)(2,1)S(1)}, f16[528,128]{1,0:T(8,128)(2,1)S(1)}, u32[]{:S(2)}, u32[]{:S(2)}) collective-permute-start(f16[528,128]{1,0:T(8,128)(2,1)S(1)} %convert_element_type.41), channel_id=1, source_target_pairs={{0,2},{1,5},{2,0},{3,7},{4,6},{5,1},{6,4},{7,3},{8,10},{9,13},{10,... | collective-permute-start | bytes 405512 | tf_op jit(solution)/shard_map/ppermute | solution.py:336
  63.8 3.2 %collective-permute-start.3 = (f16[272,128]{1,0:T(8,128)(2,1)S(1)}, f16[272,128]{1,0:T(8,128)(2,1)S(1)}, u32[]{:S(2)}, u32[]{:S(2)}) collective-permute-start(f16[272,128]{1,0:T(8,128)(2,1)S(1)} %convert_element_type.43), channel_id=1, source_target_pairs={{0,4},{1,3},{2,6},{3,1},{4,0},{5,7},{6,2},{7,5},{8,12},{9,11},{10,... | collective-permute-start | bytes 208904 | tf_op jit(solution)/shard_map/ppermute | solution.py:336
  67.2 4.5 %collective-permute-start.4 = (f16[272,128]{1,0:T(8,128)(2,1)S(1)}, f16[272,128]{1,0:T(8,128)(2,1)S(1)}, u32[]{:S(2)}, u32[]{:S(2)}) collective-permute-start(f16[272,128]{1,0:T(8,128)(2,1)S(1)} %convert_element_type.45), channel_id=1, source_target_pairs={{0,14},{1,15},{2,12},{3,13},{4,10},{5,11},{6,8},{7,9},{8,6},{9,7},... | collective-permute-start | bytes 208904 | tf_op jit(solution)/shard_map/ppermute | solution.py:336
  71.7 4.1 %collective-permute-start.5 = (bf16[2,128,128]{2,1,0:T(8,128)(2,1)S(1)}, bf16[2,128,128]{2,1,0:T(8,128)(2,1)S(1)}, u32[]{:S(2)}, u32[]{:S(2)}) collective-permute-start(bf16[2,128,128]{2,1,0:T(8,128)(2,1)S(1)} %get-tuple-element.31), channel_id=1, source_target_pairs={{0,4},{1,5},{2,6},{3,7},{4,0},{5,1},{6,2},{7,3},{8,12},{9,13},{10,... | collective-permute-start | bytes 196616 | tf_op jit(solution)/shard_map/ppermute | solution.py:336
  75.8 7.1 %collective-permute-start.7 = (bf16[4,128,128]{2,1,0:T(8,128)(2,1)S(1)}, bf16[4,128,128]{2,1,0:T(8,128)(2,1)S(1)}, u32[]{:S(2)}, u32[]{:S(2)}) collective-permute-start(bf16[4,128,128]{2,1,0:T(8,128)(2,1)S(1)} %constant_dynamic-update-slice_fusion), channel_id=1, source_target_pairs={{0,2},{1,3},{2,0},{3,1},{4,6},{5,7},{6,4},{7,5},{8,10},{9,11},{10,... | collective-permute-start | bytes 393224 | tf_op jit(solution)/shard_map/ppermute | solution.py:336
  78.5 9.2 %collective-permute-start.6 = (bf16[4,128,128]{2,1,0:T(8,128)(2,1)S(1)}, bf16[4,128,128]{2,1,0:T(8,128)(2,1)S(1)}, u32[]{:S(2)}, u32[]{:S(2)}) collective-permute-start(bf16[4,128,128]{2,1,0:T(8,128)(2,1)S(1)} %constant_dynamic-update-slice_fusion), channel_id=1, source_target_pairs={{0,1},{1,0},{2,3},{3,2},{4,5},{5,4},{6,7},{7,6},{8,9},{9,8},{10,11... | collective-permute-start | bytes 393224 | tf_op jit(solution)/shard_map/ppermute | solution.py:360
  83.0 4.7 %collective-permute-start.8 = (bf16[4,128,128]{2,1,0:T(8,128)(2,1)S(1)}, bf16[4,128,128]{2,1,0:T(8,128)(2,1)S(1)}, u32[]{:S(2)}, u32[]{:S(2)}) collective-permute-start(bf16[4,128,128]{2,1,0:T(8,128)(2,1)S(1)} %collective-permute-done.7), channel_id=1, source_target_pairs={{0,1},{1,0},{2,3},{3,2},{4,5},{5,4},{6,7},{7,6},{8,9},{9,8},{10,11... | collective-permute-start | bytes 393224 | tf_op jit(solution)/shard_map/ppermute | solution.py:360
  111.5 4.0 %collective-permute-start.9 = (f16[1048,128]{1,0:T(8,128)(2,1)S(1)}, f16[1048,128]{1,0:T(8,128)(2,1)S(1)}, u32[]{:S(2)}, u32[]{:S(2)}) collective-permute-start(f16[1048,128]{1,0:T(8,128)(2,1)S(1)} %convert_element_type.47), channel_id=1, source_target_pairs={{0,1},{1,0},{2,3},{3,2},{4,5},{5,4},{6,7},{7,6},{8,9},{9,8},{10,11... | collective-permute-start | bytes 804872 | tf_op jit(solution)/shard_map/ppermute | solution.py:360

commit v8 on v7

--- a/solution.py
+++ b/solution.py
@@ -262,8 +262,8 @@
         return [total[rows_at(z * cells, cells), :] for z in at]
 
     emit(
-        blocks([own, jnp.bitwise_xor(own, 2 - core[0])]),
-        blocks([jnp.bitwise_xor(own, 1 + core[0]), jnp.bitwise_xor(own, 3)]),
+        blocks([own, jnp.bitwise_xor(own, 1 + core[0])]),
+        blocks([jnp.bitwise_xor(own, 2 - core[0]), jnp.bitwise_xor(own, 3)]),
         sums,
         kept,
         coded,
@@ -345,11 +345,11 @@
 
 
 def first(z, core):
+    return z ^ (2 - core)
+
+
+def second(z, core):
     return z ^ (1 + core)
-
-
-def second(z, core):
-    return z ^ (2 - core)
 
 
 def mirror(z, core):

time: 132 us -> 131 us (level)
  starting transfers between devices: 29.6 us -> 33.1 us
  waiting for transfers between devices: 22.6 us -> 19.3 us
    ppermute x5, waiting for transfers between devices: 16.4 us -> 13 us  [along_z(): return lax.ppermute(value, ('z', 'core'), pairs)]
    ppermute x5, starting transfers between devices: 4.36 us -> 7.23 us  [along_z(): return lax.ppermute(value, ('z', 'core'), pairs)]
where the time goes in v8:
time: 131 us
  blocking collectives  61.3 us (47%)
  starting transfers between devices  33.1 us (25%)
  waiting for transfers between devices  19.3 us (15%)
  Pallas kernels  10.5 us (8%)
  between operations  2.92 us (2%)
  other arithmetic  2.34 us (2%)
  local copies, waits for them, and re-layouts  1.48 us (1%)
    all_to_all x5, blocking collectives, exchange(): return lax.all_to_all(value, axis, 0, 0)  61.3 us
    ppermute x5, starting transfers between devices, swap(): return lax.ppermute(value, 'core', [(0, 1), (1, 0)])  16.9 us
    ppermute x5, waiting for transfers between devices, along_z(): return lax.ppermute(value, ('z', 'core'), pairs)  13 us
    pallas_call x18, Pallas kernels, call(): pl.pallas_call(kernel, out_shape=out_shape, in_specs=[pl.BlockSpec(memory...  10.5 us
    all_to_all x1, starting transfers between devices, exchange(): return lax.all_to_all(value, axis, 0, 0)  9.01 us
    ppermute x5, starting transfers between devices, along_z(): return lax.ppermute(value, ('z', 'core'), pairs)  7.23 us
    all_to_all x1, waiting for transfers between devices, exchange(): return lax.all_to_all(value, axis, 0, 0)  5.99 us
  transfers between devices with their start and end apart: 11, of which 7 were waited for; matrix products, arithmetic and copies ran while one was open for 2% of the time, Pallas kernels for 3%

profile of v8, /device:TPU:1, one launch (start us, length us, event | category | flops | bytes accessed | tf_op | source)
XLA Modules:
  0.0 131.0 jit_solution(7471297247687238713)
XLA Ops:
  0.6 0.0 copy-start
  0.6 0.8 copy-done
  1.5 0.7 shard_map.95
  2.2 9.0 %all-to-all-start = ((bf16[8,128,128]{2,1,0:T(8,128)(2,1)}), bf16[8,128,128]{2,1,0:T(8,128)(2,1)S(1)}, u32[]{:S(2)}, u32[]{:S(2)}) async-start(bf16[8,128,128]{2,1,0:T(8,128)(2,1)} %shard_map.95), calls=%async_computation | async-start | bytes 524288 | tf_op jit(solution)/shard_map/all_to_all | solution.py:327
  11.9 0.0 copy-start.5
  11.9 0.0 copy-start.1
  11.9 1.8 %broadcast_select_fusion.tiles = bf16[16,256,256]{2,1,0:T(8,128)(2,1)S(1)} fusion(bf16[16,256,256]{2,1,0:T(8,128)(2,1)} %param.8, pred[16]{0:T(512)(128)(4,1)S(1)} %iota_compare_fusion.1), kind=kLoop, calls=%fused_computation | loop fusion | flops 1048576 | bytes 4194320 | tf_op jit(solution)/shard_map/jit(_where)/select_n | solution.py:377
  13.8 0.5 slice.5
  15.6 6.0 %all-to-all-done = bf16[8,128,128]{2,1,0:T(8,128)(2,1)S(1)} async-done(((bf16[8,128,128]{2,1,0:T(8,128)(2,1)}), bf16[8,128,128]{2,1,0:T(8,128)(2,1)S(1)}, u32[]{:S(2)}, u32[]{:S(2)}) %all-to-all-start) | async-done | bytes 262176 | tf_op jit(solution)/shard_map/all_to_all | solution.py:327
  21.6 2.5 %collective-permute-start = (bf16[8,128,128]{2,1,0:T(8,128)(2,1)S(1)}, bf16[8,128,128]{2,1,0:T(8,128)(2,1)S(1)}, u32[]{:S(2)}, u32[]{:S(2)}) collective-permute-start(bf16[8,128,128]{2,1,0:T(8,128)(2,1)S(1)} %broadcast_multiply_fusion.own.gathered), channel_id=1, source_target_pairs={{0,1},{1,0},{2,3},{3,2},{4,5},{5,4},{6,7},{7,6},{8,9},{9,8},{10,11... | collective-permute-start | bytes 786440 | tf_op jit(solution)/shard_map/ppermute | solution.py:360
  24.2 0.1 select_reduce_fusion
  24.2 0.1 broadcast_in_dim.31.reg_ref
  24.4 1.0 shard_map.96.own_total
  25.5 1.0 shard_map.98
  26.5 14.8 %all_to_all.30.got = bf16[16,64,128]{2,1,0:T(8,128)(2,1)S(1)} all-to-all(bf16[16,64,128]{2,1,0:T(8,128)(2,1)S(1)} %shard_map.98), channel_id=1, replica_groups=mesh['y'=4,'x'=4,'z'=8,'core'=2] {'y','x'}, dimensions={0} | all-to-all | bytes 524288 | tf_op jit(solution)/shard_map/all_to_all | solution.py:327
  41.3 0.1 shard_map.99
  41.5 10.7 %all_to_all.31.got = bf16[16,80,128]{2,1,0:T(8,128)(2,1)S(1)} all-to-all(bf16[16,80,128]{2,1,0:T(8,128)(2,1)S(1)} %shard_map.99), channel_id=1, replica_groups=mesh['y'=4,'x'=4,'z'=8,'core'=2] {'y','x'}, dimensions={0} | all-to-all | bytes 655360 | tf_op jit(solution)/shard_map/all_to_all | solution.py:327
  52.1 1.1 shard_map.100.after
  53.3 2.7 %collective-permute-start.1 = (f16[1048,128]{1,0:T(8,128)(2,1)S(1)}, f16[1048,128]{1,0:T(8,128)(2,1)S(1)}, u32[]{:S(2)}, u32[]{:S(2)}) collective-permute-start(f16[1048,128]{1,0:T(8,128)(2,1)S(1)} %convert_element_type.39), channel_id=1, source_target_pairs={{0,1},{1,0},{2,3},{3,2},{4,5},{5,4},{6,7},{7,6},{8,9},{9,8},{10,11... | collective-permute-start | bytes 804872 | tf_op jit(solution)/shard_map/ppermute | solution.py:360
  56.0 1.0 shard_map.101
  57.0 0.1 collective-permute-done.1
  57.2 0.1 shard_map.102
  57.4 0.4 collective-permute-start.2
  57.8 3.6 %collective-permute-done.2 = f16[528,128]{1,0:T(8,128)(2,1)S(1)} collective-permute-done((f16[528,128]{1,0:T(8,128)(2,1)S(1)}, f16[528,128]{1,0:T(8,128)(2,1)S(1)}, u32[]{:S(2)}, u32[]{:S(2)}) %collective-permute-start.2) | collective-permute-done | bytes 135200 | tf_op jit(solution)/shard_map/ppermute | solution.py:336
  61.4 0.1 shard_map.103
  61.5 0.1 collective-permute-start.3
  61.6 4.0 %collective-permute-done.3 = f16[272,128]{1,0:T(8,128)(2,1)S(1)} collective-permute-done((f16[272,128]{1,0:T(8,128)(2,1)S(1)}, f16[272,128]{1,0:T(8,128)(2,1)S(1)}, u32[]{:S(2)}, u32[]{:S(2)}) %collective-permute-start.3) | collective-permute-done | bytes 69664 | tf_op jit(solution)/shard_map/ppermute | solution.py:336
  65.6 0.1 shard_map.104
  65.7 1.1 collective-permute-start.4
  66.9 3.3 %collective-permute-done.4 = f16[272,128]{1,0:T(8,128)(2,1)S(1)} collective-permute-done((f16[272,128]{1,0:T(8,128)(2,1)S(1)}, f16[272,128]{1,0:T(8,128)(2,1)S(1)}, u32[]{:S(2)}, u32[]{:S(2)}) %collective-permute-start.4) | collective-permute-done | bytes 69664 | tf_op jit(solution)/shard_map/ppermute | solution.py:336
  70.2 0.1 shard_map.105
  70.3 2.0 %collective-permute-start.5 = (bf16[2,128,128]{2,1,0:T(8,128)(2,1)S(1)}, bf16[2,128,128]{2,1,0:T(8,128)(2,1)S(1)}, u32[]{:S(2)}, u32[]{:S(2)}) collective-permute-start(bf16[2,128,128]{2,1,0:T(8,128)(2,1)S(1)} %get-tuple-element.31), channel_id=1, source_target_pairs={{0,4},{1,5},{2,6},{3,7},{4,0},{5,1},{6,2},{7,3},{8,12},{9,13},{10,... | collective-permute-start | bytes 196616 | tf_op jit(solution)/shard_map/ppermute | solution.py:336
  72.3 2.1 %collective-permute-done.5 = bf16[2,128,128]{2,1,0:T(8,128)(2,1)S(1)} collective-permute-done((bf16[2,128,128]{2,1,0:T(8,128)(2,1)S(1)}, bf16[2,128,128]{2,1,0:T(8,128)(2,1)S(1)}, u32[]{:S(2)}, u32[]{:S(2)}) %collective-permute-start.5) | collective-permute-done | bytes 65568 | tf_op jit(solution)/shard_map/ppermute | solution.py:336
  74.4 3.6 %collective-permute-start.7 = (bf16[4,128,128]{2,1,0:T(8,128)(2,1)S(1)}, bf16[4,128,128]{2,1,0:T(8,128)(2,1)S(1)}, u32[]{:S(2)}, u32[]{:S(2)}) collective-permute-start(bf16[4,128,128]{2,1,0:T(8,128)(2,1)S(1)} %constant_dynamic-update-slice_fusion), channel_id=1, source_target_pairs={{0,2},{1,3},{2,0},{3,1},{4,6},{5,7},{6,4},{7,5},{8,10},{9,11},{10,... | collective-permute-start | bytes 393224 | tf_op jit(solution)/shard_map/ppermute | solution.py:336
  78.0 5.5 %collective-permute-start.6 = (bf16[4,128,128]{2,1,0:T(8,128)(2,1)S(1)}, bf16[4,128,128]{2,1,0:T(8,128)(2,1)S(1)}, u32[]{:S(2)}, u32[]{:S(2)}) collective-permute-start(bf16[4,128,128]{2,1,0:T(8,128)(2,1)S(1)} %constant_dynamic-update-slice_fusion), channel_id=1, source_target_pairs={{0,1},{1,0},{2,3},{3,2},{4,5},{5,4},{6,7},{7,6},{8,9},{9,8},{10,11... | collective-permute-start | bytes 393224 | tf_op jit(solution)/shard_map/ppermute | solution.py:360
  83.4 3.4 %collective-permute-start.8 = (bf16[4,128,128]{2,1,0:T(8,128)(2,1)S(1)}, bf16[4,128,128]{2,1,0:T(8,128)(2,1)S(1)}, u32[]{:S(2)}, u32[]{:S(2)}) collective-permute-start(bf16[4,128,128]{2,1,0:T(8,128)(2,1)S(1)} %collective-permute-done.7), channel_id=1, source_target_pairs={{0,1},{1,0},{2,3},{3,2},{4,5},{5,4},{6,7},{7,6},{8,9},{9,8},{10,11... | collective-permute-start | bytes 393224 | tf_op jit(solution)/shard_map/ppermute | solution.py:360
  86.8 1.0 shard_map.106.own_total
  87.9 1.0 shard_map.107
  88.9 10.8 %all_to_all.32.got = bf16[16,64,128]{2,1,0:T(8,128)(2,1)S(1)} all-to-all(bf16[16,64,128]{2,1,0:T(8,128)(2,1)S(1)} %shard_map.107), channel_id=1, replica_groups=mesh['y'=4,'x'=4,'z'=8,'core'=2] {'y','x'}, dimensions={0} | all-to-all | bytes 524288 | tf_op jit(solution)/shard_map/all_to_all | solution.py:327
  99.8 0.1 shard_map.108
  99.9 10.6 %all_to_all.33.got = bf16[16,80,128]{2,1,0:T(8,128)(2,1)S(1)} all-to-all(bf16[16,80,128]{2,1,0:T(8,128)(2,1)S(1)} %shard_map.108), channel_id=1, replica_groups=mesh['y'=4,'x'=4,'z'=8,'core'=2] {'y','x'}, dimensions={0} | all-to-all | bytes 655360 | tf_op jit(solution)/shard_map/all_to_all | solution.py:327
  110.5 1.1 shard_map.109.after
  111.7 2.8 %collective-permute-start.9 = (f16[1048,128]{1,0:T(8,128)(2,1)S(1)}, f16[1048,128]{1,0:T(8,128)(2,1)S(1)}, u32[]{:S(2)}, u32[]{:S(2)}) collective-permute-start(f16[1048,128]{1,0:T(8,128)(2,1)S(1)} %convert_element_type.47), channel_id=1, source_target_pairs={{0,1},{1,0},{2,3},{3,2},{4,5},{5,4},{6,7},{7,6},{8,9},{9,8},{10,11... | collective-permute-start | bytes 804872 | tf_op jit(solution)/shard_map/ppermute | solution.py:360
  114.5 1.0 shard_map.110
  115.5 0.1 collective-permute-done.9
  115.7 0.1 shard_map.111
  115.9 14.4 %all_to_all.34 = f16[8,136,128]{2,1,0:T(8,128)(2,1)S(1)} all-to-all(f16[8,136,128]{2,1,0:T(8,128)(2,1)S(1)} %convert_element_type.49), channel_id=1, replica_groups=mesh['y'=4,'x'=4,'z'=8,'core'=2] {'z'}, dimensions={0} | all-to-all | bytes 557056 | tf_op jit(solution)/shard_map/all_to_all | solution.py:327
  130.3 0.7 shard_map.112
  (34 shorter events, 0.5 us)
Async XLA Ops:
  0.6 0.8 copy-start
  2.2 19.4 %all-to-all-start = ((bf16[8,128,128]{2,1,0:T(8,128)(2,1)}), bf16[8,128,128]{2,1,0:T(8,128)(2,1)S(1)}, u32[]{:S(2)}, u32[]{:S(2)}) async-start(bf16[8,128,128]{2,1,0:T(8,128)(2,1)} %shard_map.95), calls=%async_computation | async-start | bytes 524288 | tf_op jit(solution)/shard_map/all_to_all | solution.py:327
  11.9 12.3 %copy-start.5 = (f32[32]{0:T(128)S(1)}, f32[32]{0:T(128)}, u32[]{:S(2)}) copy-start(f32[32]{0:T(128)} %param.14) | copy-start | bytes 388
  11.9 12.3 %copy-start.6 = (s32[128]{0:T(128)S(1)}, s32[128]{0:T(128)}, u32[]{:S(2)}) copy-start(s32[128]{0:T(128)} %param.13) | copy-start | bytes 1540
  11.9 12.4 %copy-start.1 = (f32[128,128]{1,0:T(8,128)S(1)}, f32[128,128]{1,0:T(8,128)}, u32[]{:S(2)}) copy-start(f32[128,128]{1,0:T(8,128)} %right_ref.9) | copy-start | bytes 196612
  11.9 12.5 %copy-start.3 = (s32[16]{0:T(128)S(1)}, s32[16]{0:T(128)}, u32[]{:S(2)}) copy-start(s32[16]{0:T(128)} %param.10) | copy-start | bytes 196
  11.9 12.5 %copy-start.4 = (s32[16]{0:T(128)S(1)}, s32[16]{0:T(128)}, u32[]{:S(2)}) copy-start(s32[16]{0:T(128)} %param.9) | copy-start | bytes 196
  21.6 3.8 %collective-permute-start = (bf16[8,128,128]{2,1,0:T(8,128)(2,1)S(1)}, bf16[8,128,128]{2,1,0:T(8,128)(2,1)S(1)}, u32[]{:S(2)}, u32[]{:S(2)}) collective-permute-start(bf16[8,128,128]{2,1,0:T(8,128)(2,1)S(1)} %broadcast_multiply_fusion.own.gathered), channel_id=1, source_target_pairs={{0,1},{1,0},{2,3},{3,2},{4,5},{5,4},{6,7},{7,6},{8,9},{9,8},{10,11... | collective-permute-start | bytes 786440 | tf_op jit(solution)/shard_map/ppermute | solution.py:360
  25.4 15.9 %copy-start.2 = (f32[1024]{0:T(1024)S(1)}, f32[1024]{0:T(1024)}, u32[]{:S(2)}) copy-start(f32[1024]{0:T(1024)} %param.12) | copy-start | bytes 12292
  53.3 3.9 %collective-permute-start.1 = (f16[1048,128]{1,0:T(8,128)(2,1)S(1)}, f16[1048,128]{1,0:T(8,128)(2,1)S(1)}, u32[]{:S(2)}, u32[]{:S(2)}) collective-permute-start(f16[1048,128]{1,0:T(8,128)(2,1)S(1)} %convert_element_type.39), channel_id=1, source_target_pairs={{0,1},{1,0},{2,3},{3,2},{4,5},{5,4},{6,7},{7,6},{8,9},{9,8},{10,11... | collective-permute-start | bytes 804872 | tf_op jit(solution)/shard_map/ppermute | solution.py:360
  57.4 3.9 %collective-permute-start.2 = (f16[528,128]{1,0:T(8,128)(2,1)S(1)}, f16[528,128]{1,0:T(8,128)(2,1)S(1)}, u32[]{:S(2)}, u32[]{:S(2)}) collective-permute-start(f16[528,128]{1,0:T(8,128)(2,1)S(1)} %convert_element_type.41), channel_id=1, source_target_pairs={{0,4},{1,3},{2,6},{3,1},{4,0},{5,7},{6,2},{7,5},{8,12},{9,11},{10,... | collective-permute-start | bytes 405512 | tf_op jit(solution)/shard_map/ppermute | solution.py:336
  61.5 4.1 %collective-permute-start.3 = (f16[272,128]{1,0:T(8,128)(2,1)S(1)}, f16[272,128]{1,0:T(8,128)(2,1)S(1)}, u32[]{:S(2)}, u32[]{:S(2)}) collective-permute-start(f16[272,128]{1,0:T(8,128)(2,1)S(1)} %convert_element_type.43), channel_id=1, source_target_pairs={{0,2},{1,5},{2,0},{3,7},{4,6},{5,1},{6,4},{7,3},{8,10},{9,13},{10,... | collective-permute-start | bytes 208904 | tf_op jit(solution)/shard_map/ppermute | solution.py:336
  65.7 4.5 %collective-permute-start.4 = (f16[272,128]{1,0:T(8,128)(2,1)S(1)}, f16[272,128]{1,0:T(8,128)(2,1)S(1)}, u32[]{:S(2)}, u32[]{:S(2)}) collective-permute-start(f16[272,128]{1,0:T(8,128)(2,1)S(1)} %convert_element_type.45), channel_id=1, source_target_pairs={{0,14},{1,15},{2,12},{3,13},{4,10},{5,11},{6,8},{7,9},{8,6},{9,7},... | collective-permute-start | bytes 208904 | tf_op jit(solution)/shard_map/ppermute | solution.py:336
  70.3 4.1 %collective-permute-start.5 = (bf16[2,128,128]{2,1,0:T(8,128)(2,1)S(1)}, bf16[2,128,128]{2,1,0:T(8,128)(2,1)S(1)}, u32[]{:S(2)}, u32[]{:S(2)}) collective-permute-start(bf16[2,128,128]{2,1,0:T(8,128)(2,1)S(1)} %get-tuple-element.31), channel_id=1, source_target_pairs={{0,4},{1,5},{2,6},{3,7},{4,0},{5,1},{6,2},{7,3},{8,12},{9,13},{10,... | collective-permute-start | bytes 196616 | tf_op jit(solution)/shard_map/ppermute | solution.py:336
  74.4 9.1 %collective-permute-start.7 = (bf16[4,128,128]{2,1,0:T(8,128)(2,1)S(1)}, bf16[4,128,128]{2,1,0:T(8,128)(2,1)S(1)}, u32[]{:S(2)}, u32[]{:S(2)}) collective-permute-start(bf16[4,128,128]{2,1,0:T(8,128)(2,1)S(1)} %constant_dynamic-update-slice_fusion), channel_id=1, source_target_pairs={{0,2},{1,3},{2,0},{3,1},{4,6},{5,7},{6,4},{7,5},{8,10},{9,11},{10,... | collective-permute-start | bytes 393224 | tf_op jit(solution)/shard_map/ppermute | solution.py:336
  78.0 9.9 %collective-permute-start.6 = (bf16[4,128,128]{2,1,0:T(8,128)(2,1)S(1)}, bf16[4,128,128]{2,1,0:T(8,128)(2,1)S(1)}, u32[]{:S(2)}, u32[]{:S(2)}) collective-permute-start(bf16[4,128,128]{2,1,0:T(8,128)(2,1)S(1)} %constant_dynamic-update-slice_fusion), channel_id=1, source_target_pairs={{0,1},{1,0},{2,3},{3,2},{4,5},{5,4},{6,7},{7,6},{8,9},{9,8},{10,11... | collective-permute-start | bytes 393224 | tf_op jit(solution)/shard_map/ppermute | solution.py:360
  83.4 4.4 %collective-permute-start.8 = (bf16[4,128,128]{2,1,0:T(8,128)(2,1)S(1)}, bf16[4,128,128]{2,1,0:T(8,128)(2,1)S(1)}, u32[]{:S(2)}, u32[]{:S(2)}) collective-permute-start(bf16[4,128,128]{2,1,0:T(8,128)(2,1)S(1)} %collective-permute-done.7), channel_id=1, source_target_pairs={{0,1},{1,0},{2,3},{3,2},{4,5},{5,4},{6,7},{7,6},{8,9},{9,8},{10,11... | collective-permute-start | bytes 393224 | tf_op jit(solution)/shard_map/ppermute | solution.py:360
  111.7 4.0 %collective-permute-start.9 = (f16[1048,128]{1,0:T(8,128)(2,1)S(1)}, f16[1048,128]{1,0:T(8,128)(2,1)S(1)}, u32[]{:S(2)}, u32[]{:S(2)}) collective-permute-start(f16[1048,128]{1,0:T(8,128)(2,1)S(1)} %convert_element_type.47), channel_id=1, source_target_pairs={{0,1},{1,0},{2,3},{3,2},{4,5},{5,4},{6,7},{7,6},{8,9},{9,8},{10,11... | collective-permute-start | bytes 804872 | tf_op jit(solution)/shard_map/ppermute | solution.py:360

commit v9 on v8

--- a/solution.py
+++ b/solution.py
@@ -336,14 +336,6 @@
     return lax.ppermute(value, ("z", "core"), pairs)
 
 
-def near(z, core):
-    return z ^ 1
-
-
-def far(z, core):
-    return z ^ 2
-
-
 def first(z, core):
     return z ^ (2 - core)
 
@@ -380,8 +372,10 @@
     half, chip = height >> 2, height & 3
     same = (tile_cols >> 2) == half
     apart = jnp.where(same, tile_cols & 3, 3 - (tile_cols & 3)) ^ chip
-    place = ((apart & 1) * 2 + (apart >> 1)) * 2 + jnp.where(same, 0, 1)
-    last_slots = tile_rows * COLS + place
+    turned = (apart & 1) * 2 + (apart >> 1)
+    rest = tile_rows * COLS + jnp.where(same, 0, 1)
+    own_slots = rest + 2 * jnp.where(core == 0, apart, turned)
+    other_slots = rest + 2 * jnp.where(core == 0, turned, apart)
     levels = jnp.arange(depth_reg.shape[0], dtype=jnp.int32)
     level_hot = (depth_level[:, None] == levels[None, :]).astype(jnp.float32)
     reg_cell = jnp.sum(level_hot * depth_reg[None, :], axis=1)
@@ -389,14 +383,14 @@
     sums = call(start_kernel, f32(SUMS, probes), (right_side, reg))
     weights = data_weight.reshape(-1, chunk * PACK)
 
-    def products(own, other, sums, places):
+    def products(own, other, sums, places, other_places):
         total = call(
             forward_own_kernel, f32(group_rows, probes), (core, places, own, tiles), smem=2
         )
         partial = call(
             forward_other_kernel,
             bf16(n_dp, chunk, probes),
-            (dp, core, places, other, tiles, total, sums),
+            (dp, core, other_places, other, tiles, total, sums),
             smem=3,
             scratch=[pltpu.VMEM((group_rows, probes), jnp.float32)],
         )
@@ -436,7 +430,7 @@
         return kept, along_z(coded.astype(jnp.float16), to).astype(jnp.float32), sums
 
     whole, extra = f32(cells, probes), f32(SUMS, probes)
-    terms = products(own, swap(own), sums, slots)
+    terms = products(own, swap(own), sums, slots, slots)
     terms = halved(
         spread_kernel,
         4,
@@ -453,11 +447,11 @@
         (height, *terms, own, right_side, reg),
         smem=1,
     )
-    low = jnp.concatenate([low, along_z(low, far)], axis=0)
-    later = along_z(low, near)
+    low = jnp.concatenate([low, along_z(low, second)], axis=0)
+    later = along_z(low, first)
     other = jnp.concatenate([swap(low), swap(later)], axis=0)
     low = jnp.concatenate([low, later], axis=0)
-    terms = call(pair_kernel, f32(n_z, cells + SUMS, probes), products(low, other, sums, last_slots))
+    terms = call(pair_kernel, f32(n_z, cells + SUMS, probes), products(low, other, sums, own_slots, other_slots))
     got = exchange(terms.astype(jnp.float16), "z").astype(jnp.float32)
     return call(
         last_update_kernel,

time: 131 us -> 134 us (1.023)
  starting transfers between devices: 33.1 us -> 35.2 us
    ppermute x5, starting transfers between devices: 16.9 us -> 19 us  [swap(): return lax.ppermute(value, 'core', [(0, 1), (1, 0)])]
where the time goes in v9:
time: 134 us
  blocking collectives  62 us (46%)
  starting transfers between devices  35.2 us (26%)
  waiting for transfers between devices  19.2 us (14%)
  Pallas kernels  10.6 us (8%)
  between operations  2.93 us (2%)
  other arithmetic  2.35 us (2%)
  local copies, waits for them, and re-layouts  1.48 us (1%)
    all_to_all x5, blocking collectives, exchange(): return lax.all_to_all(value, axis, 0, 0)  62 us
    ppermute x5, starting transfers between devices, swap(): return lax.ppermute(value, 'core', [(0, 1), (1, 0)])  19 us
    ppermute x5, waiting for transfers between devices, along_z(): return lax.ppermute(value, ('z', 'core'), pairs)  13 us
    pallas_call x18, Pallas kernels, call(): pl.pallas_call(kernel, out_shape=out_shape, in_specs=[pl.BlockSpec(memory...  10.6 us
    all_to_all x1, starting transfers between devices, exchange(): return lax.all_to_all(value, axis, 0, 0)  9.01 us
    ppermute x5, starting transfers between devices, along_z(): return lax.ppermute(value, ('z', 'core'), pairs)  7.24 us
    all_to_all x1, waiting for transfers between devices, exchange(): return lax.all_to_all(value, axis, 0, 0)  5.94 us
  transfers between devices with their start and end apart: 11, of which 7 were waited for; matrix products, arithmetic and copies ran while one was open for 2% of the time, Pallas kernels for 3%

profile of v9, /device:TPU:1, one launch (start us, length us, event | category | flops | bytes accessed | tf_op | source)
XLA Modules:
  0.0 133.8 jit_solution(9469827757720525111)
XLA Ops:
  0.6 0.0 copy-start
  0.6 0.8 copy-done
  1.5 0.7 shard_map.95
  2.2 9.0 %all-to-all-start = ((bf16[8,128,128]{2,1,0:T(8,128)(2,1)}), bf16[8,128,128]{2,1,0:T(8,128)(2,1)S(1)}, u32[]{:S(2)}, u32[]{:S(2)}) async-start(bf16[8,128,128]{2,1,0:T(8,128)(2,1)} %shard_map.95), calls=%async_computation | async-start | bytes 524288 | tf_op jit(solution)/shard_map/all_to_all | solution.py:327
  11.9 0.0 copy-start.4
  11.9 0.0 copy-start.5
  11.9 1.8 %broadcast_select_fusion.tiles = bf16[16,256,256]{2,1,0:T(8,128)(2,1)S(1)} fusion(bf16[16,256,256]{2,1,0:T(8,128)(2,1)} %param.8, pred[16]{0:T(512)(128)(4,1)S(1)} %iota_compare_fusion.1), kind=kLoop, calls=%fused_computation | loop fusion | flops 1048576 | bytes 4194320 | tf_op jit(solution)/shard_map/jit(_where)/select_n | solution.py:369
  13.8 0.5 slice.5
  15.7 5.9 %all-to-all-done = bf16[8,128,128]{2,1,0:T(8,128)(2,1)S(1)} async-done(((bf16[8,128,128]{2,1,0:T(8,128)(2,1)}), bf16[8,128,128]{2,1,0:T(8,128)(2,1)S(1)}, u32[]{:S(2)}, u32[]{:S(2)}) %all-to-all-start) | async-done | bytes 262176 | tf_op jit(solution)/shard_map/all_to_all | solution.py:327
  21.6 2.5 %collective-permute-start = (bf16[8,128,128]{2,1,0:T(8,128)(2,1)S(1)}, bf16[8,128,128]{2,1,0:T(8,128)(2,1)S(1)}, u32[]{:S(2)}, u32[]{:S(2)}) collective-permute-start(bf16[8,128,128]{2,1,0:T(8,128)(2,1)S(1)} %broadcast_multiply_fusion.own.gathered), channel_id=1, source_target_pairs={{0,1},{1,0},{2,3},{3,2},{4,5},{5,4},{6,7},{7,6},{8,9},{9,8},{10,11... | collective-permute-start | bytes 786440 | tf_op jit(solution)/shard_map/ppermute | solution.py:352
  24.2 0.1 select_reduce_fusion
  24.3 0.1 broadcast_in_dim.49.reg_ref
  24.4 1.0 shard_map.96.own_total
  25.4 1.0 shard_map.98
  26.5 14.8 %all_to_all.30.got = bf16[16,64,128]{2,1,0:T(8,128)(2,1)S(1)} all-to-all(bf16[16,64,128]{2,1,0:T(8,128)(2,1)S(1)} %shard_map.98), channel_id=1, replica_groups=mesh['y'=4,'x'=4,'z'=8,'core'=2] {'y','x'}, dimensions={0} | all-to-all | bytes 524288 | tf_op jit(solution)/shard_map/all_to_all | solution.py:327
  41.3 0.1 shard_map.99
  41.4 10.7 %all_to_all.31.got = bf16[16,80,128]{2,1,0:T(8,128)(2,1)S(1)} all-to-all(bf16[16,80,128]{2,1,0:T(8,128)(2,1)S(1)} %shard_map.99), channel_id=1, replica_groups=mesh['y'=4,'x'=4,'z'=8,'core'=2] {'y','x'}, dimensions={0} | all-to-all | bytes 655360 | tf_op jit(solution)/shard_map/all_to_all | solution.py:327
  52.0 1.1 shard_map.100.after
  53.2 2.8 %collective-permute-start.1 = (f16[1048,128]{1,0:T(8,128)(2,1)S(1)}, f16[1048,128]{1,0:T(8,128)(2,1)S(1)}, u32[]{:S(2)}, u32[]{:S(2)}) collective-permute-start(f16[1048,128]{1,0:T(8,128)(2,1)S(1)} %convert_element_type.39), channel_id=1, source_target_pairs={{0,1},{1,0},{2,3},{3,2},{4,5},{5,4},{6,7},{7,6},{8,9},{9,8},{10,11... | collective-permute-start | bytes 804872 | tf_op jit(solution)/shard_map/ppermute | solution.py:352
  56.0 1.0 shard_map.101
  57.0 0.1 collective-permute-done.1
  57.2 0.1 shard_map.102
  57.4 0.4 collective-permute-start.2
  57.8 3.6 %collective-permute-done.2 = f16[528,128]{1,0:T(8,128)(2,1)S(1)} collective-permute-done((f16[528,128]{1,0:T(8,128)(2,1)S(1)}, f16[528,128]{1,0:T(8,128)(2,1)S(1)}, u32[]{:S(2)}, u32[]{:S(2)}) %collective-permute-start.2) | collective-permute-done | bytes 135200 | tf_op jit(solution)/shard_map/ppermute | solution.py:336
  61.4 0.1 shard_map.103
  61.5 0.1 collective-permute-start.3
  61.6 4.0 %collective-permute-done.3 = f16[272,128]{1,0:T(8,128)(2,1)S(1)} collective-permute-done((f16[272,128]{1,0:T(8,128)(2,1)S(1)}, f16[272,128]{1,0:T(8,128)(2,1)S(1)}, u32[]{:S(2)}, u32[]{:S(2)}) %collective-permute-start.3) | collective-permute-done | bytes 69664 | tf_op jit(solution)/shard_map/ppermute | solution.py:336
  65.6 0.1 shard_map.104
  65.7 1.2 collective-permute-start.4
  66.9 3.3 %collective-permute-done.4 = f16[272,128]{1,0:T(8,128)(2,1)S(1)} collective-permute-done((f16[272,128]{1,0:T(8,128)(2,1)S(1)}, f16[272,128]{1,0:T(8,128)(2,1)S(1)}, u32[]{:S(2)}, u32[]{:S(2)}) %collective-permute-start.4) | collective-permute-done | bytes 69664 | tf_op jit(solution)/shard_map/ppermute | solution.py:336
  70.2 0.1 shard_map.105
  70.3 2.0 %collective-permute-start.5 = (bf16[2,128,128]{2,1,0:T(8,128)(2,1)S(1)}, bf16[2,128,128]{2,1,0:T(8,128)(2,1)S(1)}, u32[]{:S(2)}, u32[]{:S(2)}) collective-permute-start(bf16[2,128,128]{2,1,0:T(8,128)(2,1)S(1)} %get-tuple-element.31), channel_id=1, source_target_pairs={{0,2},{1,5},{2,0},{3,7},{4,6},{5,1},{6,4},{7,3},{8,10},{9,13},{10,... | collective-permute-start | bytes 196616 | tf_op jit(solution)/shard_map/ppermute | solution.py:336
  72.3 2.1 %collective-permute-done.5 = bf16[2,128,128]{2,1,0:T(8,128)(2,1)S(1)} collective-permute-done((bf16[2,128,128]{2,1,0:T(8,128)(2,1)S(1)}, bf16[2,128,128]{2,1,0:T(8,128)(2,1)S(1)}, u32[]{:S(2)}, u32[]{:S(2)}) %collective-permute-start.5) | collective-permute-done | bytes 65568 | tf_op jit(solution)/shard_map/ppermute | solution.py:336
  74.4 3.6 %collective-permute-start.7 = (bf16[4,128,128]{2,1,0:T(8,128)(2,1)S(1)}, bf16[4,128,128]{2,1,0:T(8,128)(2,1)S(1)}, u32[]{:S(2)}, u32[]{:S(2)}) collective-permute-start(bf16[4,128,128]{2,1,0:T(8,128)(2,1)S(1)} %constant_dynamic-update-slice_fusion), channel_id=1, source_target_pairs={{0,4},{1,3},{2,6},{3,1},{4,0},{5,7},{6,2},{7,5},{8,12},{9,11},{10,... | collective-permute-start | bytes 393224 | tf_op jit(solution)/shard_map/ppermute | solution.py:336
  78.0 4.2 %collective-permute-start.6 = (bf16[4,128,128]{2,1,0:T(8,128)(2,1)S(1)}, bf16[4,128,128]{2,1,0:T(8,128)(2,1)S(1)}, u32[]{:S(2)}, u32[]{:S(2)}) collective-permute-start(bf16[4,128,128]{2,1,0:T(8,128)(2,1)S(1)} %constant_dynamic-update-slice_fusion), channel_id=1, source_target_pairs={{0,1},{1,0},{2,3},{3,2},{4,5},{5,4},{6,7},{7,6},{8,9},{9,8},{10,11... | collective-permute-start | bytes 393224 | tf_op jit(solution)/shard_map/ppermute | solution.py:352
  82.1 6.7 %collective-permute-start.8 = (bf16[4,128,128]{2,1,0:T(8,128)(2,1)S(1)}, bf16[4,128,128]{2,1,0:T(8,128)(2,1)S(1)}, u32[]{:S(2)}, u32[]{:S(2)}) collective-permute-start(bf16[4,128,128]{2,1,0:T(8,128)(2,1)S(1)} %collective-permute-done.7), channel_id=1, source_target_pairs={{0,1},{1,0},{2,3},{3,2},{4,5},{5,4},{6,7},{7,6},{8,9},{9,8},{10,11... | collective-permute-start | bytes 393224 | tf_op jit(solution)/shard_map/ppermute | solution.py:352
  88.9 1.0 shard_map.106.own_total
  89.9 1.0 shard_map.107
  91.0 10.9 %all_to_all.32.got = bf16[16,64,128]{2,1,0:T(8,128)(2,1)S(1)} all-to-all(bf16[16,64,128]{2,1,0:T(8,128)(2,1)S(1)} %shard_map.107), channel_id=1, replica_groups=mesh['y'=4,'x'=4,'z'=8,'core'=2] {'y','x'}, dimensions={0} | all-to-all | bytes 524288 | tf_op jit(solution)/shard_map/all_to_all | solution.py:327
  101.8 0.1 shard_map.108
  102.0 10.6 %all_to_all.33.got = bf16[16,80,128]{2,1,0:T(8,128)(2,1)S(1)} all-to-all(bf16[16,80,128]{2,1,0:T(8,128)(2,1)S(1)} %shard_map.108), channel_id=1, replica_groups=mesh['y'=4,'x'=4,'z'=8,'core'=2] {'y','x'}, dimensions={0} | all-to-all | bytes 655360 | tf_op jit(solution)/shard_map/all_to_all | solution.py:327
  112.6 1.1 shard_map.109.after
  113.7 2.8 %collective-permute-start.9 = (f16[1048,128]{1,0:T(8,128)(2,1)S(1)}, f16[1048,128]{1,0:T(8,128)(2,1)S(1)}, u32[]{:S(2)}, u32[]{:S(2)}) collective-permute-start(f16[1048,128]{1,0:T(8,128)(2,1)S(1)} %convert_element_type.47), channel_id=1, source_target_pairs={{0,1},{1,0},{2,3},{3,2},{4,5},{5,4},{6,7},{7,6},{8,9},{9,8},{10,11... | collective-permute-start | bytes 804872 | tf_op jit(solution)/shard_map/ppermute | solution.py:352
  116.5 1.0 shard_map.110
  117.6 0.1 collective-permute-done.9
  117.8 0.1 shard_map.111
  118.0 15.1 %all_to_all.34 = f16[8,136,128]{2,1,0:T(8,128)(2,1)S(1)} all-to-all(f16[8,136,128]{2,1,0:T(8,128)(2,1)S(1)} %convert_element_type.49), channel_id=1, replica_groups=mesh['y'=4,'x'=4,'z'=8,'core'=2] {'z'}, dimensions={0} | all-to-all | bytes 557056 | tf_op jit(solution)/shard_map/all_to_all | solution.py:327
  133.0 0.7 shard_map.112
  (35 shorter events, 0.5 us)
Async XLA Ops:
  0.6 0.8 copy-start
  2.2 19.4 %all-to-all-start = ((bf16[8,128,128]{2,1,0:T(8,128)(2,1)}), bf16[8,128,128]{2,1,0:T(8,128)(2,1)S(1)}, u32[]{:S(2)}, u32[]{:S(2)}) async-start(bf16[8,128,128]{2,1,0:T(8,128)(2,1)} %shard_map.95), calls=%async_computation | async-start | bytes 524288 | tf_op jit(solution)/shard_map/all_to_all | solution.py:327
  11.9 3.7 %copy-start.3 = (s32[16]{0:T(128)S(1)}, s32[16]{0:T(128)}, u32[]{:S(2)}) copy-start(s32[16]{0:T(128)} %param.10) | copy-start | bytes 196
  11.9 3.7 %copy-start.4 = (s32[16]{0:T(128)S(1)}, s32[16]{0:T(128)}, u32[]{:S(2)}) copy-start(s32[16]{0:T(128)} %param.9) | copy-start | bytes 196
  11.9 12.3 %copy-start.5 = (f32[32]{0:T(128)S(1)}, f32[32]{0:T(128)}, u32[]{:S(2)}) copy-start(f32[32]{0:T(128)} %param.14) | copy-start | bytes 388
  11.9 12.2 %copy-start.6 = (s32[128]{0:T(128)S(1)}, s32[128]{0:T(128)}, u32[]{:S(2)}) copy-start(s32[128]{0:T(128)} %param.13) | copy-start | bytes 1540
  11.9 12.4 %copy-start.1 = (f32[128,128]{1,0:T(8,128)S(1)}, f32[128,128]{1,0:T(8,128)}, u32[]{:S(2)}) copy-start(f32[128,128]{1,0:T(8,128)} %right_ref.9) | copy-start | bytes 196612
  21.6 3.8 %collective-permute-start = (bf16[8,128,128]{2,1,0:T(8,128)(2,1)S(1)}, bf16[8,128,128]{2,1,0:T(8,128)(2,1)S(1)}, u32[]{:S(2)}, u32[]{:S(2)}) collective-permute-start(bf16[8,128,128]{2,1,0:T(8,128)(2,1)S(1)} %broadcast_multiply_fusion.own.gathered), channel_id=1, source_target_pairs={{0,1},{1,0},{2,3},{3,2},{4,5},{5,4},{6,7},{7,6},{8,9},{9,8},{10,11... | collective-permute-start | bytes 786440 | tf_op jit(solution)/shard_map/ppermute | solution.py:352
  25.4 15.9 %copy-start.2 = (f32[1024]{0:T(1024)S(1)}, f32[1024]{0:T(1024)}, u32[]{:S(2)}) copy-start(f32[1024]{0:T(1024)} %param.12) | copy-start | bytes 12292
  53.2 3.9 %collective-permute-start.1 = (f16[1048,128]{1,0:T(8,128)(2,1)S(1)}, f16[1048,128]{1,0:T(8,128)(2,1)S(1)}, u32[]{:S(2)}, u32[]{:S(2)}) collective-permute-start(f16[1048,128]{1,0:T(8,128)(2,1)S(1)} %convert_element_type.39), channel_id=1, source_target_pairs={{0,1},{1,0},{2,3},{3,2},{4,5},{5,4},{6,7},{7,6},{8,9},{9,8},{10,11... | collective-permute-start | bytes 804872 | tf_op jit(solution)/shard_map/ppermute | solution.py:352
  57.4 3.9 %collective-permute-start.2 = (f16[528,128]{1,0:T(8,128)(2,1)S(1)}, f16[528,128]{1,0:T(8,128)(2,1)S(1)}, u32[]{:S(2)}, u32[]{:S(2)}) collective-permute-start(f16[528,128]{1,0:T(8,128)(2,1)S(1)} %convert_element_type.41), channel_id=1, source_target_pairs={{0,4},{1,3},{2,6},{3,1},{4,0},{5,7},{6,2},{7,5},{8,12},{9,11},{10,... | collective-permute-start | bytes 405512 | tf_op jit(solution)/shard_map/ppermute | solution.py:336
  61.5 4.1 %collective-permute-start.3 = (f16[272,128]{1,0:T(8,128)(2,1)S(1)}, f16[272,128]{1,0:T(8,128)(2,1)S(1)}, u32[]{:S(2)}, u32[]{:S(2)}) collective-permute-start(f16[272,128]{1,0:T(8,128)(2,1)S(1)} %convert_element_type.43), channel_id=1, source_target_pairs={{0,2},{1,5},{2,0},{3,7},{4,6},{5,1},{6,4},{7,3},{8,10},{9,13},{10,... | collective-permute-start | bytes 208904 | tf_op jit(solution)/shard_map/ppermute | solution.py:336
  65.7 4.5 %collective-permute-start.4 = (f16[272,128]{1,0:T(8,128)(2,1)S(1)}, f16[272,128]{1,0:T(8,128)(2,1)S(1)}, u32[]{:S(2)}, u32[]{:S(2)}) collective-permute-start(f16[272,128]{1,0:T(8,128)(2,1)S(1)} %convert_element_type.45), channel_id=1, source_target_pairs={{0,14},{1,15},{2,12},{3,13},{4,10},{5,11},{6,8},{7,9},{8,6},{9,7},... | collective-permute-start | bytes 208904 | tf_op jit(solution)/shard_map/ppermute | solution.py:336
  70.3 4.1 %collective-permute-start.5 = (bf16[2,128,128]{2,1,0:T(8,128)(2,1)S(1)}, bf16[2,128,128]{2,1,0:T(8,128)(2,1)S(1)}, u32[]{:S(2)}, u32[]{:S(2)}) collective-permute-start(bf16[2,128,128]{2,1,0:T(8,128)(2,1)S(1)} %get-tuple-element.31), channel_id=1, source_target_pairs={{0,2},{1,5},{2,0},{3,7},{4,6},{5,1},{6,4},{7,3},{8,10},{9,13},{10,... | collective-permute-start | bytes 196616 | tf_op jit(solution)/shard_map/ppermute | solution.py:336
  74.4 7.8 %collective-permute-start.7 = (bf16[4,128,128]{2,1,0:T(8,128)(2,1)S(1)}, bf16[4,128,128]{2,1,0:T(8,128)(2,1)S(1)}, u32[]{:S(2)}, u32[]{:S(2)}) collective-permute-start(bf16[4,128,128]{2,1,0:T(8,128)(2,1)S(1)} %constant_dynamic-update-slice_fusion), channel_id=1, source_target_pairs={{0,4},{1,3},{2,6},{3,1},{4,0},{5,7},{6,2},{7,5},{8,12},{9,11},{10,... | collective-permute-start | bytes 393224 | tf_op jit(solution)/shard_map/ppermute | solution.py:336
  78.0 11.9 %collective-permute-start.6 = (bf16[4,128,128]{2,1,0:T(8,128)(2,1)S(1)}, bf16[4,128,128]{2,1,0:T(8,128)(2,1)S(1)}, u32[]{:S(2)}, u32[]{:S(2)}) collective-permute-start(bf16[4,128,128]{2,1,0:T(8,128)(2,1)S(1)} %constant_dynamic-update-slice_fusion), channel_id=1, source_target_pairs={{0,1},{1,0},{2,3},{3,2},{4,5},{5,4},{6,7},{7,6},{8,9},{9,8},{10,11... | collective-permute-start | bytes 393224 | tf_op jit(solution)/shard_map/ppermute | solution.py:352
  82.1 7.8 %collective-permute-start.8 = (bf16[4,128,128]{2,1,0:T(8,128)(2,1)S(1)}, bf16[4,128,128]{2,1,0:T(8,128)(2,1)S(1)}, u32[]{:S(2)}, u32[]{:S(2)}) collective-permute-start(bf16[4,128,128]{2,1,0:T(8,128)(2,1)S(1)} %collective-permute-done.7), channel_id=1, source_target_pairs={{0,1},{1,0},{2,3},{3,2},{4,5},{5,4},{6,7},{7,6},{8,9},{9,8},{10,11... | collective-permute-start | bytes 393224 | tf_op jit(solution)/shard_map/ppermute | solution.py:352
  113.7 4.0 %collective-permute-start.9 = (f16[1048,128]{1,0:T(8,128)(2,1)S(1)}, f16[1048,128]{1,0:T(8,128)(2,1)S(1)}, u32[]{:S(2)}, u32[]{:S(2)}) collective-permute-start(f16[1048,128]{1,0:T(8,128)(2,1)S(1)} %convert_element_type.47), channel_id=1, source_target_pairs={{0,1},{1,0},{2,3},{3,2},{4,5},{5,4},{6,7},{7,6},{8,9},{9,8},{10,11... | collective-permute-start | bytes 804872 | tf_op jit(solution)/shard_map/ppermute | solution.py:352
